TPU v7x, 512 devices: a whole 4x4x16 slice. The times are simulated.
512 devices in a mesh: seq: 32 (over y, x, core), head: 16 (over z).
Axes of the slice: x: 4, y: 4, z: 16, core: 2. Of those that a mesh axis runs over, the one named last changes fastest.
Arguments:
- queries: bfloat16 [8192, 4096], P('seq', 'head'), may hold values from -6 to 6
- keys: bfloat16 [8192, 4096], P('seq', 'head'), may hold values from -6 to 6
- values: bfloat16 [8192, 4096], P('seq', 'head'), may hold values from -6 to 6
- gate: bfloat16 [8192, 4096], P('seq', 'head'), may hold values from -6 to 6
- log_forget: float32 [32, 8192], P('head', 'seq'), may hold values from -1.5 to 0
- write_rate: float32 [32, 8192], P('head', 'seq'), may hold values from 0 to 1
- level_weight: float32 [32, 8, 8192], P('head', None, 'seq'), may hold values from 0.25 to 2.5
- w_out: bfloat16 [4096, 4096], P('head'), may hold values from -0.09375 to 0.09375
Outputs:
- mixed: bfloat16 [8192, 4096], P(('seq', 'head'))
All inputs are finite; a program needn't handle non-finite values.
Results may differ from a plain program's by a relative error of at most 0.02.
Values may be sent and summed in bfloat16 or wider, within the bound.
No kernel may reach another device: no remote copies, remote signals or barrier semaphores. Data moves between devices by JAX's collectives and lax.ppermute only.
A program may use at most 64 MiB of HBM per device.

v0:
```python
import jax
import jax.numpy as jnp
from jax import lax
from jax.sharding import PartitionSpec as P

DK = 128
BLOCK = 64


EPSILON = 1e-06
PRECISE = lax.Precision.HIGHEST


def as_sent(shard):

    def short(part):
        return part.astype(jnp.bfloat16) if part.dtype == jnp.float32 else part

    return jax.tree.map(short, shard)


def swapped(block, axis, stride):
    count = lax.axis_size(axis)
    route = []
    for low in range(count):
        high = low | 1 << stride
        if high != low and high < count:
            route += [(low, high), (high, low)]
    return lax.ppermute(block, axis, route)


def unit_rows(matrix):
    floated = matrix.astype(jnp.float32)
    return floated * lax.rsqrt(jnp.sum(floated * floated, axis=-1, keepdims=True) + EPSILON)


def matmul(left, right):
    return jnp.einsum("...ij,...jk->...ik", left, right, precision=PRECISE)


def compose(leading, trailing):
    return (matmul(leading[0], trailing[1]) + trailing[0], matmul(leading[1], trailing[1]))


def partner_blocks(tensor, stride):
    shaped = tensor.reshape(
        tensor.shape[0],
        tensor.shape[1] // (2 * stride),
        2,
        stride,
        tensor.shape[2],
        tensor.shape[3],
    )
    return jnp.flip(shaped, axis=2).reshape(tensor.shape)


def on_device(queries, keys, values, gate, log_forget, write_rate, level_weight, w_out):
    tokens_here = queries.shape[0]
    heads_here = log_forget.shape[0]
    blocks = tokens_here // BLOCK
    inner_bits = blocks.bit_length() - 1
    outer_bits = lax.axis_size("seq").bit_length() - 1

    def arrange(matrix):
        return jnp.transpose(matrix.reshape(blocks, BLOCK, heads_here, DK), (2, 0, 1, 3))

    query_rows = arrange(unit_rows(queries.reshape(tokens_here, heads_here, DK)))
    key_rows = arrange(unit_rows(keys.reshape(tokens_here, heads_here, DK)))
    value_rows = arrange(values.astype(jnp.float32))
    decay_logs = log_forget.reshape(heads_here, blocks, BLOCK)
    strength = write_rate.reshape(heads_here, blocks, BLOCK)
    rows_index = lax.broadcasted_iota(jnp.int32, (BLOCK, BLOCK), 0)
    cols_index = lax.broadcasted_iota(jnp.int32, (BLOCK, BLOCK), 1)
    inclusive = rows_index >= cols_index
    strict = rows_index > cols_index
    cumulative = jnp.einsum(
        "hnc,tc->hnt", decay_logs, inclusive.astype(jnp.float32), precision=PRECISE
    )
    spread = cumulative[..., :, None] - cumulative[..., None, :]
    fading = jnp.exp(jnp.where(inclusive, spread, -1e30))
    key_key = jnp.einsum("hncd,hnsd->hncs", key_rows, key_rows, precision=PRECISE)
    query_key = jnp.einsum("hncd,hnsd->hncs", query_rows, key_rows, precision=PRECISE)
    unit_block = jnp.eye(BLOCK, dtype=jnp.float32)
    rated_keys = strength[..., :, None] * key_key
    lower_keys = unit_block + jnp.where(strict, rated_keys, 0.0)
    lower_values = unit_block + jnp.where(strict, rated_keys * fading, 0.0)
    key_bases = jax.scipy.linalg.solve_triangular(
        lower_keys, strength[..., None] * key_rows, lower=True, unit_diagonal=True
    )
    writes = jax.scipy.linalg.solve_triangular(
        lower_values, strength[..., None] * value_rows, lower=True, unit_diagonal=True
    )
    reach_rows = jnp.exp(cumulative)[..., None] * (
        query_rows
        - jnp.einsum(
            "hnts,hnsd->hntd", jnp.where(inclusive, query_key, 0.0), key_bases, precision=PRECISE
        )
    )
    own_read = jnp.einsum("hnts,hnsd->hntd", query_key * fading, writes, precision=PRECISE)
    final_log = cumulative[..., -1]
    unit_state = jnp.eye(DK, dtype=jnp.float32)
    moving = jnp.exp(final_log)[..., None, None] * (
        unit_state - jnp.einsum("hnti,hntj->hnij", key_bases, key_rows, precision=PRECISE)
    )
    tail_decay = jnp.exp(final_log[..., None] - cumulative)
    ending = jnp.einsum(
        "hnti,hntj->hnij", writes * tail_decay[..., None], key_rows, precision=PRECISE
    )
    totals = (ending, moving)
    prefix = jnp.broadcast_to(unit_state, (heads_here, blocks, DK, DK))
    inner_levels = []
    block_ids = jnp.arange(blocks, dtype=jnp.int32)
    for exponent in range(inner_bits):
        stride = 2**exponent
        partner = (partner_blocks(totals[0], stride), partner_blocks(totals[1], stride))
        upper_half = (block_ids // stride % 2 == 1)[None, :, None, None]
        inner_levels.append(jnp.where(upper_half, matmul(partner[0], prefix), 0.0))
        prefix = jnp.where(upper_half, matmul(partner[1], prefix), prefix)
        leading = (
            jnp.where(upper_half, partner[0], totals[0]),
            jnp.where(upper_half, partner[1], totals[1]),
        )
        trailing = (
            jnp.where(upper_half, totals[0], partner[0]),
            jnp.where(upper_half, totals[1], partner[1]),
        )
        totals = compose(leading, trailing)
    slab_end = totals[0][:, 0]
    slab_move = totals[1][:, 0]
    position = lax.axis_index("seq")
    identity_heads = jnp.broadcast_to(unit_state, (heads_here, DK, DK))
    totals_here = (slab_end, slab_move)
    before = identity_heads
    collected = []
    for exponent in range(outer_bits):
        partner = swapped((as_sent(totals_here[0]), as_sent(totals_here[1])), "seq", exponent)
        upper_half = position // 2**exponent % 2 == 1
        collected.append(jnp.where(upper_half, matmul(partner[0], before), 0.0))
        before = jnp.where(upper_half, matmul(partner[1], before), before)
        leading = (
            jnp.where(upper_half, partner[0], totals_here[0]),
            jnp.where(upper_half, partner[1], totals_here[1]),
        )
        trailing = (
            jnp.where(upper_half, totals_here[0], partner[0]),
            jnp.where(upper_half, totals_here[1], partner[1]),
        )
        totals_here = compose(leading, trailing)
    outer_levels = jnp.stack(collected)
    weights = level_weight.reshape(heads_here, level_weight.shape[1], blocks, BLOCK)
    core_rows = weights[:, 0, :, :, None] * own_read
    stacked = jnp.stack(inner_levels, axis=1)
    level_reads = jnp.einsum("hlnij,hncj->hlnci", stacked, reach_rows, precision=PRECISE)
    core_rows = core_rows + jnp.einsum(
        "hlnc,hlnci->hnci", weights[:, 1 : 1 + inner_bits], level_reads, precision=PRECISE
    )
    lifted = jnp.einsum("hnij,hncj->hnci", prefix, reach_rows, precision=PRECISE)
    cross_reads = jnp.einsum("lhij,hncj->hlnci", outer_levels, lifted, precision=PRECISE)
    core_rows = core_rows + jnp.einsum(
        "hlnc,hlnci->hnci", weights[:, 1 + inner_bits :], cross_reads, precision=PRECISE
    )
    core_rows = jnp.transpose(core_rows, (1, 2, 0, 3)).reshape(tokens_here, heads_here, DK)
    scaled = core_rows * lax.rsqrt(
        jnp.mean(core_rows * core_rows, axis=-1, keepdims=True) + EPSILON
    )
    gated = scaled * jax.nn.silu(gate.astype(jnp.float32).reshape(tokens_here, heads_here, DK))
    normed = gated.reshape(tokens_here, heads_here * DK).astype(jnp.bfloat16)
    return lax.psum_scatter(
        jnp.dot(normed, w_out, preferred_element_type=jnp.float32).astype(jnp.bfloat16),
        "head",
        scatter_dimension=0,
        tiled=True,
    )


def solution(mesh):
    in_specs = (
        P("seq", "head"),
        P("seq", "head"),
        P("seq", "head"),
        P("seq", "head"),
        P("head", "seq"),
        P("head", "seq"),
        P("head", None, "seq"),
        P("head", None),
    )
    out_specs = P(("seq", "head"), None)
    return jax.shard_map(
        on_device, mesh=mesh, in_specs=in_specs, out_specs=out_specs, check_vma=False
    )
```

profile of v0, /device:TPU:6, one launch (start us, length us, event | category | flops | bytes accessed | tf_op | source)
XLA Modules:
  0.0 272.9 jit_solution(11016563930725041472)
XLA Ops:
  6.6 0.9 reshape.165
  7.8 0.6 exp.24
  8.4 0.6 subtract_exponential_fusion
  9.0 1.0 reshape.177
  10.1 0.9 convert_multiply_fusion.1
  11.0 0.8 mul.133
  11.8 1.0 reshape.178
  13.0 0.3 reduce_sum.28
  13.5 1.4 add_bitcast_fusion.1
  14.9 39.3 %custom-call.4 = f32[2,4,1,64,64]{3,4,2,1,0:T(8,128)S(1)} custom-call(f32[2,4,1,64,64]{4,3,2,1,0:T(8,128)S(1)} %get-tuple-element.10), custom_call_target="InvertDiagBlocksLowerTriangular" | custom-call | tf_op jit(solution)/shard_map/jit(_solve_triangular)/vmap(vmap())/triangular_solve | solution.py:90
  54.2 40.1 %custom-call.5 = f32[2,4,1,64,64]{3,4,2,1,0:T(8,128)S(1)} custom-call(f32[2,4,1,64,64]{4,3,2,1,0:T(8,128)} %get-tuple-element.11), custom_call_target="InvertDiagBlocksLowerTriangular" | custom-call | tf_op jit(solution)/shard_map/jit(_solve_triangular)/vmap(vmap())/triangular_solve | solution.py:87
  94.3 1.5 fusion.36
  95.8 0.7 fusion.38
  96.5 1.2 fusion.41
  97.6 0.9 rev.14
  98.6 2.0 fusion.4
  100.7 1.6 fusion.26
  102.3 1.5 convolution_add_fusion
  103.8 1.1 rev.16
  104.9 1.9 rev.17
  106.8 1.4 broadcast_select_fusion
  108.2 0.7 fusion.24
  108.9 0.7 fusion.99
  109.6 1.9 collective-permute-start
  111.5 1.0 fusion.101
  112.5 2.6 collective-permute-start.1
  115.1 1.4 reshape.164
  116.5 1.3 slice_bitcast_fusion.2
  117.8 1.3 slice_bitcast_fusion.1
  119.1 1.3 slice_bitcast_fusion
  120.4 1.8 reshape.176
  122.2 1.7 convert_multiply_fusion.2
  123.9 2.4 fusion.2
  126.3 1.2 convolution_select_fusion.1
  127.6 1.5 fusion.3
  129.0 1.4 convolution_select_fusion
  130.5 1.6 copy.43
  132.0 1.1 mul.125
  133.1 0.3 reduce_sum.27
  133.6 0.7 fusion.44
  134.3 1.1 fusion.5
  135.4 2.5 convolution_bitcast_fusion.1
  137.9 4.5 %fusion.29 = f32[2,4,64,1,128]{4,3,2,1,0:T(1,128)} fusion(f32[2,2,4,64,1]{1,4,3,2,0:T(1,128)S(1)} %copy-done.12, f32[2,2,4,64,128]{4,3,1,2,0:T(8,128)S(1)} %convolution_bitcast_fusion.1), kind=kOutput, calls=%fused_computation.58 | convolution fusion | flops 1572864 | bytes 790528 | tf_op jit(solution)/shard_map/hlnc,hlnci->hnci/dot_general | solution.py:154
  142.4 1.1 convolution_bitcast_fusion.2
  144.1 2.7 %collective-permute-start.3 = (bf16[2,128,128]{2,1,0:T(8,128)(2,1)S(1)}, bf16[2,128,128]{2,1,0:T(8,128)(2,1)S(1)}, u32[]{:S(2)}, u32[]{:S(2)}) collective-permute-start(bf16[2,128,128]{2,1,0:T(8,128)(2,1)S(1)} %get-tuple-element.18), channel_id=1, source_target_pairs={{0,32},{32,0},{16,48},{48,16},{64,96},{96,64},{80,112},{112,80},{1... | collective-permute-start | bytes 196616 | tf_op jit(solution)/shard_map/ppermute | solution.py:29
  146.8 1.3 fusion.102
  148.2 3.1 %collective-permute-start.2 = (bf16[2,128,128]{2,1,0:T(8,128)(2,1)S(1)}, bf16[2,128,128]{2,1,0:T(8,128)(2,1)S(1)}, u32[]{:S(2)}, u32[]{:S(2)}) collective-permute-start(bf16[2,128,128]{2,1,0:T(8,128)(2,1)S(1)} %get-tuple-element.16), channel_id=1, source_target_pairs={{0,32},{32,0},{16,48},{48,16},{64,96},{96,64},{80,112},{112,80},{1... | collective-permute-start | bytes 196616 | tf_op jit(solution)/shard_map/ppermute | solution.py:29
  151.5 1.0 fusion.18
  152.8 7.2 %collective-permute-start.5 = (bf16[2,128,128]{2,1,0:T(8,128)(2,1)S(1)}, bf16[2,128,128]{2,1,0:T(8,128)(2,1)S(1)}, u32[]{:S(2)}, u32[]{:S(2)}) collective-permute-start(bf16[2,128,128]{2,1,0:T(8,128)(2,1)S(1)} %get-tuple-element.22), channel_id=1, source_target_pairs={{0,64},{64,0},{16,80},{80,16},{32,96},{96,32},{48,112},{112,48},{1... | collective-permute-start | bytes 196616 | tf_op jit(solution)/shard_map/ppermute | solution.py:29
  160.4 2.6 collective-permute-start.4
  163.5 0.3 fusion.107
  163.8 2.1 collective-permute-start.7
  165.9 2.1 collective-permute-done.4
  168.0 0.3 fusion.106
  168.3 1.9 collective-permute-start.6
  170.7 3.8 %collective-permute-done.6 = bf16[2,128,128]{2,1,0:T(8,128)(2,1)S(1)} collective-permute-done((bf16[2,128,128]{2,1,0:T(8,128)(2,1)S(1)}, bf16[2,128,128]{2,1,0:T(8,128)(2,1)S(1)}, u32[]{:S(2)}, u32[]{:S(2)}) %collective-permute-start.6) | collective-permute-done | bytes 65568 | tf_op jit(solution)/shard_map/ppermute | solution.py:29
  174.8 1.9 collective-permute-start.8
  177.1 5.3 %collective-permute-done.8 = bf16[2,128,128]{2,1,0:T(8,128)(2,1)S(1)} collective-permute-done((bf16[2,128,128]{2,1,0:T(8,128)(2,1)S(1)}, bf16[2,128,128]{2,1,0:T(8,128)(2,1)S(1)}, u32[]{:S(2)}, u32[]{:S(2)}) %collective-permute-start.8) | collective-permute-done | bytes 65568 | tf_op jit(solution)/shard_map/ppermute | solution.py:29
  182.7 1.2 convolution_bitcast_fusion
  183.9 4.2 %fusion = f32[2,4,64,1,128]{4,3,2,1,0:T(1,128)S(1)} fusion(f32[2,5,4,64,1]{1,4,3,2,0:T(1,128)S(1)} %copy.51, f32[2,5,4,64,128]{4,3,1,2,0:T(8,128)S(1)} %convolution_bitcast_fusion), kind=kOutput, calls=%fused_computation.1 | convolution fusion | flops 3932160 | bytes 1583104 | tf_op jit(solution)/shard_map/hlnc,hlnci->hnci/dot_general | solution.py:159
  188.1 0.6 multiply_reduce_fusion
  189.1 0.3 mul.148
  189.5 2.1 convolution_convert_fusion
  191.6 74.4 %reduce-scatter.2.cloned.1.call-done = bf16[16,4096]{1,0:T(8,128)(2,1)} async-done(((bf16[256,4096]{1,0:T(8,128)(2,1)}), bf16[16,4096]{1,0:T(8,128)(2,1)}) %reduce-scatter.2.cloned.1.call-update) | async-done | bytes 131088 | tf_op jit(solution)/shard_map/reduce_scatter | solution.py:168
  (83 shorter events, 4.2 us)
Async XLA Ops:
  6.5 182.9 %copy-start = (bf16[256,4096]{1,0:T(8,128)(2,1)S(1)}, bf16[256,4096]{1,0:T(8,128)(2,1)}, u32[]{:S(2)}) copy-start(bf16[256,4096]{1,0:T(8,128)(2,1)} %param.17) | copy-start | bytes 6291460
  6.5 259.5 %reduce-scatter.2.cloned.1.call-start = ((), (), s32[]{:S(2)}) async-start(), calls=%async_computation.1 | async-start | bytes 2228224 | tf_op jit(solution)/shard_map/reduce_scatter | solution.py:168
  6.5 102.3 %copy-start.19 = (pred[4]{0:T(512)(128)(4,1)}, pred[4]{0:T(512)(128)(4,1)S(1)}, u32[]{:S(2)}) copy-start(pred[4]{0:T(512)(128)(4,1)S(1)} %fusion.94) | copy-start | bytes 16
  6.6 95.7 %copy-start.17 = (pred[4]{0:T(512)(128)(4,1)}, pred[4]{0:T(512)(128)(4,1)S(1)}, u32[]{:S(2)}) copy-start(pred[4]{0:T(512)(128)(4,1)S(1)} %fusion.93) | copy-start | bytes 16
  14.9 83.7 %copy-start.21 = (f32[2,4]{1,0:T(2,128)S(1)}, f32[2,4]{1,0:T(2,128)}, u32[]{:S(2)}) copy-start(f32[2,4]{1,0:T(2,128)} %exp.24) | copy-start | bytes 100
  96.5 1.2 copy-start.8
  97.6 3.0 %copy-start.4 = (f32[2,4,128,128]{3,2,1,0:T(8,128)}, f32[2,4,128,128]{3,2,1,0:T(8,128)S(1)}, u32[]{:S(2)}) copy-start(f32[2,4,128,128]{3,2,1,0:T(8,128)S(1)} %fusion.41) | copy-start | bytes 1572868
  100.7 1.6 copy-start.2
  100.7 1.6 copy-start.5
  106.7 1.4 copy-start.1
  109.6 37.2 %collective-permute-start = (bf16[2,128,128]{2,1,0:T(8,128)(2,1)}, bf16[2,128,128]{2,1,0:T(8,128)(2,1)}, u32[]{:S(2)}, u32[]{:S(2)}) collective-permute-start(bf16[2,128,128]{2,1,0:T(8,128)(2,1)} %get-tuple-element.6), channel_id=1, source_target_pairs={{0,16},{16,0},{32,48},{48,32},{64,80},{80,64},{96,112},{112,96},{1... | collective-permute-start | bytes 196616 | tf_op jit(solution)/shard_map/ppermute | solution.py:29
  112.5 31.3 %collective-permute-start.1 = (bf16[2,128,128]{2,1,0:T(8,128)(2,1)}, bf16[2,128,128]{2,1,0:T(8,128)(2,1)S(1)}, u32[]{:S(2)}, u32[]{:S(2)}) collective-permute-start(bf16[2,128,128]{2,1,0:T(8,128)(2,1)} %get-tuple-element.14), channel_id=1, source_target_pairs={{0,16},{16,0},{32,48},{48,32},{64,80},{80,64},{96,112},{112,96},{1... | collective-permute-start | bytes 196616 | tf_op jit(solution)/shard_map/ppermute | solution.py:29
  122.2 5.4 %copy-start.20 = (pred[4]{0:T(512)(128)(4,1)S(1)}, pred[4]{0:T(512)(128)(4,1)}, u32[]{:S(2)}) copy-start(pred[4]{0:T(512)(128)(4,1)} %copy-done.19) | copy-start | bytes 16
  122.2 6.9 %copy-start.3 = (f32[2,1,2,2,128,128]{5,4,3,2,0,1:T(8,128)S(1)}, f32[2,1,2,2,128,128]{5,4,3,2,0,1:T(8,128)}, u32[]{:S(2)}) copy-start(f32[2,1,2,2,128,128]{5,4,3,2,0,1:T(8,128)} %rev.17) | copy-start | bytes 1572868
  127.5 6.0 %copy-start.7 = (f32[4,64,2,128]{3,2,1,0:T(2,128)S(1)}, f32[4,64,2,128]{3,2,1,0:T(2,128)}, u32[]{:S(2)}) copy-start(f32[4,64,2,128]{3,2,1,0:T(2,128)} %reshape.176) | copy-start | bytes 786436
  129.0 5.2 %copy-start.6 = (f32[2,4,64,128]{3,2,1,0:T(8,128)S(1)}, f32[2,4,64,128]{3,2,1,0:T(8,128)}, u32[]{:S(2)}) copy-start(f32[2,4,64,128]{3,2,1,0:T(8,128)} %fusion.36) | copy-start | bytes 786436
  133.6 0.7 copy-start.16
  133.6 4.3 %copy-start.12 = (f32[2,2,4,64,1]{1,4,3,2,0:T(1,128)S(1)}, f32[2,2,4,64,1]{1,4,3,2,0:T(1,128)}, u32[]{:S(2)}) copy-start(f32[2,2,4,64,1]{1,4,3,2,0:T(1,128)} %copy.43) | copy-start | bytes 12292
  135.4 7.0 %copy-start.10 = (f32[2,4,128,128]{3,2,1,0:T(8,128)S(1)}, f32[2,4,128,128]{3,2,1,0:T(8,128)}, u32[]{:S(2)}) copy-start(f32[2,4,128,128]{3,2,1,0:T(8,128)} %convolution_select_fusion) | copy-start | bytes 1572868
  135.4 8.2 %copy-start.15 = (f32[2,5,4,64,1]{3,2,1,0,4:T(4,128)S(1)}, f32[2,5,4,64,1]{3,2,1,0,4:T(4,128)}, u32[]{:S(2)}) copy-start(f32[2,5,4,64,1]{3,2,1,0,4:T(4,128)} %slice_bitcast_fusion) | copy-start | bytes 30724
  137.9 5.9 %copy-start.11 = (f32[2,128,128]{2,1,0:T(8,128)S(1)}, f32[2,128,128]{2,1,0:T(8,128)}, u32[]{:S(2)}) copy-start(f32[2,128,128]{2,1,0:T(8,128)} %get-tuple-element.15) | copy-start | bytes 393220
  144.1 8.4 %collective-permute-start.3 = (bf16[2,128,128]{2,1,0:T(8,128)(2,1)S(1)}, bf16[2,128,128]{2,1,0:T(8,128)(2,1)S(1)}, u32[]{:S(2)}, u32[]{:S(2)}) collective-permute-start(bf16[2,128,128]{2,1,0:T(8,128)(2,1)S(1)} %get-tuple-element.18), channel_id=1, source_target_pairs={{0,32},{32,0},{16,48},{48,16},{64,96},{96,64},{80,112},{112,80},{1... | collective-permute-start | bytes 196616 | tf_op jit(solution)/shard_map/ppermute | solution.py:29
  148.2 11.9 %collective-permute-start.2 = (bf16[2,128,128]{2,1,0:T(8,128)(2,1)S(1)}, bf16[2,128,128]{2,1,0:T(8,128)(2,1)S(1)}, u32[]{:S(2)}, u32[]{:S(2)}) collective-permute-start(bf16[2,128,128]{2,1,0:T(8,128)(2,1)S(1)} %get-tuple-element.16), channel_id=1, source_target_pairs={{0,32},{32,0},{16,48},{48,16},{64,96},{96,64},{80,112},{112,80},{1... | collective-permute-start | bytes 196616 | tf_op jit(solution)/shard_map/ppermute | solution.py:29
  152.8 10.6 %collective-permute-start.5 = (bf16[2,128,128]{2,1,0:T(8,128)(2,1)S(1)}, bf16[2,128,128]{2,1,0:T(8,128)(2,1)S(1)}, u32[]{:S(2)}, u32[]{:S(2)}) collective-permute-start(bf16[2,128,128]{2,1,0:T(8,128)(2,1)S(1)} %get-tuple-element.22), channel_id=1, source_target_pairs={{0,64},{64,0},{16,80},{80,16},{32,96},{96,32},{48,112},{112,48},{1... | collective-permute-start | bytes 196616 | tf_op jit(solution)/shard_map/ppermute | solution.py:29
  160.4 7.7 %collective-permute-start.4 = (bf16[2,128,128]{2,1,0:T(8,128)(2,1)S(1)}, bf16[2,128,128]{2,1,0:T(8,128)(2,1)S(1)}, u32[]{:S(2)}, u32[]{:S(2)}) collective-permute-start(bf16[2,128,128]{2,1,0:T(8,128)(2,1)S(1)} %get-tuple-element.20), channel_id=1, source_target_pairs={{0,64},{64,0},{16,80},{80,16},{32,96},{96,32},{48,112},{112,48},{1... | collective-permute-start | bytes 196616 | tf_op jit(solution)/shard_map/ppermute | solution.py:29
  163.8 6.9 %collective-permute-start.7 = (bf16[2,128,128]{2,1,0:T(8,128)(2,1)S(1)}, bf16[2,128,128]{2,1,0:T(8,128)(2,1)S(1)}, u32[]{:S(2)}, u32[]{:S(2)}) collective-permute-start(bf16[2,128,128]{2,1,0:T(8,128)(2,1)S(1)} %get-tuple-element.26), channel_id=1, source_target_pairs={{0,128},{128,0},{16,144},{144,16},{32,160},{160,32},{48,176},{176,... | collective-permute-start | bytes 196616 | tf_op jit(solution)/shard_map/ppermute | solution.py:29
  168.3 6.2 %collective-permute-start.6 = (bf16[2,128,128]{2,1,0:T(8,128)(2,1)S(1)}, bf16[2,128,128]{2,1,0:T(8,128)(2,1)S(1)}, u32[]{:S(2)}, u32[]{:S(2)}) collective-permute-start(bf16[2,128,128]{2,1,0:T(8,128)(2,1)S(1)} %get-tuple-element.24), channel_id=1, source_target_pairs={{0,128},{128,0},{16,144},{144,16},{32,160},{160,32},{48,176},{176,... | collective-permute-start | bytes 196616 | tf_op jit(solution)/shard_map/ppermute | solution.py:29
  174.8 7.7 %collective-permute-start.8 = (bf16[2,128,128]{2,1,0:T(8,128)(2,1)S(1)}, bf16[2,128,128]{2,1,0:T(8,128)(2,1)S(1)}, u32[]{:S(2)}, u32[]{:S(2)}) collective-permute-start(bf16[2,128,128]{2,1,0:T(8,128)(2,1)S(1)} %fusion.19), channel_id=1, source_target_pairs={{0,256},{256,0},{16,272},{272,16},{32,288},{288,32},{48,304},{304,... | collective-permute-start | bytes 196616 | tf_op jit(solution)/shard_map/ppermute | solution.py:29
  182.6 5.4 %copy-start.9 = (f32[2,4,64,128]{3,2,1,0:T(8,128)S(1)}, f32[2,4,64,128]{3,2,1,0:T(8,128)}, u32[]{:S(2)}) copy-start(f32[2,4,64,128]{3,2,1,0:T(8,128)} %copy-done.8) | copy-start | bytes 786436
  182.7 5.4 %copy-start.13 = (f32[2,4,64,1,128]{4,3,2,1,0:T(1,128)S(1)}, f32[2,4,64,1,128]{4,3,2,1,0:T(1,128)}, u32[]{:S(2)}) copy-start(f32[2,4,64,1,128]{4,3,2,1,0:T(1,128)} %fusion.29) | copy-start | bytes 786436
  182.7 5.4 %copy-start.18 = (f32[4,64,2]{1,0,2:T(4,128)S(1)}, f32[4,64,2]{1,0,2:T(4,128)}, u32[]{:S(2)}) copy-start(f32[4,64,2]{1,0,2:T(4,128)} %slice_bitcast_fusion.2) | copy-start | bytes 6148
  183.9 5.6 %copy-start.14 = (bf16[256,256]{1,0:T(8,128)(2,1)S(1)}, bf16[256,256]{1,0:T(8,128)(2,1)}, u32[]{:S(2)}) copy-start(bf16[256,256]{1,0:T(8,128)(2,1)} %param.13) | copy-start | bytes 393220
Sparse Core Ops, SparseCore 0:
  191.7 74.2 reduce-scatter.1
where the time goes:
time: 274 us; the launch traced here: 273 us
  other arithmetic  85.6 us (31%)
  waiting for transfers between devices  85.6 us (31%)
  matrix products  42 us (15%)
  starting transfers between devices  26.2 us (10%)
  local copies, waits for them, and re-layouts  19.3 us (7%)
  between operations  14.2 us (5%)
    reduce_scatter x1, waiting for transfers between devices, on_device(): lax.psum_scatter(jnp.dot(normed, w_out, preferred_element_type=jnp.float3...  74.4 us
    another operation x1, other arithmetic, on_device(): jax.scipy.linalg.solve_triangular(lower_keys, strength[..., None] * key_r...  40.1 us
    another operation x4, other arithmetic, on_device(): jax.scipy.linalg.solve_triangular(lower_values, strength[..., None] * val...  39.4 us
    ppermute x9, starting transfers between devices, swapped(): return lax.ppermute(block, axis, route)  26.2 us
    dot_general x23, matrix products, matmul(): return jnp.einsum('...ij,...jk->...ik', left, right, precision=PRECISE)  16.1 us
    ppermute x9, waiting for transfers between devices, swapped(): return lax.ppermute(block, axis, route)  11.2 us
  transfers between devices with their start and end apart: 10, of which 4 were waited for; matrix products, arithmetic and copies ran while one was open for 13% of the time, Pallas kernels for 0%

commit v1 on v0

v1 whole, which is shorter than its diff:
```python
import jax
import jax.numpy as jnp
from jax import lax
from jax.experimental import pallas as pl
from jax.experimental.pallas import tpu as pltpu
from jax.sharding import PartitionSpec as P

DK = 128
BLOCK = 64
EPSILON = 1e-06
F32 = jnp.float32
BF16 = jnp.bfloat16
VMEM = pl.BlockSpec(memory_space=pltpu.VMEM)
SMEM = pl.BlockSpec(memory_space=pltpu.SMEM)
VMEM_BYTES = 48 * 1024 * 1024


def dot(left, right, dims=((1,), (0,)), precision=None):
    return lax.dot_general(left, right, (dims, ((), ())), precision=precision, preferred_element_type=F32)


def halves(matrix):
    high = matrix.astype(BF16)
    return high, (matrix - high.astype(F32)).astype(BF16)


def dot3(left, right):
    (lh, ll), (rh, rl) = left, right
    return dot(lh, rh) + (dot(lh, rl) + dot(ll, rh))


def dot2(left, right):
    high, low = halves(left)
    return dot(high, right) + dot(low, right)


def block_masks(tokens):
    row = lax.broadcasted_iota(jnp.int32, (tokens, tokens), 0)
    col = lax.broadcasted_iota(jnp.int32, (tokens, tokens), 1)
    same = row // BLOCK == col // BLOCK
    return row, col, same


def states_kernel(k_ref, v_ref, lf_ref, wr_ref, x_ref, y_ref, w_ref, u_ref, rows_ref):
    tokens = k_ref.shape[0]
    heads = lf_ref.shape[0]
    blocks = tokens // BLOCK
    row, col, same = block_masks(tokens)
    inclusive = same & (row >= col)
    strict = same & (row > col)
    eye = (row == col).astype(F32)
    log_forget = lf_ref[...]
    rate = wr_ref[...]
    exact = lax.Precision.HIGHEST
    cum = dot(log_forget, inclusive.astype(F32), ((1,), (1,)), exact)
    total = dot(log_forget, same.astype(F32), ((1,), (1,)), exact)
    pad = jnp.zeros((8 - 3 * heads, tokens), F32)
    columns = jnp.concatenate([cum, total, rate, pad], axis=0).T
    eye_state = (
        lax.broadcasted_iota(jnp.int32, (DK, DK), 0) == lax.broadcasted_iota(jnp.int32, (DK, DK), 1)
    ).astype(F32)
    inv_key_rows = []
    lowers, keys, norms = [], [], []
    for h in range(heads):
        key = k_ref[:, h * DK : (h + 1) * DK]
        key_f = key.astype(F32)
        key_key = dot(key, key, ((1,), (1,)))
        inv_col = lax.rsqrt(jnp.sum(key_f * key_f, axis=1, keepdims=True) + EPSILON)
        inv_row = lax.rsqrt(jnp.sum(key_key * eye, axis=0, keepdims=True) + EPSILON)
        inv_key_rows.append(inv_row)
        rate_col = columns[:, 2 * heads + h : 2 * heads + h + 1]
        lowers.append(jnp.where(strict, key_key * (rate_col * inv_col) * inv_row, 0.0))
        keys.append((key, key_f))
        norms.append((inv_col, inv_row))
    inverses = [eye - jnp.where(row // 2 == col // 2, lower, 0.0) for lower in lowers]
    width = 2
    while width < BLOCK:
        band = (row // width != col // width) & (row // (2 * width) == col // (2 * width))
        nexts = []
        for h in range(heads):
            inverse = halves(inverses[h])
            inner = dot3(halves(jnp.where(band, lowers[h], 0.0)), inverse)
            nexts.append(inverses[h] - dot3(inverse, halves(inner)))
        inverses = nexts
        width *= 2
    for h in range(heads):
        key, key_f = keys[h]
        inv_col, inv_row = norms[h]
        value = v_ref[:, h * DK : (h + 1) * DK]
        cum_row = cum[h : h + 1]
        cum_col = columns[:, h : h + 1]
        total_col = columns[:, heads + h : heads + h + 1]
        rate_row = rate[h : h + 1]
        fading = jnp.exp(jnp.where(inclusive, cum_col - cum_row, -1e30))
        solved = inverses[h] * rate_row
        bases = dot2(solved * inv_row, key)
        writes = dot2(solved * fading, value)
        w_ref[:, h * DK : (h + 1) * DK] = bases
        u_ref[:, h * DK : (h + 1) * DK] = writes
        both = jnp.concatenate(
            [writes * (jnp.exp(total_col - cum_col) * inv_col), bases * inv_col], axis=1
        )
        both_high, both_low = halves(both)
        leaf = []
        for g in range(blocks):
            span = slice(g * BLOCK, (g + 1) * BLOCK)
            turned = key_f[span].T.astype(BF16)
            raw = dot(turned, both_high[span]) + dot(turned, both_low[span])
            fade = jnp.exp(total[h : h + 1, g * BLOCK : g * BLOCK + 1])
            leaf.append(jnp.concatenate([raw[:, :DK], fade * (eye_state - raw[:, DK:])], axis=1))
        short = [x.astype(BF16) for x in leaf]

        def merge(lead, trail):
            moved = dot(trail[:, DK:].astype(BF16), lead.astype(BF16))
            return jnp.concatenate([moved[:, :DK] + trail[:, :DK], moved[:, DK:]], axis=1)

        first = merge(leaf[0], leaf[1])
        second = merge(leaf[2], leaf[3])
        y_ref[h, 0] = short[0]
        y_ref[h, 1] = first.astype(BF16)
        y_ref[h, 2] = dot(short[2][:, DK:], first.astype(BF16)).astype(BF16)
        y_ref[h, 3] = short[2]
        x_ref[h] = merge(first, second).astype(BF16)
    rows_ref[...] = jnp.concatenate([cum] + inv_key_rows + [jnp.zeros((8 - 2 * heads, tokens), F32)], axis=0)


def reads_kernel(q_ref, k_ref, w_ref, u_ref, rows_ref, y_ref, lw_ref, core_ref, lift_ref):
    tokens = k_ref.shape[0]
    heads = y_ref.shape[0]
    row, col, same = block_masks(tokens)
    inclusive = same & (row >= col)
    rows = rows_ref[...]
    columns = rows.T
    levels = lw_ref.shape[1]
    weights = lw_ref[...].reshape(heads * levels, tokens).T
    for h in range(heads):
        lanes = slice(h * DK, (h + 1) * DK)
        query = q_ref[:, lanes]
        key = k_ref[:, lanes]
        query_f = query.astype(F32)
        inv_query = lax.rsqrt(jnp.sum(query_f * query_f, axis=1, keepdims=True) + EPSILON)
        query_key = dot(query, key, ((1,), (1,))) * inv_query * rows[heads + h : heads + h + 1]
        cum_col = columns[:, h : h + 1]
        fading = jnp.exp(jnp.where(inclusive, cum_col - rows[h : h + 1], -1e30))
        own = dot3(halves(query_key * fading), halves(u_ref[:, lanes]))
        masked = jnp.where(inclusive, query_key, 0.0)
        reach = jnp.exp(cum_col) * (query_f * inv_query - dot3(halves(masked), halves(w_ref[:, lanes])))
        reach_s = reach.astype(BF16)

        def weight(level, span):
            at = h * levels + level
            return weights[span, at : at + 1]

        spans = [slice(g * BLOCK, (g + 1) * BLOCK) for g in range(4)]
        read1 = dot(reach_s[spans[1]], y_ref[h, 0])
        read2 = dot(reach_s[spans[2]], y_ref[h, 1])
        read3 = dot(reach_s[spans[3]], y_ref[h, 2])
        near3 = dot(reach_s[spans[3]], y_ref[h, 3, :, :DK])
        core_ref[spans[0], lanes] = weight(0, spans[0]) * own[spans[0]]
        core_ref[spans[1], lanes] = weight(0, spans[1]) * own[spans[1]] + weight(1, spans[1]) * read1[:, :DK]
        core_ref[spans[2], lanes] = weight(0, spans[2]) * own[spans[2]] + weight(2, spans[2]) * read2[:, :DK]
        core_ref[spans[3], lanes] = (
            weight(0, spans[3]) * own[spans[3]]
            + weight(1, spans[3]) * near3
            + weight(2, spans[3]) * read3[:, :DK]
        )
        lift_ref[spans[0], lanes] = reach_s[spans[0]]
        lift_ref[spans[1], lanes] = read1[:, DK:].astype(BF16)
        lift_ref[spans[2], lanes] = read2[:, DK:].astype(BF16)
        lift_ref[spans[3], lanes] = read3[:, DK:].astype(BF16)


def merge_kernel(bit, pos_ref, mine_ref, theirs_ref, before_ref, total_ref, level_ref, after_ref):
    upper = (pos_ref[0] >> bit) & 1 == 1
    heads = mine_ref.shape[0]

    def joined(lead, trail):
        moved = dot(trail[:, DK:], lead)
        return jnp.concatenate([moved[:, :DK] + trail[:, :DK].astype(F32), moved[:, DK:]], axis=1).astype(BF16)

    @pl.when(upper)
    def _():
        for h in range(heads):
            total_ref[h] = joined(theirs_ref[h], mine_ref[h])
        for h in range(heads):
            if bit == 0:
                level_ref[h] = theirs_ref[h, :, :DK]
                after_ref[h] = theirs_ref[h, :, DK:]
            else:
                read = dot(before_ref[h], theirs_ref[h]).astype(BF16)
                level_ref[h] = read[:, :DK]
                after_ref[h] = read[:, DK:]

    @pl.when(jnp.logical_not(upper))
    def _():
        for h in range(heads):
            total_ref[h] = joined(mine_ref[h], theirs_ref[h])
        level_ref[...] = jnp.zeros(level_ref.shape, level_ref.dtype)
        after_ref[...] = before_ref[...]


def final_kernel(outer, ring, pos_ref, core_ref, lift_ref, last_ref, before_ref, lw_ref, gate_ref, out_w_ref, *rest):
    level_refs, out_ref, norm_ref, turn_ref = rest[:-3], rest[-3], rest[-2], rest[-1]
    heads = before_ref.shape[0]
    tokens = core_ref.shape[0]
    levels = lw_ref.shape[1]
    weights = lw_ref[...].reshape(heads * levels, tokens).T
    upper = ((pos_ref[0] >> (outer - 1)) & 1 == 1).astype(F32)
    normed = []
    for h in range(heads):
        lanes = slice(h * DK, (h + 1) * DK)
        lifted = lift_ref[:, lanes].astype(F32)
        last = (dot(before_ref[h], last_ref[h]) * upper).astype(BF16)
        scaled, stack = [], []
        for b in range(outer):
            at = h * levels + levels - outer + b
            scaled.append((lifted * weights[:, at : at + 1]).astype(BF16))
            stack.append(level_refs[b][h] if b < outer - 1 else last)
        core = core_ref[:, lanes] + dot(jnp.concatenate(scaled, axis=1), jnp.concatenate(stack, axis=0))
        core = core * lax.rsqrt(jnp.mean(core * core, axis=1, keepdims=True) + EPSILON)
        gate = gate_ref[:, lanes].astype(F32)
        normed.append((core * (gate / (1.0 + jnp.exp(-gate)))).astype(BF16))
    norm_ref[...] = jnp.concatenate(normed, axis=1)
    chunk = tokens // ring
    for j in range(ring):
        owner = lax.rem(pos_ref[1] + ring + ring // 2 - j, ring)
        turn_ref[j * chunk : (j + 1) * chunk] = norm_ref[pl.ds(pl.multiple_of(owner * chunk, chunk), chunk)]
    normed = turn_ref[...]
    step = 512
    for c in range(0, out_ref.shape[1], step):
        out_ref[:, c : c + step] = dot(normed, out_w_ref[:, c : c + step]).astype(BF16)


def call(body, out_shape, specs, flops, bytes_accessed, scratch=()):
    return pl.pallas_call(
        body,
        out_shape=out_shape,
        in_specs=specs,
        out_specs=jax.tree.map(lambda _: VMEM, out_shape),
        scratch_shapes=scratch,
        compiler_params=pltpu.CompilerParams(vmem_limit_bytes=VMEM_BYTES),
        cost_estimate=pl.CostEstimate(flops=flops, bytes_accessed=bytes_accessed, transcendentals=0),
    )


def ring_sum(partial, ring):
    chunk = partial.shape[0] // ring
    half = ring // 2
    right = [(i, (i + 1) % ring) for i in range(ring)]
    left = [(i, (i - 1) % ring) for i in range(ring)]

    def term(j):
        return lax.slice_in_dim(partial, j * chunk, (j + 1) * chunk).astype(F32)

    ahead = term(0).astype(BF16)
    behind = term(ring - 1).astype(BF16)
    for t in range(1, half):
        ahead = (lax.ppermute(ahead, "head", right).astype(F32) + term(t)).astype(BF16)
        if t < half - 1:
            behind = (lax.ppermute(behind, "head", left).astype(F32) + term(ring - 1 - t)).astype(BF16)
    ahead = lax.ppermute(ahead, "head", right).astype(F32)
    behind = lax.ppermute(behind, "head", left).astype(F32)
    return (ahead + behind + term(half)).astype(BF16)


def on_device(queries, keys, values, gate, log_forget, write_rate, level_weight, w_out):
    tokens = queries.shape[0]
    heads = log_forget.shape[0]
    seq = lax.axis_size("seq")
    outer = seq.bit_length() - 1
    ring = lax.axis_size("head")
    position = jnp.stack([lax.axis_index("seq"), lax.axis_index("head")]).astype(jnp.int32)
    wide = heads * DK

    def shape(dims, dtype=BF16):
        return jax.ShapeDtypeStruct(dims, dtype)

    total, inner, bases, writes, rows = call(
        states_kernel,
        (
            shape((heads, DK, 2 * DK)),
            shape((heads, 4, DK, 2 * DK)),
            shape((tokens, wide), F32),
            shape((tokens, wide), F32),
            shape((8, tokens), F32),
        ),
        [VMEM] * 4,
        2_000_000_000,
        1_000_000,
    )(keys, values, log_forget, write_rate)

    core, lifted = call(
        reads_kernel,
        (shape((tokens, wide), F32), shape((tokens, wide))),
        [VMEM] * 7,
        1_000_000_000,
        1_000_000,
    )(queries, keys, bases, writes, rows, inner, level_weight)

    before = jnp.zeros((heads, DK, DK), BF16) + jnp.eye(DK, dtype=BF16)
    collected = []
    for b in range(outer - 1):
        theirs = lax.ppermute(total, "seq", [(i, i ^ (1 << b)) for i in range(seq)])
        total, level, before = call(
            lambda *refs, b=b: merge_kernel(b, *refs),
            (shape((heads, DK, 2 * DK)), shape((heads, DK, DK)), shape((heads, DK, DK))),
            [SMEM] + [VMEM] * 3,
            40_000_000,
            500_000,
        )(position, total, theirs, before)
        collected.append(level)
    top = 1 << (outer - 1)
    last = lax.ppermute(total[:, :, :DK], "seq", [(i, i + top) for i in range(top)])
    partial = call(
        lambda *refs: final_kernel(outer, ring, *refs),
        shape((tokens, w_out.shape[1])),
        [SMEM] + [VMEM] * (7 + outer - 1),
        600_000_000,
        5_000_000,
        [pltpu.VMEM((tokens, wide), BF16)] * 2,
    )(position, core, lifted, last, before, level_weight, gate, w_out, *collected)
    return ring_sum(partial, ring)


def solution(mesh):
    in_specs = (
        P("seq", "head"),
        P("seq", "head"),
        P("seq", "head"),
        P("seq", "head"),
        P("head", "seq"),
        P("head", "seq"),
        P("head", None, "seq"),
        P("head", None),
    )
    out_specs = P(("seq", "head"), None)
    return jax.shard_map(
        on_device, mesh=mesh, in_specs=in_specs, out_specs=out_specs, check_vma=False
    )
```

time: 274 us -> 137 us (0.50)
  the two profiles are of different devices: /device:TPU:6 before, /device:TPU:62 now
where the time goes in v1:
time: 137 us; the launch traced here: 136 us
  starting transfers between devices  59.9 us (44%)
  waiting for transfers between devices  59.7 us (44%)
  Pallas kernels  11.9 us (9%)
  local copies, waits for them, and re-layouts  3.24 us (2%)
    ppermute x7, starting transfers between devices, ring_sum(): lax.ppermute(ahead, 'head', right).astype(F32) + term(t)  24.2 us
    ppermute x6, waiting for transfers between devices, ring_sum(): lax.ppermute(behind, 'head', left).astype(F32) + term(ring - 1 - t)  18.6 us
    ppermute x6, starting transfers between devices, ring_sum(): lax.ppermute(behind, 'head', left).astype(F32) + term(ring - 1 - t)  17.8 us
    ppermute x7, waiting for transfers between devices, ring_sum(): lax.ppermute(ahead, 'head', right).astype(F32) + term(t)  15.8 us
    ppermute x4, waiting for transfers between devices, on_device(): theirs = lax.ppermute(total, 'seq', [(i, i ^ 1 << b) for i in range(seq)])  15.2 us
    ppermute x4, starting transfers between devices, on_device(): theirs = lax.ppermute(total, 'seq', [(i, i ^ 1 << b) for i in range(seq)])  10.7 us
    pallas_call x1, Pallas kernels, on_device(): call(states_kernel, (shape((heads, DK, 2 * DK)), shape((heads, 4, DK, 2 *...  5.6 us
    ppermute x1, waiting for transfers between devices, on_device(): lax.ppermute(total[:, :, :DK], 'seq', [(i, i + top) for i in range(top)])  5.16 us
  transfers between devices with their start and end apart: 20, of which 19 were waited for; matrix products, arithmetic and copies ran while one was open for 0% of the time, Pallas kernels for 1%

profile of v1, /device:TPU:62, one launch (start us, length us, event | category | flops | bytes accessed | tf_op | source)
XLA Modules:
  0.0 136.2 jit_solution(5653188241925656798)
XLA Ops:
  0.0 0.9 copy-done.3
  0.9 0.9 copy-done.5
  1.8 0.7 copy-done.7
  2.5 0.7 copy-done.8
  3.2 5.6 %shard_map.82 = (bf16[2,128,256]{2,1,0:T(8,128)(2,1)S(1)}, bf16[2,4,128,256]{3,2,1,0:T(8,128)(2,1)S(1)}, f32[256,256]{1,0:T(8,128)S(1)}, f32[256,256]{1,0:T(8,128)S(1)}, f32[8,256]{1,0:T(8,128)S(1)}) custom-call(bf16[256,256]{1,0:T(8,128)(2,1)S(1)} %copy-done.5, bf16[256,256]{1,0:T(8,128)(2,1)S(1)} %copy-done.3, f32[2,256]{1,0:T(2,128)S(1)} %copy-done.7, ...), custom_call_target="tpu_custom_call" | custom-call | flops 2000000000 | bytes 1000000 | tf_op jit(solution)/shard_map/pallas_call | solution.py:278
  8.8 1.9 %collective-permute-start = (bf16[2,128,256]{2,1,0:T(8,128)(2,1)S(1)}, bf16[2,128,256]{2,1,0:T(8,128)(2,1)S(1)}, u32[]{:S(2)}, u32[]{:S(2)}) collective-permute-start(bf16[2,128,256]{2,1,0:T(8,128)(2,1)S(1)} %get-tuple-element.30.refs_1_), channel_id=1, source_target_pairs={{0,16},{16,0},{32,48},{48,32},{64,80},{80,64},{96,112},{112,96},{1... | collective-permute-start | bytes 393224 | tf_op jit(solution)/shard_map/ppermute | solution.py:303
  10.7 0.1 pad_add_fusion.refs_0_
  10.8 1.2 collective-permute-done.refs_2_
  12.0 0.7 shard_map.84
  12.8 2.7 %collective-permute-start.1 = (bf16[2,128,256]{2,1,0:T(8,128)(2,1)S(1)}, bf16[2,128,256]{2,1,0:T(8,128)(2,1)S(1)}, u32[]{:S(2)}, u32[]{:S(2)}) collective-permute-start(bf16[2,128,256]{2,1,0:T(8,128)(2,1)S(1)} %get-tuple-element.31.refs_1_), channel_id=1, source_target_pairs={{0,32},{16,48},{32,0},{48,16},{64,96},{80,112},{96,64},{112,80},{1... | collective-permute-start | bytes 393224 | tf_op jit(solution)/shard_map/ppermute | solution.py:303
  15.5 4.7 %collective-permute-done.1.refs_2_ = bf16[2,128,256]{2,1,0:T(8,128)(2,1)S(1)} collective-permute-done((bf16[2,128,256]{2,1,0:T(8,128)(2,1)S(1)}, bf16[2,128,256]{2,1,0:T(8,128)(2,1)S(1)}, u32[]{:S(2)}, u32[]{:S(2)}) %collective-permute-start.1) | collective-permute-done | bytes 131104 | tf_op jit(solution)/shard_map/ppermute | solution.py:303
  20.2 0.8 shard_map.85
  21.0 3.3 %collective-permute-start.2 = (bf16[2,128,256]{2,1,0:T(8,128)(2,1)S(1)}, bf16[2,128,256]{2,1,0:T(8,128)(2,1)S(1)}, u32[]{:S(2)}, u32[]{:S(2)}) collective-permute-start(bf16[2,128,256]{2,1,0:T(8,128)(2,1)S(1)} %get-tuple-element.33.refs_1_), channel_id=1, source_target_pairs={{0,64},{16,80},{32,96},{48,112},{64,0},{80,16},{96,32},{112,48},{1... | collective-permute-start | bytes 393224 | tf_op jit(solution)/shard_map/ppermute | solution.py:303
  24.3 5.1 %collective-permute-done.2.refs_2_ = bf16[2,128,256]{2,1,0:T(8,128)(2,1)S(1)} collective-permute-done((bf16[2,128,256]{2,1,0:T(8,128)(2,1)S(1)}, bf16[2,128,256]{2,1,0:T(8,128)(2,1)S(1)}, u32[]{:S(2)}, u32[]{:S(2)}) %collective-permute-start.2) | collective-permute-done | bytes 131104 | tf_op jit(solution)/shard_map/ppermute | solution.py:303
  29.4 0.8 shard_map.86
  30.1 0.0 copy-start
  30.1 0.0 copy-start.1
  30.1 2.8 %collective-permute-start.3 = (bf16[2,128,256]{2,1,0:T(8,128)(2,1)S(1)}, bf16[2,128,256]{2,1,0:T(8,128)(2,1)S(1)}, u32[]{:S(2)}, u32[]{:S(2)}) collective-permute-start(bf16[2,128,256]{2,1,0:T(8,128)(2,1)S(1)} %get-tuple-element.35.refs_1_), channel_id=1, source_target_pairs={{0,128},{16,144},{32,160},{48,176},{64,192},{80,208},{96,224},{112... | collective-permute-start | bytes 393224 | tf_op jit(solution)/shard_map/ppermute | solution.py:303
  32.9 4.2 %collective-permute-done.3.refs_2_ = bf16[2,128,256]{2,1,0:T(8,128)(2,1)S(1)} collective-permute-done((bf16[2,128,256]{2,1,0:T(8,128)(2,1)S(1)}, bf16[2,128,256]{2,1,0:T(8,128)(2,1)S(1)}, u32[]{:S(2)}, u32[]{:S(2)}) %collective-permute-start.3) | collective-permute-done | bytes 131104 | tf_op jit(solution)/shard_map/ppermute | solution.py:303
  37.1 0.8 shard_map.87
  37.9 1.3 collective-permute-start.4
  39.2 0.0 copy-done.2
  39.2 0.0 copy-done.4
  39.2 0.0 copy-done.6
  39.3 1.2 shard_map.83
  40.4 5.2 %collective-permute-done.4.refs_3_ = bf16[2,128,128]{2,1,0:T(8,128)(2,1)S(1)} collective-permute-done((bf16[2,128,128]{2,1,0:T(8,128)(2,1)S(1)}, bf16[2,128,128]{2,1,0:T(8,128)(2,1)S(1)}, u32[]{:S(2)}, u32[]{:S(2)}) %collective-permute-start.4) | collective-permute-done | bytes 65568 | tf_op jit(solution)/shard_map/ppermute | solution.py:313
  45.6 2.1 %shard_map.88 = bf16[256,4096]{1,0:T(8,128)(2,1)S(1)} custom-call(s32[2]{0:T(128)S(1)} %pad_add_fusion.refs_0_, f32[256,256]{1,0:T(8,128)S(1)} %get-tuple-element.28.refs_1_, bf16[256,256]{1,0:T(8,128)(2,1)S(1)} %get-tuple-element.29.refs_2_, bf16[2,128,128]{2,1,0:T(8,128)(2,1)S(1)} %collective-permute-done.4.refs_3_, ...), custom_call_target="tpu_custom_call" | custom-call | flops 600000000 | bytes 5000000 | tf_op jit(solution)/shard_map/pallas_call | solution.py:314
  47.7 3.8 %collective-permute-start.5 = (bf16[16,4096]{1,0:T(8,128)(2,1)S(1)}, bf16[16,4096]{1,0:T(8,128)(2,1)S(1)}, u32[]{:S(2)}, u32[]{:S(2)}) collective-permute-start(bf16[16,4096]{1,0:T(8,128)(2,1)S(1)} %get-tuple-element.55), channel_id=1, source_target_pairs={{0,1},{1,2},{2,3},{3,4},{4,5},{5,6},{6,7},{7,8},{8,9},{9,10},{10,1... | collective-permute-start | bytes 393224 | tf_op jit(solution)/shard_map/ppermute | solution.py:258
  51.5 2.0 %collective-permute-start.13 = (bf16[16,4096]{1,0:T(8,128)(2,1)S(1)}, bf16[16,4096]{1,0:T(8,128)(2,1)S(1)}, u32[]{:S(2)}, u32[]{:S(2)}) collective-permute-start(bf16[16,4096]{1,0:T(8,128)(2,1)S(1)} %get-tuple-element.56), channel_id=1, source_target_pairs={{0,15},{1,0},{2,1},{3,2},{4,3},{5,4},{6,5},{7,6},{8,7},{9,8},{10,9... | collective-permute-start | bytes 393224 | tf_op jit(solution)/shard_map/ppermute | solution.py:260
  53.6 1.2 collective-permute-done.5
  54.8 4.4 %collective-permute-start.6 = (bf16[16,4096]{1,0:T(8,128)(2,1)S(1)}, bf16[16,4096]{1,0:T(8,128)(2,1)S(1)}, u32[]{:S(2)}, u32[]{:S(2)}) collective-permute-start(bf16[16,4096]{1,0:T(8,128)(2,1)S(1)} %add_convert_fusion.13), channel_id=1, source_target_pairs={{0,1},{1,2},{2,3},{3,4},{4,5},{5,6},{6,7},{7,8},{8,9},{9,10},{10,1... | collective-permute-start | bytes 393224 | tf_op jit(solution)/shard_map/ppermute | solution.py:258
  59.2 0.0 collective-permute-done.13
  59.2 7.9 %collective-permute-done.6 = bf16[16,4096]{1,0:T(8,128)(2,1)S(1)} collective-permute-done((bf16[16,4096]{1,0:T(8,128)(2,1)S(1)}, bf16[16,4096]{1,0:T(8,128)(2,1)S(1)}, u32[]{:S(2)}, u32[]{:S(2)}) %collective-permute-start.6) | collective-permute-done | bytes 131104 | tf_op jit(solution)/shard_map/ppermute | solution.py:258
  67.1 0.1 add_convert_fusion.12
  67.2 1.9 %collective-permute-start.7 = (bf16[16,4096]{1,0:T(8,128)(2,1)S(1)}, bf16[16,4096]{1,0:T(8,128)(2,1)S(1)}, u32[]{:S(2)}, u32[]{:S(2)}) collective-permute-start(bf16[16,4096]{1,0:T(8,128)(2,1)S(1)} %get-tuple-element.53), channel_id=1, source_target_pairs={{0,1},{1,2},{2,3},{3,4},{4,5},{5,6},{6,7},{7,8},{8,9},{9,10},{10,1... | collective-permute-start | bytes 393224 | tf_op jit(solution)/shard_map/ppermute | solution.py:258
  69.1 5.5 %collective-permute-start.14 = (bf16[16,4096]{1,0:T(8,128)(2,1)S(1)}, bf16[16,4096]{1,0:T(8,128)(2,1)S(1)}, u32[]{:S(2)}, u32[]{:S(2)}) collective-permute-start(bf16[16,4096]{1,0:T(8,128)(2,1)S(1)} %get-tuple-element.54), channel_id=1, source_target_pairs={{0,15},{1,0},{2,1},{3,2},{4,3},{5,4},{6,5},{7,6},{8,7},{9,8},{10,9... | collective-permute-start | bytes 393224 | tf_op jit(solution)/shard_map/ppermute | solution.py:260
  74.6 1.1 collective-permute-done.7
  75.7 1.8 %collective-permute-done.14 = bf16[16,4096]{1,0:T(8,128)(2,1)S(1)} collective-permute-done((bf16[16,4096]{1,0:T(8,128)(2,1)S(1)}, bf16[16,4096]{1,0:T(8,128)(2,1)S(1)}, u32[]{:S(2)}, u32[]{:S(2)}) %collective-permute-start.14) | collective-permute-done | bytes 131104 | tf_op jit(solution)/shard_map/ppermute | solution.py:260
  77.5 0.1 add_convert_fusion.11
  77.5 2.8 %collective-permute-start.8 = (bf16[16,4096]{1,0:T(8,128)(2,1)S(1)}, bf16[16,4096]{1,0:T(8,128)(2,1)S(1)}, u32[]{:S(2)}, u32[]{:S(2)}) collective-permute-start(bf16[16,4096]{1,0:T(8,128)(2,1)S(1)} %get-tuple-element.51), channel_id=1, source_target_pairs={{0,1},{1,2},{2,3},{3,4},{4,5},{5,6},{6,7},{7,8},{8,9},{9,10},{10,1... | collective-permute-start | bytes 393224 | tf_op jit(solution)/shard_map/ppermute | solution.py:258
  80.4 4.1 %collective-permute-start.15 = (bf16[16,4096]{1,0:T(8,128)(2,1)S(1)}, bf16[16,4096]{1,0:T(8,128)(2,1)S(1)}, u32[]{:S(2)}, u32[]{:S(2)}) collective-permute-start(bf16[16,4096]{1,0:T(8,128)(2,1)S(1)} %get-tuple-element.52), channel_id=1, source_target_pairs={{0,15},{1,0},{2,1},{3,2},{4,3},{5,4},{6,5},{7,6},{8,7},{9,8},{10,9... | collective-permute-start | bytes 393224 | tf_op jit(solution)/shard_map/ppermute | solution.py:260
  84.5 1.9 %collective-permute-done.8 = bf16[16,4096]{1,0:T(8,128)(2,1)S(1)} collective-permute-done((bf16[16,4096]{1,0:T(8,128)(2,1)S(1)}, bf16[16,4096]{1,0:T(8,128)(2,1)S(1)}, u32[]{:S(2)}, u32[]{:S(2)}) %collective-permute-start.8) | collective-permute-done | bytes 131104 | tf_op jit(solution)/shard_map/ppermute | solution.py:258
  86.4 3.7 %collective-permute-done.15 = bf16[16,4096]{1,0:T(8,128)(2,1)S(1)} collective-permute-done((bf16[16,4096]{1,0:T(8,128)(2,1)S(1)}, bf16[16,4096]{1,0:T(8,128)(2,1)S(1)}, u32[]{:S(2)}, u32[]{:S(2)}) %collective-permute-start.15) | collective-permute-done | bytes 131104 | tf_op jit(solution)/shard_map/ppermute | solution.py:260
  90.1 0.1 add_convert_fusion.10
  90.2 3.7 %collective-permute-start.9 = (bf16[16,4096]{1,0:T(8,128)(2,1)S(1)}, bf16[16,4096]{1,0:T(8,128)(2,1)S(1)}, u32[]{:S(2)}, u32[]{:S(2)}) collective-permute-start(bf16[16,4096]{1,0:T(8,128)(2,1)S(1)} %get-tuple-element.49), channel_id=1, source_target_pairs={{0,1},{1,2},{2,3},{3,4},{4,5},{5,6},{6,7},{7,8},{8,9},{9,10},{10,1... | collective-permute-start | bytes 393224 | tf_op jit(solution)/shard_map/ppermute | solution.py:258
  93.9 2.1 %collective-permute-start.16 = (bf16[16,4096]{1,0:T(8,128)(2,1)S(1)}, bf16[16,4096]{1,0:T(8,128)(2,1)S(1)}, u32[]{:S(2)}, u32[]{:S(2)}) collective-permute-start(bf16[16,4096]{1,0:T(8,128)(2,1)S(1)} %get-tuple-element.50), channel_id=1, source_target_pairs={{0,15},{1,0},{2,1},{3,2},{4,3},{5,4},{6,5},{7,6},{8,7},{9,8},{10,9... | collective-permute-start | bytes 393224 | tf_op jit(solution)/shard_map/ppermute | solution.py:260
  96.0 1.7 %collective-permute-done.9 = bf16[16,4096]{1,0:T(8,128)(2,1)S(1)} collective-permute-done((bf16[16,4096]{1,0:T(8,128)(2,1)S(1)}, bf16[16,4096]{1,0:T(8,128)(2,1)S(1)}, u32[]{:S(2)}, u32[]{:S(2)}) %collective-permute-start.9) | collective-permute-done | bytes 131104 | tf_op jit(solution)/shard_map/ppermute | solution.py:258
  97.7 3.4 %collective-permute-done.16 = bf16[16,4096]{1,0:T(8,128)(2,1)S(1)} collective-permute-done((bf16[16,4096]{1,0:T(8,128)(2,1)S(1)}, bf16[16,4096]{1,0:T(8,128)(2,1)S(1)}, u32[]{:S(2)}, u32[]{:S(2)}) %collective-permute-start.16) | collective-permute-done | bytes 131104 | tf_op jit(solution)/shard_map/ppermute | solution.py:260
  101.2 0.1 add_convert_fusion.9
  101.2 3.6 %collective-permute-start.10 = (bf16[16,4096]{1,0:T(8,128)(2,1)S(1)}, bf16[16,4096]{1,0:T(8,128)(2,1)S(1)}, u32[]{:S(2)}, u32[]{:S(2)}) collective-permute-start(bf16[16,4096]{1,0:T(8,128)(2,1)S(1)} %get-tuple-element.47), channel_id=1, source_target_pairs={{0,1},{1,2},{2,3},{3,4},{4,5},{5,6},{6,7},{7,8},{8,9},{9,10},{10,1... | collective-permute-start | bytes 393224 | tf_op jit(solution)/shard_map/ppermute | solution.py:258
  104.9 2.2 %collective-permute-start.17 = (bf16[16,4096]{1,0:T(8,128)(2,1)S(1)}, bf16[16,4096]{1,0:T(8,128)(2,1)S(1)}, u32[]{:S(2)}, u32[]{:S(2)}) collective-permute-start(bf16[16,4096]{1,0:T(8,128)(2,1)S(1)} %get-tuple-element.48), channel_id=1, source_target_pairs={{0,15},{1,0},{2,1},{3,2},{4,3},{5,4},{6,5},{7,6},{8,7},{9,8},{10,9... | collective-permute-start | bytes 393224 | tf_op jit(solution)/shard_map/ppermute | solution.py:260
  107.1 1.0 collective-permute-done.10
  108.1 4.5 %collective-permute-done.17 = bf16[16,4096]{1,0:T(8,128)(2,1)S(1)} collective-permute-done((bf16[16,4096]{1,0:T(8,128)(2,1)S(1)}, bf16[16,4096]{1,0:T(8,128)(2,1)S(1)}, u32[]{:S(2)}, u32[]{:S(2)}) %collective-permute-start.17) | collective-permute-done | bytes 131104 | tf_op jit(solution)/shard_map/ppermute | solution.py:260
  112.6 0.1 add_convert_fusion.8
  112.7 3.9 %collective-permute-start.11 = (bf16[16,4096]{1,0:T(8,128)(2,1)S(1)}, bf16[16,4096]{1,0:T(8,128)(2,1)S(1)}, u32[]{:S(2)}, u32[]{:S(2)}) collective-permute-start(bf16[16,4096]{1,0:T(8,128)(2,1)S(1)} %get-tuple-element.45), channel_id=1, source_target_pairs={{0,1},{1,2},{2,3},{3,4},{4,5},{5,6},{6,7},{7,8},{8,9},{9,10},{10,1... | collective-permute-start | bytes 393224 | tf_op jit(solution)/shard_map/ppermute | solution.py:258
  116.6 1.9 %collective-permute-start.18 = (bf16[16,4096]{1,0:T(8,128)(2,1)S(1)}, bf16[16,4096]{1,0:T(8,128)(2,1)S(1)}, u32[]{:S(2)}, u32[]{:S(2)}) collective-permute-start(bf16[16,4096]{1,0:T(8,128)(2,1)S(1)} %get-tuple-element.46), channel_id=1, source_target_pairs={{0,15},{1,0},{2,1},{3,2},{4,3},{5,4},{6,5},{7,6},{8,7},{9,8},{10,9... | collective-permute-start | bytes 393224 | tf_op jit(solution)/shard_map/ppermute | solution.py:260
  118.5 1.0 collective-permute-done.11
  119.5 5.1 %collective-permute-done.18 = bf16[16,4096]{1,0:T(8,128)(2,1)S(1)} collective-permute-done((bf16[16,4096]{1,0:T(8,128)(2,1)S(1)}, bf16[16,4096]{1,0:T(8,128)(2,1)S(1)}, u32[]{:S(2)}, u32[]{:S(2)}) %collective-permute-start.18) | collective-permute-done | bytes 131104 | tf_op jit(solution)/shard_map/ppermute | solution.py:260
  124.7 0.1 add_convert_fusion.7
  124.7 3.9 %collective-permute-start.12 = (bf16[16,4096]{1,0:T(8,128)(2,1)S(1)}, bf16[16,4096]{1,0:T(8,128)(2,1)S(1)}, u32[]{:S(2)}, u32[]{:S(2)}) collective-permute-start(bf16[16,4096]{1,0:T(8,128)(2,1)S(1)} %get-tuple-element.43), channel_id=1, source_target_pairs={{0,1},{1,2},{2,3},{3,4},{4,5},{5,6},{6,7},{7,8},{8,9},{9,10},{10,1... | collective-permute-start | bytes 393224 | tf_op jit(solution)/shard_map/ppermute | solution.py:261
  128.7 1.9 %collective-permute-start.19 = (bf16[16,4096]{1,0:T(8,128)(2,1)S(1)}, bf16[16,4096]{1,0:T(8,128)(2,1)S(1)}, u32[]{:S(2)}, u32[]{:S(2)}) collective-permute-start(bf16[16,4096]{1,0:T(8,128)(2,1)S(1)} %get-tuple-element.44), channel_id=1, source_target_pairs={{0,15},{1,0},{2,1},{3,2},{4,3},{5,4},{6,5},{7,6},{8,7},{9,8},{10,9... | collective-permute-start | bytes 393224 | tf_op jit(solution)/shard_map/ppermute | solution.py:262
  130.6 1.0 collective-permute-done.12
  131.6 3.9 %collective-permute-done.19 = bf16[16,4096]{1,0:T(8,128)(2,1)S(1)} collective-permute-done((bf16[16,4096]{1,0:T(8,128)(2,1)S(1)}, bf16[16,4096]{1,0:T(8,128)(2,1)S(1)}, u32[]{:S(2)}, u32[]{:S(2)}) %collective-permute-start.19) | collective-permute-done | bytes 131104 | tf_op jit(solution)/shard_map/ppermute | solution.py:262
  135.5 0.7 add_convert_fusion
  (14 shorter events, 0.1 us)
Async XLA Ops:
  0.0 39.2 %copy-start.2 = (f32[2,8,256]{2,1,0:T(8,128)S(1)}, f32[2,8,256]{2,1,0:T(8,128)}, u32[]{:S(2)}) copy-start(f32[2,8,256]{2,1,0:T(8,128)} %refs_5_.1) | copy-start | bytes 49156
  0.0 0.9 copy-start.3
  0.9 0.9 copy-start.5
  1.8 0.7 copy-start.7
  2.5 0.7 copy-start.8
  3.2 36.0 %copy-start.4 = (bf16[256,256]{1,0:T(8,128)(2,1)S(1)}, bf16[256,256]{1,0:T(8,128)(2,1)}, u32[]{:S(2)}) copy-start(bf16[256,256]{1,0:T(8,128)(2,1)} %q_ref.1) | copy-start | bytes 393220
  3.2 36.1 %copy-start.6 = (bf16[256,256]{1,0:T(8,128)(2,1)S(1)}, bf16[256,256]{1,0:T(8,128)(2,1)}, u32[]{:S(2)}) copy-start(bf16[256,256]{1,0:T(8,128)(2,1)} %k_ref.3) | copy-start | bytes 393220
  8.8 3.2 %collective-permute-start = (bf16[2,128,256]{2,1,0:T(8,128)(2,1)S(1)}, bf16[2,128,256]{2,1,0:T(8,128)(2,1)S(1)}, u32[]{:S(2)}, u32[]{:S(2)}) collective-permute-start(bf16[2,128,256]{2,1,0:T(8,128)(2,1)S(1)} %get-tuple-element.30.refs_1_), channel_id=1, source_target_pairs={{0,16},{16,0},{32,48},{48,32},{64,80},{80,64},{96,112},{112,96},{1... | collective-permute-start | bytes 393224 | tf_op jit(solution)/shard_map/ppermute | solution.py:303
  12.8 7.4 %collective-permute-start.1 = (bf16[2,128,256]{2,1,0:T(8,128)(2,1)S(1)}, bf16[2,128,256]{2,1,0:T(8,128)(2,1)S(1)}, u32[]{:S(2)}, u32[]{:S(2)}) collective-permute-start(bf16[2,128,256]{2,1,0:T(8,128)(2,1)S(1)} %get-tuple-element.31.refs_1_), channel_id=1, source_target_pairs={{0,32},{16,48},{32,0},{48,16},{64,96},{80,112},{96,64},{112,80},{1... | collective-permute-start | bytes 393224 | tf_op jit(solution)/shard_map/ppermute | solution.py:303
  21.0 8.4 %collective-permute-start.2 = (bf16[2,128,256]{2,1,0:T(8,128)(2,1)S(1)}, bf16[2,128,256]{2,1,0:T(8,128)(2,1)S(1)}, u32[]{:S(2)}, u32[]{:S(2)}) collective-permute-start(bf16[2,128,256]{2,1,0:T(8,128)(2,1)S(1)} %get-tuple-element.33.refs_1_), channel_id=1, source_target_pairs={{0,64},{16,80},{32,96},{48,112},{64,0},{80,16},{96,32},{112,48},{1... | collective-permute-start | bytes 393224 | tf_op jit(solution)/shard_map/ppermute | solution.py:303
  30.1 15.5 %copy-start = (bf16[256,4096]{1,0:T(8,128)(2,1)S(1)}, bf16[256,4096]{1,0:T(8,128)(2,1)}, u32[]{:S(2)}) copy-start(bf16[256,4096]{1,0:T(8,128)(2,1)} %refs_7_.1) | copy-start | bytes 6291460
  30.1 15.5 %copy-start.1 = (bf16[256,256]{1,0:T(8,128)(2,1)S(1)}, bf16[256,256]{1,0:T(8,128)(2,1)}, u32[]{:S(2)}) copy-start(bf16[256,256]{1,0:T(8,128)(2,1)} %refs_6_.1) | copy-start | bytes 393220
  30.1 7.0 %collective-permute-start.3 = (bf16[2,128,256]{2,1,0:T(8,128)(2,1)S(1)}, bf16[2,128,256]{2,1,0:T(8,128)(2,1)S(1)}, u32[]{:S(2)}, u32[]{:S(2)}) collective-permute-start(bf16[2,128,256]{2,1,0:T(8,128)(2,1)S(1)} %get-tuple-element.35.refs_1_), channel_id=1, source_target_pairs={{0,128},{16,144},{32,160},{48,176},{64,192},{80,208},{96,224},{112... | collective-permute-start | bytes 393224 | tf_op jit(solution)/shard_map/ppermute | solution.py:303
  37.9 7.7 %collective-permute-start.4 = (bf16[2,128,128]{2,1,0:T(8,128)(2,1)S(1)}, bf16[2,128,128]{2,1,0:T(8,128)(2,1)S(1)}, u32[]{:S(2)}, u32[]{:S(2)}) collective-permute-start(bf16[2,128,128]{2,1,0:T(8,128)(2,1)S(1)} %slice.51), channel_id=1, source_target_pairs={{0,256},{16,272},{32,288},{48,304},{64,320},{80,336},{96,352},{112... | collective-permute-start | bytes 196616 | tf_op jit(solution)/shard_map/ppermute | solution.py:313
  47.7 7.1 %collective-permute-start.5 = (bf16[16,4096]{1,0:T(8,128)(2,1)S(1)}, bf16[16,4096]{1,0:T(8,128)(2,1)S(1)}, u32[]{:S(2)}, u32[]{:S(2)}) collective-permute-start(bf16[16,4096]{1,0:T(8,128)(2,1)S(1)} %get-tuple-element.55), channel_id=1, source_target_pairs={{0,1},{1,2},{2,3},{3,4},{4,5},{5,6},{6,7},{7,8},{8,9},{9,10},{10,1... | collective-permute-start | bytes 393224 | tf_op jit(solution)/shard_map/ppermute | solution.py:258
  51.5 7.7 %collective-permute-start.13 = (bf16[16,4096]{1,0:T(8,128)(2,1)S(1)}, bf16[16,4096]{1,0:T(8,128)(2,1)S(1)}, u32[]{:S(2)}, u32[]{:S(2)}) collective-permute-start(bf16[16,4096]{1,0:T(8,128)(2,1)S(1)} %get-tuple-element.56), channel_id=1, source_target_pairs={{0,15},{1,0},{2,1},{3,2},{4,3},{5,4},{6,5},{7,6},{8,7},{9,8},{10,9... | collective-permute-start | bytes 393224 | tf_op jit(solution)/shard_map/ppermute | solution.py:260
  54.8 12.3 %collective-permute-start.6 = (bf16[16,4096]{1,0:T(8,128)(2,1)S(1)}, bf16[16,4096]{1,0:T(8,128)(2,1)S(1)}, u32[]{:S(2)}, u32[]{:S(2)}) collective-permute-start(bf16[16,4096]{1,0:T(8,128)(2,1)S(1)} %add_convert_fusion.13), channel_id=1, source_target_pairs={{0,1},{1,2},{2,3},{3,4},{4,5},{5,6},{6,7},{7,8},{8,9},{9,10},{10,1... | collective-permute-start | bytes 393224 | tf_op jit(solution)/shard_map/ppermute | solution.py:258
  67.2 8.5 %collective-permute-start.7 = (bf16[16,4096]{1,0:T(8,128)(2,1)S(1)}, bf16[16,4096]{1,0:T(8,128)(2,1)S(1)}, u32[]{:S(2)}, u32[]{:S(2)}) collective-permute-start(bf16[16,4096]{1,0:T(8,128)(2,1)S(1)} %get-tuple-element.53), channel_id=1, source_target_pairs={{0,1},{1,2},{2,3},{3,4},{4,5},{5,6},{6,7},{7,8},{8,9},{9,10},{10,1... | collective-permute-start | bytes 393224 | tf_op jit(solution)/shard_map/ppermute | solution.py:258
  69.1 8.4 %collective-permute-start.14 = (bf16[16,4096]{1,0:T(8,128)(2,1)S(1)}, bf16[16,4096]{1,0:T(8,128)(2,1)S(1)}, u32[]{:S(2)}, u32[]{:S(2)}) collective-permute-start(bf16[16,4096]{1,0:T(8,128)(2,1)S(1)} %get-tuple-element.54), channel_id=1, source_target_pairs={{0,15},{1,0},{2,1},{3,2},{4,3},{5,4},{6,5},{7,6},{8,7},{9,8},{10,9... | collective-permute-start | bytes 393224 | tf_op jit(solution)/shard_map/ppermute | solution.py:260
  77.5 8.8 %collective-permute-start.8 = (bf16[16,4096]{1,0:T(8,128)(2,1)S(1)}, bf16[16,4096]{1,0:T(8,128)(2,1)S(1)}, u32[]{:S(2)}, u32[]{:S(2)}) collective-permute-start(bf16[16,4096]{1,0:T(8,128)(2,1)S(1)} %get-tuple-element.51), channel_id=1, source_target_pairs={{0,1},{1,2},{2,3},{3,4},{4,5},{5,6},{6,7},{7,8},{8,9},{9,10},{10,1... | collective-permute-start | bytes 393224 | tf_op jit(solution)/shard_map/ppermute | solution.py:258
  80.4 9.7 %collective-permute-start.15 = (bf16[16,4096]{1,0:T(8,128)(2,1)S(1)}, bf16[16,4096]{1,0:T(8,128)(2,1)S(1)}, u32[]{:S(2)}, u32[]{:S(2)}) collective-permute-start(bf16[16,4096]{1,0:T(8,128)(2,1)S(1)} %get-tuple-element.52), channel_id=1, source_target_pairs={{0,15},{1,0},{2,1},{3,2},{4,3},{5,4},{6,5},{7,6},{8,7},{9,8},{10,9... | collective-permute-start | bytes 393224 | tf_op jit(solution)/shard_map/ppermute | solution.py:260
  90.2 7.5 %collective-permute-start.9 = (bf16[16,4096]{1,0:T(8,128)(2,1)S(1)}, bf16[16,4096]{1,0:T(8,128)(2,1)S(1)}, u32[]{:S(2)}, u32[]{:S(2)}) collective-permute-start(bf16[16,4096]{1,0:T(8,128)(2,1)S(1)} %get-tuple-element.49), channel_id=1, source_target_pairs={{0,1},{1,2},{2,3},{3,4},{4,5},{5,6},{6,7},{7,8},{8,9},{9,10},{10,1... | collective-permute-start | bytes 393224 | tf_op jit(solution)/shard_map/ppermute | solution.py:258
  93.9 7.3 %collective-permute-start.16 = (bf16[16,4096]{1,0:T(8,128)(2,1)S(1)}, bf16[16,4096]{1,0:T(8,128)(2,1)S(1)}, u32[]{:S(2)}, u32[]{:S(2)}) collective-permute-start(bf16[16,4096]{1,0:T(8,128)(2,1)S(1)} %get-tuple-element.50), channel_id=1, source_target_pairs={{0,15},{1,0},{2,1},{3,2},{4,3},{5,4},{6,5},{7,6},{8,7},{9,8},{10,9... | collective-permute-start | bytes 393224 | tf_op jit(solution)/shard_map/ppermute | solution.py:260
  101.2 6.9 %collective-permute-start.10 = (bf16[16,4096]{1,0:T(8,128)(2,1)S(1)}, bf16[16,4096]{1,0:T(8,128)(2,1)S(1)}, u32[]{:S(2)}, u32[]{:S(2)}) collective-permute-start(bf16[16,4096]{1,0:T(8,128)(2,1)S(1)} %get-tuple-element.47), channel_id=1, source_target_pairs={{0,1},{1,2},{2,3},{3,4},{4,5},{5,6},{6,7},{7,8},{8,9},{9,10},{10,1... | collective-permute-start | bytes 393224 | tf_op jit(solution)/shard_map/ppermute | solution.py:258
  104.9 7.7 %collective-permute-start.17 = (bf16[16,4096]{1,0:T(8,128)(2,1)S(1)}, bf16[16,4096]{1,0:T(8,128)(2,1)S(1)}, u32[]{:S(2)}, u32[]{:S(2)}) collective-permute-start(bf16[16,4096]{1,0:T(8,128)(2,1)S(1)} %get-tuple-element.48), channel_id=1, source_target_pairs={{0,15},{1,0},{2,1},{3,2},{4,3},{5,4},{6,5},{7,6},{8,7},{9,8},{10,9... | collective-permute-start | bytes 393224 | tf_op jit(solution)/shard_map/ppermute | solution.py:260
  112.7 6.9 %collective-permute-start.11 = (bf16[16,4096]{1,0:T(8,128)(2,1)S(1)}, bf16[16,4096]{1,0:T(8,128)(2,1)S(1)}, u32[]{:S(2)}, u32[]{:S(2)}) collective-permute-start(bf16[16,4096]{1,0:T(8,128)(2,1)S(1)} %get-tuple-element.45), channel_id=1, source_target_pairs={{0,1},{1,2},{2,3},{3,4},{4,5},{5,6},{6,7},{7,8},{8,9},{9,10},{10,1... | collective-permute-start | bytes 393224 | tf_op jit(solution)/shard_map/ppermute | solution.py:258
  116.6 8.1 %collective-permute-start.18 = (bf16[16,4096]{1,0:T(8,128)(2,1)S(1)}, bf16[16,4096]{1,0:T(8,128)(2,1)S(1)}, u32[]{:S(2)}, u32[]{:S(2)}) collective-permute-start(bf16[16,4096]{1,0:T(8,128)(2,1)S(1)} %get-tuple-element.46), channel_id=1, source_target_pairs={{0,15},{1,0},{2,1},{3,2},{4,3},{5,4},{6,5},{7,6},{8,7},{9,8},{10,9... | collective-permute-start | bytes 393224 | tf_op jit(solution)/shard_map/ppermute | solution.py:260
  124.7 6.9 %collective-permute-start.12 = (bf16[16,4096]{1,0:T(8,128)(2,1)S(1)}, bf16[16,4096]{1,0:T(8,128)(2,1)S(1)}, u32[]{:S(2)}, u32[]{:S(2)}) collective-permute-start(bf16[16,4096]{1,0:T(8,128)(2,1)S(1)} %get-tuple-element.43), channel_id=1, source_target_pairs={{0,1},{1,2},{2,3},{3,4},{4,5},{5,6},{6,7},{7,8},{8,9},{9,10},{10,1... | collective-permute-start | bytes 393224 | tf_op jit(solution)/shard_map/ppermute | solution.py:261
  128.7 6.9 %collective-permute-start.19 = (bf16[16,4096]{1,0:T(8,128)(2,1)S(1)}, bf16[16,4096]{1,0:T(8,128)(2,1)S(1)}, u32[]{:S(2)}, u32[]{:S(2)}) collective-permute-start(bf16[16,4096]{1,0:T(8,128)(2,1)S(1)} %get-tuple-element.44), channel_id=1, source_target_pairs={{0,15},{1,0},{2,1},{3,2},{4,3},{5,4},{6,5},{7,6},{8,7},{9,8},{10,9... | collective-permute-start | bytes 393224 | tf_op jit(solution)/shard_map/ppermute | solution.py:262

commit v2 on v1

--- a/solution.py
+++ b/solution.py
@@ -199,14 +199,13 @@
         after_ref[...] = before_ref[...]
 
 
-def final_kernel(outer, ring, pos_ref, core_ref, lift_ref, last_ref, before_ref, lw_ref, gate_ref, out_w_ref, *rest):
-    level_refs, out_ref, norm_ref, turn_ref = rest[:-3], rest[-3], rest[-2], rest[-1]
+def finish_kernel(outer, ring, pos_ref, core_ref, lift_ref, last_ref, before_ref, lw_ref, gate_ref, *rest):
+    level_refs, keep_ref, give_ref, norm_ref = rest[:-3], rest[-3], rest[-2], rest[-1]
     heads = before_ref.shape[0]
     tokens = core_ref.shape[0]
     levels = lw_ref.shape[1]
     weights = lw_ref[...].reshape(heads * levels, tokens).T
     upper = ((pos_ref[0] >> (outer - 1)) & 1 == 1).astype(F32)
-    normed = []
     for h in range(heads):
         lanes = slice(h * DK, (h + 1) * DK)
         lifted = lift_ref[:, lanes].astype(F32)
@@ -219,16 +218,22 @@
         core = core_ref[:, lanes] + dot(jnp.concatenate(scaled, axis=1), jnp.concatenate(stack, axis=0))
         core = core * lax.rsqrt(jnp.mean(core * core, axis=1, keepdims=True) + EPSILON)
         gate = gate_ref[:, lanes].astype(F32)
-        normed.append((core * (gate / (1.0 + jnp.exp(-gate)))).astype(BF16))
-    norm_ref[...] = jnp.concatenate(normed, axis=1)
-    chunk = tokens // ring
+        norm_ref[:, lanes] = (core * (gate / (1.0 + jnp.exp(-gate)))).astype(BF16)
+    chunk = tokens // (2 * ring)
+    pair = pos_ref[1] // 2
+    parity = lax.rem(pos_ref[1], 2)
     for j in range(ring):
-        owner = lax.rem(pos_ref[1] + ring + ring // 2 - j, ring)
-        turn_ref[j * chunk : (j + 1) * chunk] = norm_ref[pl.ds(pl.multiple_of(owner * chunk, chunk), chunk)]
-    normed = turn_ref[...]
-    step = 512
-    for c in range(0, out_ref.shape[1], step):
-        out_ref[:, c : c + step] = dot(normed, out_w_ref[:, c : c + step]).astype(BF16)
+        owner = 2 * lax.rem(pair + ring + ring // 2 - j, ring)
+        rows = slice(j * chunk, (j + 1) * chunk)
+        keep_ref[rows] = norm_ref[pl.ds(pl.multiple_of((owner + parity) * chunk, chunk), chunk)]
+        give_ref[rows] = norm_ref[pl.ds(pl.multiple_of((owner + 1 - parity) * chunk, chunk), chunk)]
+
+
+def project_kernel(keep_ref, got_ref, mine_ref, theirs_ref, *out_refs):
+    sums = dot(keep_ref[...], mine_ref[...]) + dot(got_ref[...], theirs_ref[...])
+    chunk = out_refs[0].shape[0]
+    for j, out_ref in enumerate(out_refs):
+        out_ref[...] = sums[j * chunk : (j + 1) * chunk].astype(BF16)
 
 
 def call(body, out_shape, specs, flops, bytes_accessed, scratch=()):
@@ -243,24 +248,20 @@
     )
 
 
-def ring_sum(partial, ring):
-    chunk = partial.shape[0] // ring
+def ring_sum(terms):
+    ring = len(terms)
     half = ring // 2
-    right = [(i, (i + 1) % ring) for i in range(ring)]
-    left = [(i, (i - 1) % ring) for i in range(ring)]
-
-    def term(j):
-        return lax.slice_in_dim(partial, j * chunk, (j + 1) * chunk).astype(F32)
-
-    ahead = term(0).astype(BF16)
-    behind = term(ring - 1).astype(BF16)
+    count = 2 * ring
+    right = [(i, (i + 2) % count) for i in range(count)]
+    left = [(i, (i - 2) % count) for i in range(count)]
+    ahead, behind = terms[0], terms[ring - 1]
     for t in range(1, half):
-        ahead = (lax.ppermute(ahead, "head", right).astype(F32) + term(t)).astype(BF16)
+        ahead = (lax.ppermute(ahead, "head", right).astype(F32) + terms[t].astype(F32)).astype(BF16)
         if t < half - 1:
-            behind = (lax.ppermute(behind, "head", left).astype(F32) + term(ring - 1 - t)).astype(BF16)
+            behind = (lax.ppermute(behind, "head", left).astype(F32) + terms[ring - 1 - t].astype(F32)).astype(BF16)
     ahead = lax.ppermute(ahead, "head", right).astype(F32)
     behind = lax.ppermute(behind, "head", left).astype(F32)
-    return (ahead + behind + term(half)).astype(BF16)
+    return (ahead + behind + terms[half].astype(F32)).astype(BF16)
 
 
 def on_device(queries, keys, values, gate, log_forget, write_rate, level_weight, w_out):
@@ -271,6 +272,8 @@
     ring = lax.axis_size("head")
     position = jnp.stack([lax.axis_index("seq"), lax.axis_index("head")]).astype(jnp.int32)
     wide = heads * DK
+    pairs = [(i, i ^ 1) for i in range(ring)]
+    w_pair = lax.ppermute(w_out, "head", pairs)
 
     def shape(dims, dtype=BF16):
         return jax.ShapeDtypeStruct(dims, dtype)
@@ -311,15 +314,30 @@
         collected.append(level)
     top = 1 << (outer - 1)
     last = lax.ppermute(total[:, :, :DK], "seq", [(i, i + top) for i in range(top)])
-    partial = call(
-        lambda *refs: final_kernel(outer, ring, *refs),
-        shape((tokens, w_out.shape[1])),
-        [SMEM] + [VMEM] * (7 + outer - 1),
-        600_000_000,
-        5_000_000,
-        [pltpu.VMEM((tokens, wide), BF16)] * 2,
-    )(position, core, lifted, last, before, level_weight, gate, w_out, *collected)
-    return ring_sum(partial, ring)
+    keep, give = call(
+        lambda *refs: finish_kernel(outer, ring // 2, *refs),
+        (shape((tokens // 2, wide)), shape((tokens // 2, wide))),
+        [SMEM] + [VMEM] * (6 + outer - 1),
+        100_000_000,
+        1_000_000,
+        [pltpu.VMEM((tokens, wide), BF16)],
+    )(position, core, lifted, last, before, level_weight, gate, *collected)
+    got = lax.ppermute(give, "head", pairs)
+    columns = w_out.shape[1]
+    step = columns // 4
+    chunk = tokens // ring
+    whole = pl.BlockSpec((tokens // 2, wide), lambda c: (0, 0))
+    block = pl.BlockSpec((wide, step), lambda c: (0, c))
+    terms = pl.pallas_call(
+        project_kernel,
+        grid=(columns // step,),
+        out_shape=[shape((chunk, columns))] * (ring // 2),
+        in_specs=[whole, whole, block, block],
+        out_specs=[pl.BlockSpec((chunk, step), lambda c: (0, c))] * (ring // 2),
+        compiler_params=pltpu.CompilerParams(vmem_limit_bytes=VMEM_BYTES),
+        cost_estimate=pl.CostEstimate(flops=600_000_000, bytes_accessed=6_000_000, transcendentals=0),
+    )(keep, got, w_out, w_pair)
+    return ring_sum(terms)
 
 
 def solution(mesh):

time: 137 us -> 107 us (0.78)
  waiting for transfers between devices: 59.7 us -> 36.6 us
  starting transfers between devices: 59.9 us -> 50.6 us
  local copies, waits for them, and re-layouts: 3.24 us -> 4.83 us
    ppermute x13 -> x7, waiting for transfers between devices: 34.4 us -> 10.2 us  [the longest x3 7.91 us: ring_sum(): lax.ppermute(ahead, 'head', right).astype(F32) + terms[t].astype(F32)]
    ppermute x13 -> x7, starting transfers between devices: 42 us -> 30.6 us  [the longest x2 15.6 us: ring_sum(): lax.ppermute(behind, 'head', left).astype(F32)]
    ppermute x1, waiting for transfers between devices: 1 us -> 7.03 us  [ring_sum(): ahead = lax.ppermute(ahead, 'head', right).astype(F32)]
    ppermute x1, starting transfers between devices: 1.92 us -> 6.03 us  [ring_sum(): behind = lax.ppermute(behind, 'head', left).astype(F32)]
    ppermute x1, waiting for transfers between devices: 3.93 us -> 0.01 us  [ring_sum(): behind = lax.ppermute(behind, 'head', left).astype(F32)]
    ppermute x1, starting transfers between devices: 3.92 us -> 1.92 us  [ring_sum(): ahead = lax.ppermute(ahead, 'head', right).astype(F32)]
    unnamed x18 -> x22, local copies, waits for them, and re-layouts: 3.21 us -> 4.82 us
    pallas_call x1 -> x2, Pallas kernels: 2.08 us -> 3.23 us  [the longest x1 1.72 us: on_device(): pl.pallas_call(project_kernel, grid=(columns // step,), out_shape=[shape(...]
  transfers between devices with their start and end apart: 20 -> 14, of which waited for: 19 -> 10; matrix products, arithmetic and copies ran while one was open for 0% -> 0% of each run, Pallas kernels for 1% -> 11%
where the time goes in v2:
time: 107 us; the launch traced here: 106 us
  starting transfers between devices  50.6 us (47%)
  waiting for transfers between devices  36.6 us (34%)
  Pallas kernels  13 us (12%)
  local copies, waits for them, and re-layouts  4.83 us (5%)
    ppermute x2, starting transfers between devices, ring_sum(): lax.ppermute(behind, 'head', left).astype(F32)  15.6 us
    ppermute x4, waiting for transfers between devices, on_device(): theirs = lax.ppermute(total, 'seq', [(i, i ^ 1 << b) for i in range(seq)])  15.1 us
    ppermute x4, starting transfers between devices, on_device(): theirs = lax.ppermute(total, 'seq', [(i, i ^ 1 << b) for i in range(seq)])  10.8 us
    ppermute x3, starting transfers between devices, ring_sum(): lax.ppermute(ahead, 'head', right).astype(F32) + terms[t].astype(F32)  9.03 us
    ppermute x3, waiting for transfers between devices, ring_sum(): lax.ppermute(ahead, 'head', right).astype(F32) + terms[t].astype(F32)  7.91 us
    ppermute x1, waiting for transfers between devices, ring_sum(): ahead = lax.ppermute(ahead, 'head', right).astype(F32)  7.03 us
    ppermute x1, starting transfers between devices, ring_sum(): behind = lax.ppermute(behind, 'head', left).astype(F32)  6.03 us
    pallas_call x1, Pallas kernels, on_device(): call(states_kernel, (shape((heads, DK, 2 * DK)), shape((heads, 4, DK, 2 *...  5.59 us
  transfers between devices with their start and end apart: 14, of which 10 were waited for; matrix products, arithmetic and copies ran while one was open for 0% of the time, Pallas kernels for 11%

profile of v2, /device:TPU:62, one launch (start us, length us, event | category | flops | bytes accessed | tf_op | source)
XLA Modules:
  0.0 106.3 jit_solution(11627864939239137023)
XLA Ops:
  0.0 0.0 copy-start.2
  0.0 2.1 %collective-permute-start.6 = (bf16[256,4096]{1,0:T(8,128)(2,1)}, bf16[256,4096]{1,0:T(8,128)(2,1)S(1)}, u32[]{:S(2)}, u32[]{:S(2)}) collective-permute-start(bf16[256,4096]{1,0:T(8,128)(2,1)} %mine_ref.1), channel_id=1, source_target_pairs={{0,1},{1,0},{2,3},{3,2},{4,5},{5,4},{6,7},{7,6},{8,9},{9,8},{10,11... | collective-permute-start | bytes 6291464 | tf_op jit(solution)/shard_map/ppermute | solution.py:276
  2.1 0.0 copy-start.3
  2.2 0.9 copy-done.3
  3.1 0.0 copy-start.5
  3.1 0.9 copy-done.5
  4.0 0.0 copy-start.7
  4.0 0.7 copy-done.7
  4.6 0.0 copy-start.8
  4.6 0.7 copy-done.8
  5.3 0.0 copy-start.4
  5.3 0.0 copy-start.6
  5.3 5.6 %shard_map.82 = (bf16[2,128,256]{2,1,0:T(8,128)(2,1)S(1)}, bf16[2,4,128,256]{3,2,1,0:T(8,128)(2,1)S(1)}, f32[256,256]{1,0:T(8,128)S(1)}, f32[256,256]{1,0:T(8,128)S(1)}, f32[8,256]{1,0:T(8,128)S(1)}) custom-call(bf16[256,256]{1,0:T(8,128)(2,1)S(1)} %copy-done.5, bf16[256,256]{1,0:T(8,128)(2,1)S(1)} %copy-done.3, f32[2,256]{1,0:T(2,128)S(1)} %copy-done.7, ...), custom_call_target="tpu_custom_call" | custom-call | flops 2000000000 | bytes 1000000 | tf_op jit(solution)/shard_map/pallas_call | solution.py:281
  10.9 0.0 copy-start.9
  10.9 0.7 copy-done.9
  11.6 1.9 %collective-permute-start = (bf16[2,128,256]{2,1,0:T(8,128)(2,1)S(1)}, bf16[2,128,256]{2,1,0:T(8,128)(2,1)S(1)}, u32[]{:S(2)}, u32[]{:S(2)}) collective-permute-start(bf16[2,128,256]{2,1,0:T(8,128)(2,1)S(1)} %get-tuple-element.40.refs_1_), channel_id=1, source_target_pairs={{0,16},{16,0},{32,48},{48,32},{64,80},{80,64},{96,112},{112,96},{1... | collective-permute-start | bytes 393224 | tf_op jit(solution)/shard_map/ppermute | solution.py:306
  13.5 0.1 pad_add_fusion.refs_0_
  13.6 1.2 %collective-permute-done.refs_2_ = bf16[2,128,256]{2,1,0:T(8,128)(2,1)S(1)} collective-permute-done((bf16[2,128,256]{2,1,0:T(8,128)(2,1)S(1)}, bf16[2,128,256]{2,1,0:T(8,128)(2,1)S(1)}, u32[]{:S(2)}, u32[]{:S(2)}) %collective-permute-start) | collective-permute-done | bytes 131104 | tf_op jit(solution)/shard_map/ppermute | solution.py:306
  14.9 0.7 shard_map.84
  15.6 2.7 %collective-permute-start.1 = (bf16[2,128,256]{2,1,0:T(8,128)(2,1)S(1)}, bf16[2,128,256]{2,1,0:T(8,128)(2,1)S(1)}, u32[]{:S(2)}, u32[]{:S(2)}) collective-permute-start(bf16[2,128,256]{2,1,0:T(8,128)(2,1)S(1)} %get-tuple-element.41.refs_1_), channel_id=1, source_target_pairs={{0,32},{16,48},{32,0},{48,16},{64,96},{80,112},{96,64},{112,80},{1... | collective-permute-start | bytes 393224 | tf_op jit(solution)/shard_map/ppermute | solution.py:306
  18.3 4.7 %collective-permute-done.1.refs_2_ = bf16[2,128,256]{2,1,0:T(8,128)(2,1)S(1)} collective-permute-done((bf16[2,128,256]{2,1,0:T(8,128)(2,1)S(1)}, bf16[2,128,256]{2,1,0:T(8,128)(2,1)S(1)}, u32[]{:S(2)}, u32[]{:S(2)}) %collective-permute-start.1) | collective-permute-done | bytes 131104 | tf_op jit(solution)/shard_map/ppermute | solution.py:306
  23.0 0.8 shard_map.85
  23.8 3.3 %collective-permute-start.2 = (bf16[2,128,256]{2,1,0:T(8,128)(2,1)S(1)}, bf16[2,128,256]{2,1,0:T(8,128)(2,1)S(1)}, u32[]{:S(2)}, u32[]{:S(2)}) collective-permute-start(bf16[2,128,256]{2,1,0:T(8,128)(2,1)S(1)} %get-tuple-element.43.refs_1_), channel_id=1, source_target_pairs={{0,64},{16,80},{32,96},{48,112},{64,0},{80,16},{96,32},{112,48},{1... | collective-permute-start | bytes 393224 | tf_op jit(solution)/shard_map/ppermute | solution.py:306
  27.1 5.0 %collective-permute-done.2.refs_2_ = bf16[2,128,256]{2,1,0:T(8,128)(2,1)S(1)} collective-permute-done((bf16[2,128,256]{2,1,0:T(8,128)(2,1)S(1)}, bf16[2,128,256]{2,1,0:T(8,128)(2,1)S(1)}, u32[]{:S(2)}, u32[]{:S(2)}) %collective-permute-start.2) | collective-permute-done | bytes 131104 | tf_op jit(solution)/shard_map/ppermute | solution.py:306
  32.2 0.8 shard_map.86
  32.9 0.0 copy-start.1
  32.9 2.8 %collective-permute-start.3 = (bf16[2,128,256]{2,1,0:T(8,128)(2,1)S(1)}, bf16[2,128,256]{2,1,0:T(8,128)(2,1)S(1)}, u32[]{:S(2)}, u32[]{:S(2)}) collective-permute-start(bf16[2,128,256]{2,1,0:T(8,128)(2,1)S(1)} %get-tuple-element.45.refs_1_), channel_id=1, source_target_pairs={{0,128},{16,144},{32,160},{48,176},{64,192},{80,208},{96,224},{112... | collective-permute-start | bytes 393224 | tf_op jit(solution)/shard_map/ppermute | solution.py:306
  35.7 4.2 %collective-permute-done.3.refs_2_ = bf16[2,128,256]{2,1,0:T(8,128)(2,1)S(1)} collective-permute-done((bf16[2,128,256]{2,1,0:T(8,128)(2,1)S(1)}, bf16[2,128,256]{2,1,0:T(8,128)(2,1)S(1)}, u32[]{:S(2)}, u32[]{:S(2)}) %collective-permute-start.3) | collective-permute-done | bytes 131104 | tf_op jit(solution)/shard_map/ppermute | solution.py:306
  39.9 0.8 shard_map.87
  40.7 1.3 %collective-permute-start.4 = (bf16[2,128,128]{2,1,0:T(8,128)(2,1)S(1)}, bf16[2,128,128]{2,1,0:T(8,128)(2,1)S(1)}, u32[]{:S(2)}, u32[]{:S(2)}) collective-permute-start(bf16[2,128,128]{2,1,0:T(8,128)(2,1)S(1)} %slice.3), channel_id=1, source_target_pairs={{0,256},{16,272},{32,288},{48,304},{64,320},{80,336},{96,352},{112... | collective-permute-start | bytes 196616 | tf_op jit(solution)/shard_map/ppermute | solution.py:316
  42.0 0.0 copy-done.2
  42.0 0.0 copy-done.4
  42.0 0.0 copy-done.6
  42.0 0.0 copy-start.10
  42.1 0.9 copy-done.10
  43.0 0.0 copy-start
  43.0 1.2 %shard_map.83 = (f32[256,256]{1,0:T(8,128)S(1)}, bf16[256,256]{1,0:T(8,128)(2,1)S(1)}) custom-call(bf16[256,256]{1,0:T(8,128)(2,1)S(1)} %copy-done.4, bf16[256,256]{1,0:T(8,128)(2,1)S(1)} %copy-done.6, f32[256,256]{1,0:T(8,128)S(1)} %get-tuple-element.34.w_ref, f32[256,256]{1,0:T(8,128)S(1)} %copy-done.10, f32[8,256]{1,0:T(8,128)S(1)} %get-tuple-element.36.rows_ref, ...), custom_call_target="tpu_custom_call" | custom-call | flops 1000000000 | bytes 1000000 | tf_op jit(solution)/shard_map/pallas_call | solution.py:295
  44.2 4.2 %collective-permute-done.4.refs_3_ = bf16[2,128,128]{2,1,0:T(8,128)(2,1)S(1)} collective-permute-done((bf16[2,128,128]{2,1,0:T(8,128)(2,1)S(1)}, bf16[2,128,128]{2,1,0:T(8,128)(2,1)S(1)}, u32[]{:S(2)}, u32[]{:S(2)}) %collective-permute-start.4) | collective-permute-done | bytes 65568 | tf_op jit(solution)/shard_map/ppermute | solution.py:316
  48.4 0.0 copy-done.1
  48.4 1.5 %shard_map.88 = (bf16[128,256]{1,0:T(8,128)(2,1)S(1)}, bf16[128,256]{1,0:T(8,128)(2,1)S(1)}) custom-call(s32[2]{0:T(128)S(1)} %pad_add_fusion.refs_0_, f32[256,256]{1,0:T(8,128)S(1)} %get-tuple-element.38.refs_1_, bf16[256,256]{1,0:T(8,128)(2,1)S(1)} %get-tuple-element.39.refs_2_, bf16[2,128,128]{2,1,0:T(8,128)(2,1)S(1)} %collective-permute-done.4.refs_3_, ...), custom_call_target="tpu_custom_call" | custom-call | flops 100000000 | bytes 1000000 | tf_op jit(solution)/shard_map/pallas_call | solution.py:317
  49.9 3.8 %collective-permute-start.5 = (bf16[128,256]{1,0:T(8,128)(2,1)S(1)}, bf16[128,256]{1,0:T(8,128)(2,1)S(1)}, u32[]{:S(2)}, u32[]{:S(2)}) collective-permute-start(bf16[128,256]{1,0:T(8,128)(2,1)S(1)} %get-tuple-element.54), channel_id=1, source_target_pairs={{0,1},{1,0},{2,3},{3,2},{4,5},{5,4},{6,7},{7,6},{8,9},{9,8},{10,11... | collective-permute-start | bytes 196616 | tf_op jit(solution)/shard_map/ppermute | solution.py:325
  53.7 2.3 %collective-permute-done.5.got_ref = bf16[128,256]{1,0:T(8,128)(2,1)S(1)} collective-permute-done((bf16[128,256]{1,0:T(8,128)(2,1)S(1)}, bf16[128,256]{1,0:T(8,128)(2,1)S(1)}, u32[]{:S(2)}, u32[]{:S(2)}) %collective-permute-start.5) | collective-permute-done | bytes 65568 | tf_op jit(solution)/shard_map/ppermute | solution.py:325
  56.1 0.0 collective-permute-done.6.theirs_ref
  56.1 0.0 copy-done
  56.1 1.7 %shard_map.89 = (bf16[16,4096]{1,0:T(8,128)(2,1)S(1)}, bf16[16,4096]{1,0:T(8,128)(2,1)S(1)}, bf16[16,4096]{1,0:T(8,128)(2,1)S(1)}, bf16[16,4096]{1,0:T(8,128)(2,...) custom-call(bf16[128,256]{1,0:T(8,128)(2,1)S(1)} %get-tuple-element., ...), custom_call_target="tpu_custom_call" | custom-call | flops 600000000 | bytes 6000000 | tf_op jit(solution)/shard_map/pallas_call | solution.py:331
  57.8 5.2 %collective-permute-start.7 = (bf16[16,4096]{1,0:T(8,128)(2,1)S(1)}, bf16[16,4096]{1,0:T(8,128)(2,1)S(1)}, u32[]{:S(2)}, u32[]{:S(2)}) collective-permute-start(bf16[16,4096]{1,0:T(8,128)(2,1)S(1)} %get-tuple-element.55), channel_id=1, source_target_pairs={{0,2},{1,3},{2,4},{3,5},{4,6},{5,7},{6,8},{7,9},{8,10},{9,11},{10,... | collective-permute-start | bytes 393224 | tf_op jit(solution)/shard_map/ppermute | solution.py:259
  63.0 8.6 %collective-permute-start.11 = (bf16[16,4096]{1,0:T(8,128)(2,1)S(1)}, bf16[16,4096]{1,0:T(8,128)(2,1)S(1)}, u32[]{:S(2)}, u32[]{:S(2)}) collective-permute-start(bf16[16,4096]{1,0:T(8,128)(2,1)S(1)} %get-tuple-element.59), channel_id=1, source_target_pairs={{0,14},{1,15},{2,0},{3,1},{4,2},{5,3},{6,4},{7,5},{8,6},{9,7},{10,... | collective-permute-start | bytes 393224 | tf_op jit(solution)/shard_map/ppermute | solution.py:261
  71.6 2.4 %collective-permute-done.7 = bf16[16,4096]{1,0:T(8,128)(2,1)S(1)} collective-permute-done((bf16[16,4096]{1,0:T(8,128)(2,1)S(1)}, bf16[16,4096]{1,0:T(8,128)(2,1)S(1)}, u32[]{:S(2)}, u32[]{:S(2)}) %collective-permute-start.7) | collective-permute-done | bytes 131104 | tf_op jit(solution)/shard_map/ppermute | solution.py:259
  74.0 1.9 %collective-permute-start.8 = (bf16[16,4096]{1,0:T(8,128)(2,1)S(1)}, bf16[16,4096]{1,0:T(8,128)(2,1)S(1)}, u32[]{:S(2)}, u32[]{:S(2)}) collective-permute-start(bf16[16,4096]{1,0:T(8,128)(2,1)S(1)} %add_convert_fusion.5), channel_id=1, source_target_pairs={{0,2},{1,3},{2,4},{3,5},{4,6},{5,7},{6,8},{7,9},{8,10},{9,11},{10,... | collective-permute-start | bytes 393224 | tf_op jit(solution)/shard_map/ppermute | solution.py:259
  76.0 0.0 collective-permute-done.11
  76.0 7.0 %collective-permute-start.12 = (bf16[16,4096]{1,0:T(8,128)(2,1)S(1)}, bf16[16,4096]{1,0:T(8,128)(2,1)S(1)}, u32[]{:S(2)}, u32[]{:S(2)}) collective-permute-start(bf16[16,4096]{1,0:T(8,128)(2,1)S(1)} %add_convert_fusion.2), channel_id=1, source_target_pairs={{0,14},{1,15},{2,0},{3,1},{4,2},{5,3},{6,4},{7,5},{8,6},{9,7},{10,... | collective-permute-start | bytes 393224 | tf_op jit(solution)/shard_map/ppermute | solution.py:261
  83.0 3.6 %collective-permute-done.8 = bf16[16,4096]{1,0:T(8,128)(2,1)S(1)} collective-permute-done((bf16[16,4096]{1,0:T(8,128)(2,1)S(1)}, bf16[16,4096]{1,0:T(8,128)(2,1)S(1)}, u32[]{:S(2)}, u32[]{:S(2)}) %collective-permute-start.8) | collective-permute-done | bytes 131104 | tf_op jit(solution)/shard_map/ppermute | solution.py:259
  86.7 1.9 %collective-permute-start.9 = (bf16[16,4096]{1,0:T(8,128)(2,1)S(1)}, bf16[16,4096]{1,0:T(8,128)(2,1)S(1)}, u32[]{:S(2)}, u32[]{:S(2)}) collective-permute-start(bf16[16,4096]{1,0:T(8,128)(2,1)S(1)} %add_convert_fusion.4), channel_id=1, source_target_pairs={{0,2},{1,3},{2,4},{3,5},{4,6},{5,7},{6,8},{7,9},{8,10},{9,11},{10,... | collective-permute-start | bytes 393224 | tf_op jit(solution)/shard_map/ppermute | solution.py:259
  88.6 0.0 collective-permute-done.12
  88.7 6.0 %collective-permute-start.13 = (bf16[16,4096]{1,0:T(8,128)(2,1)S(1)}, bf16[16,4096]{1,0:T(8,128)(2,1)S(1)}, u32[]{:S(2)}, u32[]{:S(2)}) collective-permute-start(bf16[16,4096]{1,0:T(8,128)(2,1)S(1)} %add_convert_fusion.1), channel_id=1, source_target_pairs={{0,14},{1,15},{2,0},{3,1},{4,2},{5,3},{6,4},{7,5},{8,6},{9,7},{10,... | collective-permute-start | bytes 393224 | tf_op jit(solution)/shard_map/ppermute | solution.py:263
  94.7 1.9 %collective-permute-done.9 = bf16[16,4096]{1,0:T(8,128)(2,1)S(1)} collective-permute-done((bf16[16,4096]{1,0:T(8,128)(2,1)S(1)}, bf16[16,4096]{1,0:T(8,128)(2,1)S(1)}, u32[]{:S(2)}, u32[]{:S(2)}) %collective-permute-start.9) | collective-permute-done | bytes 131104 | tf_op jit(solution)/shard_map/ppermute | solution.py:259
  96.6 1.9 %collective-permute-start.10 = (bf16[16,4096]{1,0:T(8,128)(2,1)S(1)}, bf16[16,4096]{1,0:T(8,128)(2,1)S(1)}, u32[]{:S(2)}, u32[]{:S(2)}) collective-permute-start(bf16[16,4096]{1,0:T(8,128)(2,1)S(1)} %add_convert_fusion.3), channel_id=1, source_target_pairs={{0,2},{1,3},{2,4},{3,5},{4,6},{5,7},{6,8},{7,9},{8,10},{9,11},{10,... | collective-permute-start | bytes 393224 | tf_op jit(solution)/shard_map/ppermute | solution.py:262
  98.6 0.0 collective-permute-done.13
  98.6 7.0 %collective-permute-done.10 = bf16[16,4096]{1,0:T(8,128)(2,1)S(1)} collective-permute-done((bf16[16,4096]{1,0:T(8,128)(2,1)S(1)}, bf16[16,4096]{1,0:T(8,128)(2,1)S(1)}, u32[]{:S(2)}, u32[]{:S(2)}) %collective-permute-start.10) | collective-permute-done | bytes 131104 | tf_op jit(solution)/shard_map/ppermute | solution.py:262
  105.6 0.7 add_convert_fusion
  (8 shorter events, 0.2 us)
Async XLA Ops:
  0.0 42.0 %copy-start.2 = (f32[2,8,256]{2,1,0:T(8,128)S(1)}, f32[2,8,256]{2,1,0:T(8,128)}, u32[]{:S(2)}) copy-start(f32[2,8,256]{2,1,0:T(8,128)} %refs_5_.1) | copy-start | bytes 49156
  0.0 56.1 %collective-permute-start.6 = (bf16[256,4096]{1,0:T(8,128)(2,1)}, bf16[256,4096]{1,0:T(8,128)(2,1)S(1)}, u32[]{:S(2)}, u32[]{:S(2)}) collective-permute-start(bf16[256,4096]{1,0:T(8,128)(2,1)} %mine_ref.1), channel_id=1, source_target_pairs={{0,1},{1,0},{2,3},{3,2},{4,5},{5,4},{6,7},{7,6},{8,9},{9,8},{10,11... | collective-permute-start | bytes 6291464 | tf_op jit(solution)/shard_map/ppermute | solution.py:276
  2.1 0.9 copy-start.3
  3.1 0.9 copy-start.5
  4.0 0.7 copy-start.7
  4.6 0.7 copy-start.8
  5.3 36.7 %copy-start.4 = (bf16[256,256]{1,0:T(8,128)(2,1)S(1)}, bf16[256,256]{1,0:T(8,128)(2,1)}, u32[]{:S(2)}) copy-start(bf16[256,256]{1,0:T(8,128)(2,1)} %q_ref.1) | copy-start | bytes 393220
  5.3 36.7 %copy-start.6 = (bf16[256,256]{1,0:T(8,128)(2,1)S(1)}, bf16[256,256]{1,0:T(8,128)(2,1)}, u32[]{:S(2)}) copy-start(bf16[256,256]{1,0:T(8,128)(2,1)} %k_ref.3) | copy-start | bytes 393220
  10.9 0.7 copy-start.9
  11.6 3.2 %collective-permute-start = (bf16[2,128,256]{2,1,0:T(8,128)(2,1)S(1)}, bf16[2,128,256]{2,1,0:T(8,128)(2,1)S(1)}, u32[]{:S(2)}, u32[]{:S(2)}) collective-permute-start(bf16[2,128,256]{2,1,0:T(8,128)(2,1)S(1)} %get-tuple-element.40.refs_1_), channel_id=1, source_target_pairs={{0,16},{16,0},{32,48},{48,32},{64,80},{80,64},{96,112},{112,96},{1... | collective-permute-start | bytes 393224 | tf_op jit(solution)/shard_map/ppermute | solution.py:306
  15.6 7.4 %collective-permute-start.1 = (bf16[2,128,256]{2,1,0:T(8,128)(2,1)S(1)}, bf16[2,128,256]{2,1,0:T(8,128)(2,1)S(1)}, u32[]{:S(2)}, u32[]{:S(2)}) collective-permute-start(bf16[2,128,256]{2,1,0:T(8,128)(2,1)S(1)} %get-tuple-element.41.refs_1_), channel_id=1, source_target_pairs={{0,32},{16,48},{32,0},{48,16},{64,96},{80,112},{96,64},{112,80},{1... | collective-permute-start | bytes 393224 | tf_op jit(solution)/shard_map/ppermute | solution.py:306
  23.8 8.4 %collective-permute-start.2 = (bf16[2,128,256]{2,1,0:T(8,128)(2,1)S(1)}, bf16[2,128,256]{2,1,0:T(8,128)(2,1)S(1)}, u32[]{:S(2)}, u32[]{:S(2)}) collective-permute-start(bf16[2,128,256]{2,1,0:T(8,128)(2,1)S(1)} %get-tuple-element.43.refs_1_), channel_id=1, source_target_pairs={{0,64},{16,80},{32,96},{48,112},{64,0},{80,16},{96,32},{112,48},{1... | collective-permute-start | bytes 393224 | tf_op jit(solution)/shard_map/ppermute | solution.py:306
  32.9 15.5 %copy-start.1 = (bf16[256,256]{1,0:T(8,128)(2,1)S(1)}, bf16[256,256]{1,0:T(8,128)(2,1)}, u32[]{:S(2)}) copy-start(bf16[256,256]{1,0:T(8,128)(2,1)} %refs_6_.1) | copy-start | bytes 393220
  32.9 7.0 %collective-permute-start.3 = (bf16[2,128,256]{2,1,0:T(8,128)(2,1)S(1)}, bf16[2,128,256]{2,1,0:T(8,128)(2,1)S(1)}, u32[]{:S(2)}, u32[]{:S(2)}) collective-permute-start(bf16[2,128,256]{2,1,0:T(8,128)(2,1)S(1)} %get-tuple-element.45.refs_1_), channel_id=1, source_target_pairs={{0,128},{16,144},{32,160},{48,176},{64,192},{80,208},{96,224},{112... | collective-permute-start | bytes 393224 | tf_op jit(solution)/shard_map/ppermute | solution.py:306
  40.7 7.7 %collective-permute-start.4 = (bf16[2,128,128]{2,1,0:T(8,128)(2,1)S(1)}, bf16[2,128,128]{2,1,0:T(8,128)(2,1)S(1)}, u32[]{:S(2)}, u32[]{:S(2)}) collective-permute-start(bf16[2,128,128]{2,1,0:T(8,128)(2,1)S(1)} %slice.3), channel_id=1, source_target_pairs={{0,256},{16,272},{32,288},{48,304},{64,320},{80,336},{96,352},{112... | collective-permute-start | bytes 196616 | tf_op jit(solution)/shard_map/ppermute | solution.py:316
  42.0 1.0 copy-start.10
  43.0 13.1 %copy-start = (bf16[256,4096]{1,0:T(8,128)(2,1)S(1)}, bf16[256,4096]{1,0:T(8,128)(2,1)}, u32[]{:S(2)}) copy-start(bf16[256,4096]{1,0:T(8,128)(2,1)} %mine_ref.1) | copy-start | bytes 6291460
  49.9 6.2 %collective-permute-start.5 = (bf16[128,256]{1,0:T(8,128)(2,1)S(1)}, bf16[128,256]{1,0:T(8,128)(2,1)S(1)}, u32[]{:S(2)}, u32[]{:S(2)}) collective-permute-start(bf16[128,256]{1,0:T(8,128)(2,1)S(1)} %get-tuple-element.54), channel_id=1, source_target_pairs={{0,1},{1,0},{2,3},{3,2},{4,5},{5,4},{6,7},{7,6},{8,9},{9,8},{10,11... | collective-permute-start | bytes 196616 | tf_op jit(solution)/shard_map/ppermute | solution.py:325
  57.8 16.2 %collective-permute-start.7 = (bf16[16,4096]{1,0:T(8,128)(2,1)S(1)}, bf16[16,4096]{1,0:T(8,128)(2,1)S(1)}, u32[]{:S(2)}, u32[]{:S(2)}) collective-permute-start(bf16[16,4096]{1,0:T(8,128)(2,1)S(1)} %get-tuple-element.55), channel_id=1, source_target_pairs={{0,2},{1,3},{2,4},{3,5},{4,6},{5,7},{6,8},{7,9},{8,10},{9,11},{10,... | collective-permute-start | bytes 393224 | tf_op jit(solution)/shard_map/ppermute | solution.py:259
  63.0 13.0 %collective-permute-start.11 = (bf16[16,4096]{1,0:T(8,128)(2,1)S(1)}, bf16[16,4096]{1,0:T(8,128)(2,1)S(1)}, u32[]{:S(2)}, u32[]{:S(2)}) collective-permute-start(bf16[16,4096]{1,0:T(8,128)(2,1)S(1)} %get-tuple-element.59), channel_id=1, source_target_pairs={{0,14},{1,15},{2,0},{3,1},{4,2},{5,3},{6,4},{7,5},{8,6},{9,7},{10,... | collective-permute-start | bytes 393224 | tf_op jit(solution)/shard_map/ppermute | solution.py:261
  74.0 12.6 %collective-permute-start.8 = (bf16[16,4096]{1,0:T(8,128)(2,1)S(1)}, bf16[16,4096]{1,0:T(8,128)(2,1)S(1)}, u32[]{:S(2)}, u32[]{:S(2)}) collective-permute-start(bf16[16,4096]{1,0:T(8,128)(2,1)S(1)} %add_convert_fusion.5), channel_id=1, source_target_pairs={{0,2},{1,3},{2,4},{3,5},{4,6},{5,7},{6,8},{7,9},{8,10},{9,11},{10,... | collective-permute-start | bytes 393224 | tf_op jit(solution)/shard_map/ppermute | solution.py:259
  76.0 12.6 %collective-permute-start.12 = (bf16[16,4096]{1,0:T(8,128)(2,1)S(1)}, bf16[16,4096]{1,0:T(8,128)(2,1)S(1)}, u32[]{:S(2)}, u32[]{:S(2)}) collective-permute-start(bf16[16,4096]{1,0:T(8,128)(2,1)S(1)} %add_convert_fusion.2), channel_id=1, source_target_pairs={{0,14},{1,15},{2,0},{3,1},{4,2},{5,3},{6,4},{7,5},{8,6},{9,7},{10,... | collective-permute-start | bytes 393224 | tf_op jit(solution)/shard_map/ppermute | solution.py:261
  86.7 9.9 %collective-permute-start.9 = (bf16[16,4096]{1,0:T(8,128)(2,1)S(1)}, bf16[16,4096]{1,0:T(8,128)(2,1)S(1)}, u32[]{:S(2)}, u32[]{:S(2)}) collective-permute-start(bf16[16,4096]{1,0:T(8,128)(2,1)S(1)} %add_convert_fusion.4), channel_id=1, source_target_pairs={{0,2},{1,3},{2,4},{3,5},{4,6},{5,7},{6,8},{7,9},{8,10},{9,11},{10,... | collective-permute-start | bytes 393224 | tf_op jit(solution)/shard_map/ppermute | solution.py:259
  88.7 9.9 %collective-permute-start.13 = (bf16[16,4096]{1,0:T(8,128)(2,1)S(1)}, bf16[16,4096]{1,0:T(8,128)(2,1)S(1)}, u32[]{:S(2)}, u32[]{:S(2)}) collective-permute-start(bf16[16,4096]{1,0:T(8,128)(2,1)S(1)} %add_convert_fusion.1), channel_id=1, source_target_pairs={{0,14},{1,15},{2,0},{3,1},{4,2},{5,3},{6,4},{7,5},{8,6},{9,7},{10,... | collective-permute-start | bytes 393224 | tf_op jit(solution)/shard_map/ppermute | solution.py:263
  96.6 9.0 %collective-permute-start.10 = (bf16[16,4096]{1,0:T(8,128)(2,1)S(1)}, bf16[16,4096]{1,0:T(8,128)(2,1)S(1)}, u32[]{:S(2)}, u32[]{:S(2)}) collective-permute-start(bf16[16,4096]{1,0:T(8,128)(2,1)S(1)} %add_convert_fusion.3), channel_id=1, source_target_pairs={{0,2},{1,3},{2,4},{3,5},{4,6},{5,7},{6,8},{7,9},{8,10},{9,11},{10,... | collective-permute-start | bytes 393224 | tf_op jit(solution)/shard_map/ppermute | solution.py:262

commit v3 on v2

--- a/solution.py
+++ b/solution.py
@@ -170,60 +170,67 @@
         lift_ref[spans[3], lanes] = read3[:, DK:].astype(BF16)
 
 
-def merge_kernel(bit, pos_ref, mine_ref, theirs_ref, before_ref, total_ref, level_ref, after_ref):
-    upper = (pos_ref[0] >> bit) & 1 == 1
-    heads = mine_ref.shape[0]
-
-    def joined(lead, trail):
-        moved = dot(trail[:, DK:], lead)
-        return jnp.concatenate([moved[:, :DK] + trail[:, :DK].astype(F32), moved[:, DK:]], axis=1).astype(BF16)
-
-    @pl.when(upper)
-    def _():
-        for h in range(heads):
-            total_ref[h] = joined(theirs_ref[h], mine_ref[h])
-        for h in range(heads):
-            if bit == 0:
-                level_ref[h] = theirs_ref[h, :, :DK]
-                after_ref[h] = theirs_ref[h, :, DK:]
-            else:
-                read = dot(before_ref[h], theirs_ref[h]).astype(BF16)
-                level_ref[h] = read[:, :DK]
-                after_ref[h] = read[:, DK:]
-
-    @pl.when(jnp.logical_not(upper))
-    def _():
-        for h in range(heads):
-            total_ref[h] = joined(mine_ref[h], theirs_ref[h])
-        level_ref[...] = jnp.zeros(level_ref.shape, level_ref.dtype)
-        after_ref[...] = before_ref[...]
-
-
-def finish_kernel(outer, ring, pos_ref, core_ref, lift_ref, last_ref, before_ref, lw_ref, gate_ref, *rest):
+def merge_kernel(pos_ref, mine_ref, theirs_ref, total_ref, level_ref, after_ref):
+    upper = lax.rem(pos_ref[0], 2) == 1
+    same = lax.broadcasted_iota(jnp.int32, (DK, DK), 0) == lax.broadcasted_iota(jnp.int32, (DK, DK), 1)
+    for h in range(mine_ref.shape[0]):
+        mine, theirs = mine_ref[h], theirs_ref[h]
+        total_ref[h] = joined(jnp.where(upper, theirs, mine), jnp.where(upper, mine, theirs))
+        level_ref[h] = jnp.where(upper, theirs[:, :DK], jnp.zeros((DK, DK), BF16))
+        after_ref[h] = jnp.where(upper, theirs[:, DK:], same.astype(BF16))
+
+
+def joined(lead, trail):
+    moved = dot(trail[:, DK:], lead)
+    return jnp.concatenate([moved[:, :DK] + trail[:, :DK].astype(F32), moved[:, DK:]], axis=1).astype(BF16)
+
+
+def two_levels(digit, four_ref, before_ref, h):
+    before = before_ref[h]
+    near = dot(before, four_ref[jnp.maximum(digit - 1, 0), h]).astype(BF16)
+    odd = lax.rem(digit, 2) == 1
+    low = jnp.where(odd, near[:, :DK], jnp.zeros((DK, DK), BF16))
+    before = jnp.where(odd, near[:, DK:], before)
+    first = joined(four_ref[0, h], four_ref[1, h])
+    far = dot(before, first).astype(BF16)
+    upper = digit >= 2
+    high = jnp.where(upper, far[:, :DK], jnp.zeros((DK, DK), BF16))
+    return low, high, jnp.where(upper, far[:, DK:], before), first
+
+
+def quad_kernel(bit, pos_ref, four_ref, before_ref, total_ref, low_ref, high_ref, after_ref):
+    digit = (pos_ref[0] >> bit) & 3
+    for h in range(before_ref.shape[0]):
+        low_ref[h], high_ref[h], after_ref[h], first = two_levels(digit, four_ref, before_ref, h)
+        total_ref[h] = joined(first, joined(four_ref[2, h], four_ref[3, h]))
+
+
+def finish_kernel(outer, ring, pos_ref, core_ref, lift_ref, four_ref, before_ref, lw_ref, gate_ref, *rest):
     level_refs, keep_ref, give_ref, norm_ref = rest[:-3], rest[-3], rest[-2], rest[-1]
+    digit = (pos_ref[0] >> (outer - 2)) & 3
     heads = before_ref.shape[0]
     tokens = core_ref.shape[0]
     levels = lw_ref.shape[1]
     weights = lw_ref[...].reshape(heads * levels, tokens).T
-    upper = ((pos_ref[0] >> (outer - 1)) & 1 == 1).astype(F32)
     for h in range(heads):
         lanes = slice(h * DK, (h + 1) * DK)
         lifted = lift_ref[:, lanes].astype(F32)
-        last = (dot(before_ref[h], last_ref[h]) * upper).astype(BF16)
-        scaled, stack = [], []
+        low, high, _, _ = two_levels(digit, four_ref, before_ref, h)
+        stack = [level_ref[h] for level_ref in level_refs] + [low, high]
+        scaled = []
         for b in range(outer):
             at = h * levels + levels - outer + b
             scaled.append((lifted * weights[:, at : at + 1]).astype(BF16))
-            stack.append(level_refs[b][h] if b < outer - 1 else last)
         core = core_ref[:, lanes] + dot(jnp.concatenate(scaled, axis=1), jnp.concatenate(stack, axis=0))
         core = core * lax.rsqrt(jnp.mean(core * core, axis=1, keepdims=True) + EPSILON)
         gate = gate_ref[:, lanes].astype(F32)
         norm_ref[:, lanes] = (core * (gate / (1.0 + jnp.exp(-gate)))).astype(BF16)
+    side = 1 - 2 * lax.rem(pos_ref[0], 2)
     chunk = tokens // (2 * ring)
     pair = pos_ref[1] // 2
     parity = lax.rem(pos_ref[1], 2)
     for j in range(ring):
-        owner = 2 * lax.rem(pair + ring + ring // 2 - j, ring)
+        owner = 2 * lax.rem(pair + ring + side * (ring // 2 - j), ring)
         rows = slice(j * chunk, (j + 1) * chunk)
         keep_ref[rows] = norm_ref[pl.ds(pl.multiple_of((owner + parity) * chunk, chunk), chunk)]
         give_ref[rows] = norm_ref[pl.ds(pl.multiple_of((owner + 1 - parity) * chunk, chunk), chunk)]
@@ -252,16 +259,22 @@
     ring = len(terms)
     half = ring // 2
     count = 2 * ring
-    right = [(i, (i + 2) % count) for i in range(count)]
-    left = [(i, (i - 2) % count) for i in range(count)]
+    slabs = lax.axis_size("seq")
+
+    def hop(block, way):
+        route = []
+        for s in range(slabs):
+            step = 2 * way * (1 - 2 * (s % 2))
+            route += [(s * count + z, s * count + (z + step) % count) for z in range(count)]
+        return lax.ppermute(block, ("seq", "head"), route).astype(F32)
+
     ahead, behind = terms[0], terms[ring - 1]
     for t in range(1, half):
-        ahead = (lax.ppermute(ahead, "head", right).astype(F32) + terms[t].astype(F32)).astype(BF16)
+        ahead = (hop(ahead, 1) + terms[t].astype(F32)).astype(BF16)
         if t < half - 1:
-            behind = (lax.ppermute(behind, "head", left).astype(F32) + terms[ring - 1 - t].astype(F32)).astype(BF16)
-    ahead = lax.ppermute(ahead, "head", right).astype(F32)
-    behind = lax.ppermute(behind, "head", left).astype(F32)
-    return (ahead + behind + terms[half].astype(F32)).astype(BF16)
+            behind = (hop(behind, -1) + terms[ring - 1 - t].astype(F32)).astype(BF16)
+    ahead = hop(ahead, 1) + terms[half].astype(F32)
+    return (ahead + hop(behind, -1) if half > 1 else ahead).astype(BF16)
 
 
 def on_device(queries, keys, values, gate, log_forget, write_rate, level_weight, w_out):
@@ -300,28 +313,40 @@
         1_000_000,
     )(queries, keys, bases, writes, rows, inner, level_weight)
 
-    before = jnp.zeros((heads, DK, DK), BF16) + jnp.eye(DK, dtype=BF16)
-    collected = []
-    for b in range(outer - 1):
-        theirs = lax.ppermute(total, "seq", [(i, i ^ (1 << b)) for i in range(seq)])
-        total, level, before = call(
-            lambda *refs, b=b: merge_kernel(b, *refs),
-            (shape((heads, DK, 2 * DK)), shape((heads, DK, DK)), shape((heads, DK, DK))),
-            [SMEM] + [VMEM] * 3,
-            40_000_000,
-            500_000,
-        )(position, total, theirs, before)
-        collected.append(level)
-    top = 1 << (outer - 1)
-    last = lax.ppermute(total[:, :, :DK], "seq", [(i, i + top) for i in range(top)])
+    theirs = lax.ppermute(total, "seq", [(i, i ^ 1) for i in range(seq)])
+    matrix = shape((heads, DK, DK))
+    total, level, before = call(
+        merge_kernel,
+        (shape((heads, DK, 2 * DK)), matrix, matrix),
+        [SMEM] + [VMEM] * 2,
+        40_000_000,
+        500_000,
+    )(position, total, theirs)
+    collected = [level]
+
+    def gathered(b):
+        stride = 1 << b
+        groups = [[i + k * stride for k in range(4)] for i in range(seq) if (i >> b) & 3 == 0]
+        return lax.all_gather(total, "seq", axis=0, axis_index_groups=groups)
+
+    for b in range(1, outer - 2, 2):
+        total, low, high, before = call(
+            lambda *refs, b=b: quad_kernel(b, *refs),
+            (shape((heads, DK, 2 * DK)), matrix, matrix, matrix),
+            [SMEM] + [VMEM] * 2,
+            100_000_000,
+            1_000_000,
+        )(position, gathered(b), before)
+        collected += [low, high]
+    four = gathered(outer - 2)
     keep, give = call(
         lambda *refs: finish_kernel(outer, ring // 2, *refs),
         (shape((tokens // 2, wide)), shape((tokens // 2, wide))),
-        [SMEM] + [VMEM] * (6 + outer - 1),
+        [SMEM] + [VMEM] * (6 + outer - 2),
         100_000_000,
         1_000_000,
         [pltpu.VMEM((tokens, wide), BF16)],
-    )(position, core, lifted, last, before, level_weight, gate, *collected)
+    )(position, core, lifted, four, before, level_weight, gate, *collected)
     got = lax.ppermute(give, "head", pairs)
     columns = w_out.shape[1]
     step = columns // 4

time: 107 us -> 104 us (0.972)
  the two profiles are of different devices: /device:TPU:62 before, /device:TPU:34 now
where the time goes in v3:
time: 104 us
  starting transfers between devices  38.6 us (37%)
  blocking collectives  28.8 us (28%)
  waiting for transfers between devices  18.7 us (18%)
  Pallas kernels  13.4 us (13%)
  local copies, waits for them, and re-layouts  3.18 us (3%)
    ppermute x7, starting transfers between devices, hop(): return lax.ppermute(block, ('seq', 'head'), route).astype(F32)  32 us
    all_gather x2, blocking collectives, gathered(): return lax.all_gather(total, 'seq', axis=0, axis_index_groups=groups)  28.8 us
    ppermute x7, waiting for transfers between devices, hop(): return lax.ppermute(block, ('seq', 'head'), route).astype(F32)  15 us
    pallas_call x1, Pallas kernels, on_device(): call(states_kernel, (shape((heads, DK, 2 * DK)), shape((heads, 4, DK, 2 *...  5.6 us
    ppermute x1, waiting for transfers between devices, on_device(): got = lax.ppermute(give, 'head', pairs)  3.68 us
    pallas_call x1, Pallas kernels, on_device(): pl.pallas_call(project_kernel, grid=(columns // step,), out_shape=[shape(...  3.32 us
    unnamed x16, local copies, waits for them, and re-layouts  3.18 us
    ppermute x1, starting transfers between devices, on_device(): got = lax.ppermute(give, 'head', pairs)  2.47 us
  transfers between devices with their start and end apart: 10, of which 7 were waited for; matrix products, arithmetic and copies ran while one was open for 0% of the time, Pallas kernels for 10%

profile of v3, /device:TPU:34, one launch (start us, length us, event | category | flops | bytes accessed | tf_op | source)
XLA Modules:
  0.0 103.8 jit_solution(3810975582717812289)
XLA Ops:
  0.0 0.0 copy-start.2
  0.0 2.1 %collective-permute-start.2 = (bf16[256,4096]{1,0:T(8,128)(2,1)}, bf16[256,4096]{1,0:T(8,128)(2,1)}, u32[]{:S(2)}, u32[]{:S(2)}) collective-permute-start(bf16[256,4096]{1,0:T(8,128)(2,1)} %mine_ref.1), channel_id=1, source_target_pairs={{0,1},{1,0},{2,3},{3,2},{4,5},{5,4},{6,7},{7,6},{8,9},{9,8},{10,11... | collective-permute-start | bytes 6291464 | tf_op jit(solution)/shard_map/ppermute | solution.py:289
  2.1 0.0 copy-start.3
  2.2 0.9 copy-done.3
  3.1 0.0 copy-start.5
  3.1 0.9 copy-done.5
  4.0 0.0 copy-start.6
  4.0 0.7 copy-done.6
  4.6 0.0 copy-start.7
  4.6 0.7 copy-done.7
  5.3 0.0 copy-start.4
  5.3 5.6 %shard_map.82 = (bf16[2,128,256]{2,1,0:T(8,128)(2,1)S(1)}, bf16[2,4,128,256]{3,2,1,0:T(8,128)(2,1)S(1)}, f32[256,256]{1,0:T(8,128)S(1)}, f32[256,256]{1,0:T(8,128)S(1)}, f32[8,256]{1,0:T(8,128)S(1)}) custom-call(bf16[256,256]{1,0:T(8,128)(2,1)S(1)} %copy-done.5, bf16[256,256]{1,0:T(8,128)(2,1)S(1)} %copy-done.3, f32[2,256]{1,0:T(2,128)S(1)} %copy-done.6, ...), custom_call_target="tpu_custom_call" | custom-call | flops 2000000000 | bytes 1000000 | tf_op jit(solution)/shard_map/pallas_call | solution.py:294
  10.9 1.9 %collective-permute-start = (bf16[2,128,256]{2,1,0:T(8,128)(2,1)S(1)}, bf16[2,128,256]{2,1,0:T(8,128)(2,1)S(1)}, u32[]{:S(2)}, u32[]{:S(2)}) collective-permute-start(bf16[2,128,256]{2,1,0:T(8,128)(2,1)S(1)} %get-tuple-element.35.mine_ref), channel_id=1, source_target_pairs={{0,16},{16,0},{32,48},{48,32},{64,80},{80,64},{96,112},{112,96},{1... | collective-permute-start | bytes 393224 | tf_op jit(solution)/shard_map/ppermute | solution.py:316
  12.9 0.0 copy-done.2
  12.9 0.0 copy-done.4
  12.9 0.0 copy-start.1
  12.9 1.2 %shard_map.83 = (f32[256,256]{1,0:T(8,128)S(1)}, bf16[256,256]{1,0:T(8,128)(2,1)S(1)}) custom-call(bf16[256,256]{1,0:T(8,128)(2,1)S(1)} %copy-done.4, bf16[256,256]{1,0:T(8,128)(2,1)S(1)} %copy-done.5, f32[256,256]{1,0:T(8,128)S(1)} %get-tuple-element.29.w_ref, f32[256,256]{1,0:T(8,128)S(1)} %get-tuple-element.30.u_ref, ...), custom_call_target="tpu_custom_call" | custom-call | flops 1000000000 | bytes 1000000 | tf_op jit(solution)/shard_map/pallas_call | solution.py:308
  14.1 0.0 copy-start
  14.1 0.1 pad_add_fusion.pos_ref.refs_0_
  14.2 0.0 collective-permute-done.theirs_ref
  14.2 0.7 shard_map.84
  14.9 16.0 %all-gather = bf16[8,128,256]{2,1,0:T(8,128)(2,1)S(1)} all-gather(bf16[2,128,256]{2,1,0:T(8,128)(2,1)S(1)} %get-tuple-element.36), channel_id=2, replica_groups={{0,32,64,96},{16,48,80,112},{128,160,192,224},{144,176,208,240},{256,28..., dimensions={0}, use_global_device_ids=true | all-gather | bytes 655360 | tf_op jit(solution)/shard_map/all_gather | solution.py:330
  30.9 1.1 %shard_map.85 = (bf16[2,128,256]{2,1,0:T(8,128)(2,1)S(1)}, bf16[2,128,128]{2,1,0:T(8,128)(2,1)S(1)}, bf16[2,128,128]{2,1,0:T(8,128)(2,1)S(1)}, bf16[2,128,128]{2,1,0:T(8,128)(2,1)S(1)}) custom-call(s32[2]{0:T(128)S(1)} %pad_add_fusion.pos_ref.refs_0_, bf16[4,2,128,256]{3,2,1,0:T(8,128)(2,1)S(1)} %bitcast.5, bf16[2,128,128]{2,1,0:T(8,128)(2,1)S(1)} %get-tuple-element.37.refs_2_), custom_call_target="tpu_custom_call" | custom-call | flops 100000000 | bytes 1000000 | tf_op jit(solution)/shard_map/pallas_call | solution.py:333
  32.0 12.8 %all-gather.1 = bf16[8,128,256]{2,1,0:T(8,128)(2,1)S(1)} all-gather(bf16[2,128,256]{2,1,0:T(8,128)(2,1)S(1)} %get-tuple-element.38), channel_id=3, replica_groups={{0,128,256,384},{16,144,272,400},{32,160,288,416},{48,176,304,432},{64,..., dimensions={0}, use_global_device_ids=true | all-gather | bytes 655360 | tf_op jit(solution)/shard_map/all_gather | solution.py:330
  44.8 0.0 copy-done.1
  44.8 1.5 %shard_map.86 = (bf16[128,256]{1,0:T(8,128)(2,1)S(1)}, bf16[128,256]{1,0:T(8,128)(2,1)S(1)}) custom-call(s32[2]{0:T(128)S(1)} %pad_add_fusion.pos_ref.refs_0_, f32[256,256]{1,0:T(8,128)S(1)} %get-tuple-element.33.refs_1_, bf16[256,256]{1,0:T(8,128)(2,1)S(1)} %get-tuple-element.34.refs_2_, bf16[4,2,128,256]{3,2,1,0:T(8,128)(2,1)S(1)} %bitcast.4, ...), custom_call_target="tpu_custom_call" | custom-call | flops 100000000 | bytes 1000000 | tf_op jit(solution)/shard_map/pallas_call | solution.py:342
  46.3 2.5 %collective-permute-start.1 = (bf16[128,256]{1,0:T(8,128)(2,1)S(1)}, bf16[128,256]{1,0:T(8,128)(2,1)S(1)}, u32[]{:S(2)}, u32[]{:S(2)}) collective-permute-start(bf16[128,256]{1,0:T(8,128)(2,1)S(1)} %get-tuple-element.44), channel_id=1, source_target_pairs={{0,1},{1,0},{2,3},{3,2},{4,5},{5,4},{6,7},{7,6},{8,9},{9,8},{10,11... | collective-permute-start | bytes 196616 | tf_op jit(solution)/shard_map/ppermute | solution.py:350
  48.8 3.7 %collective-permute-done.1.got_ref = bf16[128,256]{1,0:T(8,128)(2,1)S(1)} collective-permute-done((bf16[128,256]{1,0:T(8,128)(2,1)S(1)}, bf16[128,256]{1,0:T(8,128)(2,1)S(1)}, u32[]{:S(2)}, u32[]{:S(2)}) %collective-permute-start.1) | collective-permute-done | bytes 65568 | tf_op jit(solution)/shard_map/ppermute | solution.py:350
  52.5 0.0 collective-permute-done.2.theirs_ref
  52.5 0.0 copy-done
  52.5 3.3 %shard_map.87 = (bf16[16,4096]{1,0:T(8,128)(2,1)S(1)}, bf16[16,4096]{1,0:T(8,128)(2,1)S(1)}, bf16[16,4096]{1,0:T(8,128)(2,1)S(1)}, bf16[16,4096]{1,0:T(8,128)(2,...) custom-call(bf16[128,256]{1,0:T(8,128)(2,1)S(1)} %get-tuple-element., ...), custom_call_target="tpu_custom_call" | custom-call | flops 600000000 | bytes 6000000 | tf_op jit(solution)/shard_map/pallas_call | solution.py:356
  55.8 3.8 %collective-permute-start.3 = (bf16[16,4096]{1,0:T(8,128)(2,1)S(1)}, bf16[16,4096]{1,0:T(8,128)(2,1)S(1)}, u32[]{:S(2)}, u32[]{:S(2)}) collective-permute-start(bf16[16,4096]{1,0:T(8,128)(2,1)S(1)} %get-tuple-element.45), channel_id=1, source_target_pairs={{0,2},{1,3},{2,4},{3,5},{4,6},{5,7},{6,8},{7,9},{8,10},{9,11},{10,... | collective-permute-start | bytes 393224 | tf_op jit(solution)/shard_map/ppermute | solution.py:269
  59.6 8.6 %collective-permute-start.7 = (bf16[16,4096]{1,0:T(8,128)(2,1)S(1)}, bf16[16,4096]{1,0:T(8,128)(2,1)S(1)}, u32[]{:S(2)}, u32[]{:S(2)}) collective-permute-start(bf16[16,4096]{1,0:T(8,128)(2,1)S(1)} %get-tuple-element.50), channel_id=1, source_target_pairs={{0,14},{1,15},{2,0},{3,1},{4,2},{5,3},{6,4},{7,5},{8,6},{9,7},{10,... | collective-permute-start | bytes 393224 | tf_op jit(solution)/shard_map/ppermute | solution.py:269
  68.2 2.5 %collective-permute-done.3 = bf16[16,4096]{1,0:T(8,128)(2,1)S(1)} collective-permute-done((bf16[16,4096]{1,0:T(8,128)(2,1)S(1)}, bf16[16,4096]{1,0:T(8,128)(2,1)S(1)}, u32[]{:S(2)}, u32[]{:S(2)}) %collective-permute-start.3) | collective-permute-done | bytes 131104 | tf_op jit(solution)/shard_map/ppermute | solution.py:269
  70.7 1.9 %collective-permute-start.4 = (bf16[16,4096]{1,0:T(8,128)(2,1)S(1)}, bf16[16,4096]{1,0:T(8,128)(2,1)S(1)}, u32[]{:S(2)}, u32[]{:S(2)}) collective-permute-start(bf16[16,4096]{1,0:T(8,128)(2,1)S(1)} %add_convert_fusion.5), channel_id=1, source_target_pairs={{0,2},{1,3},{2,4},{3,5},{4,6},{5,7},{6,8},{7,9},{8,10},{9,11},{10,... | collective-permute-start | bytes 393224 | tf_op jit(solution)/shard_map/ppermute | solution.py:269
  72.6 0.0 collective-permute-done.7
  72.7 7.4 %collective-permute-start.8 = (bf16[16,4096]{1,0:T(8,128)(2,1)S(1)}, bf16[16,4096]{1,0:T(8,128)(2,1)S(1)}, u32[]{:S(2)}, u32[]{:S(2)}) collective-permute-start(bf16[16,4096]{1,0:T(8,128)(2,1)S(1)} %add_convert_fusion.2), channel_id=1, source_target_pairs={{0,14},{1,15},{2,0},{3,1},{4,2},{5,3},{6,4},{7,5},{8,6},{9,7},{10,... | collective-permute-start | bytes 393224 | tf_op jit(solution)/shard_map/ppermute | solution.py:269
  80.1 3.7 %collective-permute-done.4 = bf16[16,4096]{1,0:T(8,128)(2,1)S(1)} collective-permute-done((bf16[16,4096]{1,0:T(8,128)(2,1)S(1)}, bf16[16,4096]{1,0:T(8,128)(2,1)S(1)}, u32[]{:S(2)}, u32[]{:S(2)}) %collective-permute-start.4) | collective-permute-done | bytes 131104 | tf_op jit(solution)/shard_map/ppermute | solution.py:269
  83.8 1.9 %collective-permute-start.5 = (bf16[16,4096]{1,0:T(8,128)(2,1)S(1)}, bf16[16,4096]{1,0:T(8,128)(2,1)S(1)}, u32[]{:S(2)}, u32[]{:S(2)}) collective-permute-start(bf16[16,4096]{1,0:T(8,128)(2,1)S(1)} %add_convert_fusion.4), channel_id=1, source_target_pairs={{0,2},{1,3},{2,4},{3,5},{4,6},{5,7},{6,8},{7,9},{8,10},{9,11},{10,... | collective-permute-start | bytes 393224 | tf_op jit(solution)/shard_map/ppermute | solution.py:269
  85.7 0.8 collective-permute-done.8
  86.5 6.5 %collective-permute-start.9 = (bf16[16,4096]{1,0:T(8,128)(2,1)S(1)}, bf16[16,4096]{1,0:T(8,128)(2,1)S(1)}, u32[]{:S(2)}, u32[]{:S(2)}) collective-permute-start(bf16[16,4096]{1,0:T(8,128)(2,1)S(1)} %add_convert_fusion.1), channel_id=1, source_target_pairs={{0,14},{1,15},{2,0},{3,1},{4,2},{5,3},{6,4},{7,5},{8,6},{9,7},{10,... | collective-permute-start | bytes 393224 | tf_op jit(solution)/shard_map/ppermute | solution.py:269
  93.0 0.8 collective-permute-done.5
  93.9 1.9 %collective-permute-start.6 = (bf16[16,4096]{1,0:T(8,128)(2,1)S(1)}, bf16[16,4096]{1,0:T(8,128)(2,1)S(1)}, u32[]{:S(2)}, u32[]{:S(2)}) collective-permute-start(bf16[16,4096]{1,0:T(8,128)(2,1)S(1)} %add_convert_fusion.3), channel_id=1, source_target_pairs={{0,2},{1,3},{2,4},{3,5},{4,6},{5,7},{6,8},{7,9},{8,10},{9,11},{10,... | collective-permute-start | bytes 393224 | tf_op jit(solution)/shard_map/ppermute | solution.py:269
  95.8 2.8 %collective-permute-done.9 = bf16[16,4096]{1,0:T(8,128)(2,1)S(1)} collective-permute-done((bf16[16,4096]{1,0:T(8,128)(2,1)S(1)}, bf16[16,4096]{1,0:T(8,128)(2,1)S(1)}, u32[]{:S(2)}, u32[]{:S(2)}) %collective-permute-start.9) | collective-permute-done | bytes 131104 | tf_op jit(solution)/shard_map/ppermute | solution.py:269
  98.6 4.4 %collective-permute-done.6 = bf16[16,4096]{1,0:T(8,128)(2,1)S(1)} collective-permute-done((bf16[16,4096]{1,0:T(8,128)(2,1)S(1)}, bf16[16,4096]{1,0:T(8,128)(2,1)S(1)}, u32[]{:S(2)}, u32[]{:S(2)}) %collective-permute-start.6) | collective-permute-done | bytes 131104 | tf_op jit(solution)/shard_map/ppermute | solution.py:269
  103.1 0.7 add_convert_fusion
  (5 shorter events, 0.2 us)
Async XLA Ops:
  0.0 12.9 %copy-start.2 = (f32[2,8,256]{2,1,0:T(8,128)S(1)}, f32[2,8,256]{2,1,0:T(8,128)}, u32[]{:S(2)}) copy-start(f32[2,8,256]{2,1,0:T(8,128)} %refs_5_.1) | copy-start | bytes 49156
  0.0 52.5 %collective-permute-start.2 = (bf16[256,4096]{1,0:T(8,128)(2,1)}, bf16[256,4096]{1,0:T(8,128)(2,1)}, u32[]{:S(2)}, u32[]{:S(2)}) collective-permute-start(bf16[256,4096]{1,0:T(8,128)(2,1)} %mine_ref.1), channel_id=1, source_target_pairs={{0,1},{1,0},{2,3},{3,2},{4,5},{5,4},{6,7},{7,6},{8,9},{9,8},{10,11... | collective-permute-start | bytes 6291464 | tf_op jit(solution)/shard_map/ppermute | solution.py:289
  2.1 0.9 copy-start.3
  3.1 0.9 copy-start.5
  4.0 0.7 copy-start.6
  4.6 0.7 copy-start.7
  5.3 7.5 %copy-start.4 = (bf16[256,256]{1,0:T(8,128)(2,1)S(1)}, bf16[256,256]{1,0:T(8,128)(2,1)}, u32[]{:S(2)}) copy-start(bf16[256,256]{1,0:T(8,128)(2,1)} %q_ref.1) | copy-start | bytes 393220
  10.9 3.2 %collective-permute-start = (bf16[2,128,256]{2,1,0:T(8,128)(2,1)S(1)}, bf16[2,128,256]{2,1,0:T(8,128)(2,1)S(1)}, u32[]{:S(2)}, u32[]{:S(2)}) collective-permute-start(bf16[2,128,256]{2,1,0:T(8,128)(2,1)S(1)} %get-tuple-element.35.mine_ref), channel_id=1, source_target_pairs={{0,16},{16,0},{32,48},{48,32},{64,80},{80,64},{96,112},{112,96},{1... | collective-permute-start | bytes 393224 | tf_op jit(solution)/shard_map/ppermute | solution.py:316
  12.9 31.9 %copy-start.1 = (bf16[256,256]{1,0:T(8,128)(2,1)S(1)}, bf16[256,256]{1,0:T(8,128)(2,1)}, u32[]{:S(2)}) copy-start(bf16[256,256]{1,0:T(8,128)(2,1)} %refs_6_.1) | copy-start | bytes 393220
  14.1 38.4 %copy-start = (bf16[256,4096]{1,0:T(8,128)(2,1)S(1)}, bf16[256,4096]{1,0:T(8,128)(2,1)}, u32[]{:S(2)}) copy-start(bf16[256,4096]{1,0:T(8,128)(2,1)} %mine_ref.1) | copy-start | bytes 6291460
  46.3 6.2 %collective-permute-start.1 = (bf16[128,256]{1,0:T(8,128)(2,1)S(1)}, bf16[128,256]{1,0:T(8,128)(2,1)S(1)}, u32[]{:S(2)}, u32[]{:S(2)}) collective-permute-start(bf16[128,256]{1,0:T(8,128)(2,1)S(1)} %get-tuple-element.44), channel_id=1, source_target_pairs={{0,1},{1,0},{2,3},{3,2},{4,5},{5,4},{6,7},{7,6},{8,9},{9,8},{10,11... | collective-permute-start | bytes 196616 | tf_op jit(solution)/shard_map/ppermute | solution.py:350
  55.8 14.9 %collective-permute-start.3 = (bf16[16,4096]{1,0:T(8,128)(2,1)S(1)}, bf16[16,4096]{1,0:T(8,128)(2,1)S(1)}, u32[]{:S(2)}, u32[]{:S(2)}) collective-permute-start(bf16[16,4096]{1,0:T(8,128)(2,1)S(1)} %get-tuple-element.45), channel_id=1, source_target_pairs={{0,2},{1,3},{2,4},{3,5},{4,6},{5,7},{6,8},{7,9},{8,10},{9,11},{10,... | collective-permute-start | bytes 393224 | tf_op jit(solution)/shard_map/ppermute | solution.py:269
  59.6 13.0 %collective-permute-start.7 = (bf16[16,4096]{1,0:T(8,128)(2,1)S(1)}, bf16[16,4096]{1,0:T(8,128)(2,1)S(1)}, u32[]{:S(2)}, u32[]{:S(2)}) collective-permute-start(bf16[16,4096]{1,0:T(8,128)(2,1)S(1)} %get-tuple-element.50), channel_id=1, source_target_pairs={{0,14},{1,15},{2,0},{3,1},{4,2},{5,3},{6,4},{7,5},{8,6},{9,7},{10,... | collective-permute-start | bytes 393224 | tf_op jit(solution)/shard_map/ppermute | solution.py:269
  70.7 13.0 %collective-permute-start.4 = (bf16[16,4096]{1,0:T(8,128)(2,1)S(1)}, bf16[16,4096]{1,0:T(8,128)(2,1)S(1)}, u32[]{:S(2)}, u32[]{:S(2)}) collective-permute-start(bf16[16,4096]{1,0:T(8,128)(2,1)S(1)} %add_convert_fusion.5), channel_id=1, source_target_pairs={{0,2},{1,3},{2,4},{3,5},{4,6},{5,7},{6,8},{7,9},{8,10},{9,11},{10,... | collective-permute-start | bytes 393224 | tf_op jit(solution)/shard_map/ppermute | solution.py:269
  72.7 13.8 %collective-permute-start.8 = (bf16[16,4096]{1,0:T(8,128)(2,1)S(1)}, bf16[16,4096]{1,0:T(8,128)(2,1)S(1)}, u32[]{:S(2)}, u32[]{:S(2)}) collective-permute-start(bf16[16,4096]{1,0:T(8,128)(2,1)S(1)} %add_convert_fusion.2), channel_id=1, source_target_pairs={{0,14},{1,15},{2,0},{3,1},{4,2},{5,3},{6,4},{7,5},{8,6},{9,7},{10,... | collective-permute-start | bytes 393224 | tf_op jit(solution)/shard_map/ppermute | solution.py:269
  83.8 10.1 %collective-permute-start.5 = (bf16[16,4096]{1,0:T(8,128)(2,1)S(1)}, bf16[16,4096]{1,0:T(8,128)(2,1)S(1)}, u32[]{:S(2)}, u32[]{:S(2)}) collective-permute-start(bf16[16,4096]{1,0:T(8,128)(2,1)S(1)} %add_convert_fusion.4), channel_id=1, source_target_pairs={{0,2},{1,3},{2,4},{3,5},{4,6},{5,7},{6,8},{7,9},{8,10},{9,11},{10,... | collective-permute-start | bytes 393224 | tf_op jit(solution)/shard_map/ppermute | solution.py:269
  86.5 12.1 %collective-permute-start.9 = (bf16[16,4096]{1,0:T(8,128)(2,1)S(1)}, bf16[16,4096]{1,0:T(8,128)(2,1)S(1)}, u32[]{:S(2)}, u32[]{:S(2)}) collective-permute-start(bf16[16,4096]{1,0:T(8,128)(2,1)S(1)} %add_convert_fusion.1), channel_id=1, source_target_pairs={{0,14},{1,15},{2,0},{3,1},{4,2},{5,3},{6,4},{7,5},{8,6},{9,7},{10,... | collective-permute-start | bytes 393224 | tf_op jit(solution)/shard_map/ppermute | solution.py:269
  93.9 9.2 %collective-permute-start.6 = (bf16[16,4096]{1,0:T(8,128)(2,1)S(1)}, bf16[16,4096]{1,0:T(8,128)(2,1)S(1)}, u32[]{:S(2)}, u32[]{:S(2)}) collective-permute-start(bf16[16,4096]{1,0:T(8,128)(2,1)S(1)} %add_convert_fusion.3), channel_id=1, source_target_pairs={{0,2},{1,3},{2,4},{3,5},{4,6},{5,7},{6,8},{7,9},{8,10},{9,11},{10,... | collective-permute-start | bytes 393224 | tf_op jit(solution)/shard_map/ppermute | solution.py:269

commit v4 on v3

--- a/solution.py
+++ b/solution.py
@@ -11,8 +11,7 @@
 F32 = jnp.float32
 BF16 = jnp.bfloat16
 VMEM = pl.BlockSpec(memory_space=pltpu.VMEM)
-SMEM = pl.BlockSpec(memory_space=pltpu.SMEM)
-VMEM_BYTES = 48 * 1024 * 1024
+HBM = pl.BlockSpec(memory_space=pltpu.HBM)
 
 
 def dot(left, right, dims=((1,), (0,)), precision=None):
@@ -41,7 +40,22 @@
     return row, col, same
 
 
-def states_kernel(k_ref, v_ref, lf_ref, wr_ref, x_ref, y_ref, w_ref, u_ref, rows_ref):
+def states_kernel(
+    k_in, v_in, lf_in, wr_in, full_ref, x_ref, y_ref, w_ref, u_ref, rows_ref, half_ref,
+    k_ref, v_ref, lf_ref, wr_ref, in_sems, half_sem,
+):
+    copies = [
+        pltpu.make_async_copy(source, target, in_sems.at[i])
+        for i, (source, target) in enumerate(((k_in, k_ref), (lf_in, lf_ref), (wr_in, wr_ref), (v_in, v_ref)))
+    ]
+    for copy in copies:
+        copy.start()
+    count = half_ref.shape[0]
+    first = pl.multiple_of(lax.rem(lax.axis_index("seq"), 2) * count, count)
+    half = pltpu.make_async_copy(full_ref.at[pl.ds(first, count)], half_ref, half_sem)
+    half.start()
+    for copy in copies:
+        copy.wait()
     tokens = k_ref.shape[0]
     heads = lf_ref.shape[0]
     blocks = tokens // BLOCK
@@ -121,6 +135,7 @@
         y_ref[h, 2] = dot(short[2][:, DK:], first.astype(BF16)).astype(BF16)
         y_ref[h, 3] = short[2]
         x_ref[h] = merge(first, second).astype(BF16)
+    half.wait()
     rows_ref[...] = jnp.concatenate([cum] + inv_key_rows + [jnp.zeros((8 - 2 * heads, tokens), F32)], axis=0)
 
 
@@ -170,8 +185,8 @@
         lift_ref[spans[3], lanes] = read3[:, DK:].astype(BF16)
 
 
-def merge_kernel(pos_ref, mine_ref, theirs_ref, total_ref, level_ref, after_ref):
-    upper = lax.rem(pos_ref[0], 2) == 1
+def merge_kernel(mine_ref, theirs_ref, total_ref, level_ref, after_ref):
+    upper = lax.rem(lax.axis_index("seq"), 2) == 1
     same = lax.broadcasted_iota(jnp.int32, (DK, DK), 0) == lax.broadcasted_iota(jnp.int32, (DK, DK), 1)
     for h in range(mine_ref.shape[0]):
         mine, theirs = mine_ref[h], theirs_ref[h]
@@ -198,16 +213,16 @@
     return low, high, jnp.where(upper, far[:, DK:], before), first
 
 
-def quad_kernel(bit, pos_ref, four_ref, before_ref, total_ref, low_ref, high_ref, after_ref):
-    digit = (pos_ref[0] >> bit) & 3
+def quad_kernel(bit, four_ref, before_ref, total_ref, low_ref, high_ref, after_ref):
+    digit = (lax.axis_index("seq") >> bit) & 3
     for h in range(before_ref.shape[0]):
         low_ref[h], high_ref[h], after_ref[h], first = two_levels(digit, four_ref, before_ref, h)
         total_ref[h] = joined(first, joined(four_ref[2, h], four_ref[3, h]))
 
 
-def finish_kernel(outer, ring, pos_ref, core_ref, lift_ref, four_ref, before_ref, lw_ref, gate_ref, *rest):
+def finish_kernel(outer, ring, core_ref, lift_ref, four_ref, before_ref, lw_ref, gate_ref, *rest):
     level_refs, keep_ref, give_ref, norm_ref = rest[:-3], rest[-3], rest[-2], rest[-1]
-    digit = (pos_ref[0] >> (outer - 2)) & 3
+    digit = (lax.axis_index("seq") >> (outer - 2)) & 3
     heads = before_ref.shape[0]
     tokens = core_ref.shape[0]
     levels = lw_ref.shape[1]
@@ -225,32 +240,43 @@
         core = core * lax.rsqrt(jnp.mean(core * core, axis=1, keepdims=True) + EPSILON)
         gate = gate_ref[:, lanes].astype(F32)
         norm_ref[:, lanes] = (core * (gate / (1.0 + jnp.exp(-gate)))).astype(BF16)
-    side = 1 - 2 * lax.rem(pos_ref[0], 2)
     chunk = tokens // (2 * ring)
-    pair = pos_ref[1] // 2
-    parity = lax.rem(pos_ref[1], 2)
+    pair = lax.axis_index("head") // 2
+    parity = lax.rem(lax.axis_index("head"), 2)
+    side = 1 - 2 * parity
     for j in range(ring):
-        owner = 2 * lax.rem(pair + ring + side * (ring // 2 - j), ring)
+        kept = 2 * lax.rem(pair + ring + side * (ring // 2 - j), ring) + parity
+        given = 2 * lax.rem(pair + ring - side * (ring // 2 - j), ring) + 1 - parity
         rows = slice(j * chunk, (j + 1) * chunk)
-        keep_ref[rows] = norm_ref[pl.ds(pl.multiple_of((owner + parity) * chunk, chunk), chunk)]
-        give_ref[rows] = norm_ref[pl.ds(pl.multiple_of((owner + 1 - parity) * chunk, chunk), chunk)]
-
-
-def project_kernel(keep_ref, got_ref, mine_ref, theirs_ref, *out_refs):
-    sums = dot(keep_ref[...], mine_ref[...]) + dot(got_ref[...], theirs_ref[...])
+        keep_ref[rows] = norm_ref[pl.ds(pl.multiple_of(kept * chunk, chunk), chunk)]
+        give_ref[rows] = norm_ref[pl.ds(pl.multiple_of(given * chunk, chunk), chunk)]
+
+
+def project_own_kernel(keep_ref, mine_ref, sums_ref):
+    sums_ref[...] = dot(keep_ref[...], mine_ref[...])
+
+
+def project_kernel(got_ref, sums_ref, direct_ref, across_ref, *out_refs):
+    second = lax.rem(lax.axis_index("seq"), 2) == 1
+    one, two = got_ref[:, :DK], got_ref[:, DK:]
+    sums = (
+        sums_ref[...]
+        + dot(jnp.where(second, two, one), direct_ref[...])
+        + dot(jnp.where(second, one, two), across_ref[...])
+    )
     chunk = out_refs[0].shape[0]
     for j, out_ref in enumerate(out_refs):
         out_ref[...] = sums[j * chunk : (j + 1) * chunk].astype(BF16)
 
 
-def call(body, out_shape, specs, flops, bytes_accessed, scratch=()):
+def call(body, out_shape, specs, flops, bytes_accessed, scratch=(), out_specs=None, mib=16):
     return pl.pallas_call(
         body,
         out_shape=out_shape,
         in_specs=specs,
-        out_specs=jax.tree.map(lambda _: VMEM, out_shape),
+        out_specs=jax.tree.map(lambda _: VMEM, out_shape) if out_specs is None else out_specs,
         scratch_shapes=scratch,
-        compiler_params=pltpu.CompilerParams(vmem_limit_bytes=VMEM_BYTES),
+        compiler_params=pltpu.CompilerParams(vmem_limit_bytes=mib << 20),
         cost_estimate=pl.CostEstimate(flops=flops, bytes_accessed=bytes_accessed, transcendentals=0),
     )
 
@@ -259,14 +285,10 @@
     ring = len(terms)
     half = ring // 2
     count = 2 * ring
-    slabs = lax.axis_size("seq")
 
     def hop(block, way):
-        route = []
-        for s in range(slabs):
-            step = 2 * way * (1 - 2 * (s % 2))
-            route += [(s * count + z, s * count + (z + step) % count) for z in range(count)]
-        return lax.ppermute(block, ("seq", "head"), route).astype(F32)
+        route = [(z, (z + 2 * way * (1 - 2 * (z % 2))) % count) for z in range(count)]
+        return lax.ppermute(block, "head", route).astype(F32)
 
     ahead, behind = terms[0], terms[ring - 1]
     for t in range(1, half):
@@ -283,15 +305,14 @@
     seq = lax.axis_size("seq")
     outer = seq.bit_length() - 1
     ring = lax.axis_size("head")
-    position = jnp.stack([lax.axis_index("seq"), lax.axis_index("head")]).astype(jnp.int32)
     wide = heads * DK
     pairs = [(i, i ^ 1) for i in range(ring)]
-    w_pair = lax.ppermute(w_out, "head", pairs)
 
     def shape(dims, dtype=BF16):
         return jax.ShapeDtypeStruct(dims, dtype)
 
-    total, inner, bases, writes, rows = call(
+    sources = [pltpu.with_memory_space_constraint(x, pltpu.HBM) for x in (keys, values, log_forget, write_rate, w_out)]
+    total, inner, bases, writes, rows, w_half = call(
         states_kernel,
         (
             shape((heads, DK, 2 * DK)),
@@ -299,11 +320,21 @@
             shape((tokens, wide), F32),
             shape((tokens, wide), F32),
             shape((8, tokens), F32),
+            shape((DK, w_out.shape[1])),
         ),
-        [VMEM] * 4,
+        [HBM] * 5,
         2_000_000_000,
         1_000_000,
-    )(keys, values, log_forget, write_rate)
+        [
+            pltpu.VMEM((tokens, wide), BF16),
+            pltpu.VMEM((tokens, wide), BF16),
+            pltpu.VMEM((heads, tokens), F32),
+            pltpu.VMEM((heads, tokens), F32),
+            pltpu.SemaphoreType.DMA((4,)),
+            pltpu.SemaphoreType.DMA,
+        ],
+        (VMEM,) * 5 + (HBM,),
+    )(*sources)
 
     core, lifted = call(
         reads_kernel,
@@ -313,15 +344,17 @@
         1_000_000,
     )(queries, keys, bases, writes, rows, inner, level_weight)
 
-    theirs = lax.ppermute(total, "seq", [(i, i ^ 1) for i in range(seq)])
+    cores = [(i, i ^ 1) for i in range(seq)]
+    theirs = lax.ppermute(total, "seq", cores)
+    direct = lax.ppermute(w_half, "head", pairs)
     matrix = shape((heads, DK, DK))
     total, level, before = call(
         merge_kernel,
         (shape((heads, DK, 2 * DK)), matrix, matrix),
-        [SMEM] + [VMEM] * 2,
+        [VMEM] * 2,
         40_000_000,
         500_000,
-    )(position, total, theirs)
+    )(total, theirs)
     collected = [level]
 
     def gathered(b):
@@ -333,35 +366,49 @@
         total, low, high, before = call(
             lambda *refs, b=b: quad_kernel(b, *refs),
             (shape((heads, DK, 2 * DK)), matrix, matrix, matrix),
-            [SMEM] + [VMEM] * 2,
+            [VMEM] * 2,
             100_000_000,
             1_000_000,
-        )(position, gathered(b), before)
+        )(gathered(b), before)
         collected += [low, high]
     four = gathered(outer - 2)
     keep, give = call(
         lambda *refs: finish_kernel(outer, ring // 2, *refs),
         (shape((tokens // 2, wide)), shape((tokens // 2, wide))),
-        [SMEM] + [VMEM] * (6 + outer - 2),
+        [VMEM] * (6 + outer - 2),
         100_000_000,
         1_000_000,
         [pltpu.VMEM((tokens, wide), BF16)],
-    )(position, core, lifted, four, before, level_weight, gate, *collected)
+    )(core, lifted, four, before, level_weight, gate, *collected)
+    give, direct = lax.optimization_barrier((give, direct))
     got = lax.ppermute(give, "head", pairs)
+    across = lax.ppermute(direct, "seq", cores)
     columns = w_out.shape[1]
     step = columns // 4
     chunk = tokens // ring
+
+    def by_columns(rows):
+        return pl.BlockSpec((rows, step), lambda c: (0, c))
+
     whole = pl.BlockSpec((tokens // 2, wide), lambda c: (0, 0))
-    block = pl.BlockSpec((wide, step), lambda c: (0, c))
+    sums = pl.pallas_call(
+        project_own_kernel,
+        grid=(columns // step,),
+        out_shape=shape((tokens // 2, columns), F32),
+        in_specs=[whole, by_columns(wide)],
+        out_specs=by_columns(tokens // 2),
+        compiler_params=pltpu.CompilerParams(vmem_limit_bytes=16 << 20),
+        cost_estimate=pl.CostEstimate(flops=300_000_000, bytes_accessed=4_000_000, transcendentals=0),
+    )(keep, w_out)
     terms = pl.pallas_call(
         project_kernel,
         grid=(columns // step,),
         out_shape=[shape((chunk, columns))] * (ring // 2),
-        in_specs=[whole, whole, block, block],
-        out_specs=[pl.BlockSpec((chunk, step), lambda c: (0, c))] * (ring // 2),
-        compiler_params=pltpu.CompilerParams(vmem_limit_bytes=VMEM_BYTES),
-        cost_estimate=pl.CostEstimate(flops=600_000_000, bytes_accessed=6_000_000, transcendentals=0),
-    )(keep, got, w_out, w_pair)
+        in_specs=[whole, by_columns(tokens // 2), by_columns(DK), by_columns(DK)],
+        out_specs=[by_columns(chunk)] * (ring // 2),
+        compiler_params=pltpu.CompilerParams(vmem_limit_bytes=16 << 20),
+        cost_estimate=pl.CostEstimate(flops=300_000_000, bytes_accessed=6_000_000, transcendentals=0),
+    )(got, sums, direct, across)
     return ring_sum(terms)
 
 

time: 104 us -> 101 us (0.971)
  starting transfers between devices: 38.6 us -> 44.3 us
  waiting for transfers between devices: 18.7 us -> 13.9 us
  local copies, waits for them, and re-layouts: 3.18 us -> 0.02 us
    ppermute x9 -> x10, starting transfers between devices: 36.1 us -> 41.8 us  [the longest x7 35.9 us: hop(): return lax.ppermute(block, 'head', route).astype(F32)]
    ppermute x9 -> x10, waiting for transfers between devices: 15 us -> 11.3 us  [the longest x7 11.2 us: hop(): return lax.ppermute(block, 'head', route).astype(F32)]
    unnamed x16 -> x10, local copies, waits for them, and re-layouts: 3.18 us -> 0.02 us
    pallas_call x1, Pallas kernels: 3.32 us -> 1.61 us  [on_device(): pl.pallas_call(project_kernel, grid=(columns // step,), out_shape=[shape(...]
    pallas_call x1, Pallas kernels: 5.6 us -> 6.7 us  [on_device(): call(states_kernel, (shape((heads, DK, 2 * DK)), shape((heads, 4, DK, 2 *...]
    ppermute x1, waiting for transfers between devices: 3.68 us -> 2.59 us  [on_device(): got = lax.ppermute(give, 'head', pairs)]
  transfers between devices with their start and end apart: 10 -> 11, of which waited for: 7 -> 7; matrix products, arithmetic and copies ran while one was open for 0% -> 0% of each run, Pallas kernels for 10% -> 4%
where the time goes in v4:
time: 101 us
  starting transfers between devices  44.3 us (44%)
  blocking collectives  28.8 us (29%)
  waiting for transfers between devices  13.9 us (14%)
  Pallas kernels  12.4 us (12%)
    ppermute x7, starting transfers between devices, hop(): return lax.ppermute(block, 'head', route).astype(F32)  35.9 us
    all_gather x2, blocking collectives, gathered(): return lax.all_gather(total, 'seq', axis=0, axis_index_groups=groups)  28.8 us
    ppermute x7, waiting for transfers between devices, hop(): return lax.ppermute(block, 'head', route).astype(F32)  11.2 us
    pallas_call x1, Pallas kernels, on_device(): call(states_kernel, (shape((heads, DK, 2 * DK)), shape((heads, 4, DK, 2 *...  6.7 us
    ppermute x1, waiting for transfers between devices, on_device(): got = lax.ppermute(give, 'head', pairs)  2.59 us
    ppermute x1, starting transfers between devices, on_device(): got = lax.ppermute(give, 'head', pairs)  2.52 us
    ppermute x1, starting transfers between devices, on_device(): direct = lax.ppermute(w_half, 'head', pairs)  2.02 us
  transfers between devices with their start and end apart: 11, of which 7 were waited for; matrix products, arithmetic and copies ran while one was open for 0% of the time, Pallas kernels for 4%

profile of v4, /device:TPU:34, one launch (start us, length us, event | category | flops | bytes accessed | tf_op | source)
XLA Modules:
  0.0 100.6 jit_solution(5924402652709362618)
XLA Ops:
  0.0 0.0 copy-start.4
  0.0 0.0 copy-start.2
  0.0 0.0 copy-start.3
  0.0 6.7 %shard_map.82 = (bf16[2,128,256]{2,1,0:T(8,128)(2,1)S(1)}, bf16[2,4,128,256]{3,2,1,0:T(8,128)(2,1)S(1)}, f32[256,256]{1,0:T(8,128)S(1)}, f32[256,256]{1,0:T(8,12...) custom-call(bf16[256,256]{1,0:T(8,128)(2,1)} %k_ref.1, bf16[256,256]{1,0:T(8,128)(2,1)} %v_in.1, ...), custom_call_target="tpu_custom_call" | custom-call | flops 2000000000 | bytes 1000000 | tf_op jit(solution)/shard_map/pallas_call | solution.py:315
  6.7 2.0 %collective-permute-start.1 = (bf16[128,4096]{1,0:T(8,128)(2,1)S(1)}, bf16[128,4096]{1,0:T(8,128)(2,1)S(1)}, u32[]{:S(2)}, u32[]{:S(2)}) collective-permute-start(bf16[128,4096]{1,0:T(8,128)(2,1)S(1)} %get-tuple-element.47), channel_id=1, source_target_pairs={{0,1},{1,0},{2,3},{3,2},{4,5},{5,4},{6,7},{7,6},{8,9},{9,8},{10,11... | collective-permute-start | bytes 3145736 | tf_op jit(solution)/shard_map/ppermute | solution.py:349
  8.7 1.9 %collective-permute-start = (bf16[2,128,256]{2,1,0:T(8,128)(2,1)S(1)}, bf16[2,128,256]{2,1,0:T(8,128)(2,1)S(1)}, u32[]{:S(2)}, u32[]{:S(2)}) collective-permute-start(bf16[2,128,256]{2,1,0:T(8,128)(2,1)S(1)} %get-tuple-element.38.mine_ref), channel_id=1, source_target_pairs={{0,16},{16,0},{32,48},{48,32},{64,80},{80,64},{96,112},{112,96},{1... | collective-permute-start | bytes 393224 | tf_op jit(solution)/shard_map/ppermute | solution.py:348
  10.7 0.0 copy-done.4
  10.7 0.0 copy-done.2
  10.7 0.0 copy-done.3
  10.7 0.0 copy-start.1
  10.7 1.2 %shard_map.83 = (f32[256,256]{1,0:T(8,128)S(1)}, bf16[256,256]{1,0:T(8,128)(2,1)S(1)}) custom-call(bf16[256,256]{1,0:T(8,128)(2,1)S(1)} %copy-done.3, bf16[256,256]{1,0:T(8,128)(2,1)S(1)} %copy-done.4, f32[256,256]{1,0:T(8,128)S(1)} %get-tuple-element.32.w_ref, f32[256,256]{1,0:T(8,128)S(1)} %get-tuple-element.33.u_ref, ...), custom_call_target="tpu_custom_call" | custom-call | flops 1000000000 | bytes 1000000 | tf_op jit(solution)/shard_map/pallas_call | solution.py:339
  11.9 0.0 copy-start
  11.9 0.1 collective-permute-done.theirs_ref
  12.0 0.2 shard_map.84
  12.2 16.0 %all-gather = bf16[8,128,256]{2,1,0:T(8,128)(2,1)S(1)} all-gather(bf16[2,128,256]{2,1,0:T(8,128)(2,1)S(1)} %get-tuple-element.39), channel_id=2, replica_groups={{0,32,64,96},{16,48,80,112},{128,160,192,224},{144,176,208,240},{256,28..., dimensions={0}, use_global_device_ids=true | all-gather | bytes 655360 | tf_op jit(solution)/shard_map/all_gather | solution.py:363
  28.2 0.6 shard_map.85
  28.8 12.8 %all-gather.1 = bf16[8,128,256]{2,1,0:T(8,128)(2,1)S(1)} all-gather(bf16[2,128,256]{2,1,0:T(8,128)(2,1)S(1)} %get-tuple-element.41), channel_id=3, replica_groups={{0,128,256,384},{16,144,272,400},{32,160,288,416},{48,176,304,432},{64,..., dimensions={0}, use_global_device_ids=true | all-gather | bytes 655360 | tf_op jit(solution)/shard_map/all_gather | solution.py:363
  41.6 0.0 copy-done.1
  41.6 0.9 shard_map.86
  42.5 0.0 collective-permute-done.1.direct_ref
  42.6 1.9 %collective-permute-start.3 = (bf16[128,4096]{1,0:T(8,128)(2,1)S(1)}, bf16[128,4096]{1,0:T(8,128)(2,1)S(1)}, u32[]{:S(2)}, u32[]{:S(2)}) collective-permute-start(bf16[128,4096]{1,0:T(8,128)(2,1)S(1)} %collective-permute-done.1.direct_ref), channel_id=1, source_target_pairs={{0,16},{16,0},{32,48},{48,32},{64,80},{80,64},{96,112},{112,96},{1... | collective-permute-start | bytes 3145736 | tf_op jit(solution)/shard_map/ppermute | solution.py:385
  44.5 2.5 %collective-permute-start.2 = (bf16[128,256]{1,0:T(8,128)(2,1)S(1)}, bf16[128,256]{1,0:T(8,128)(2,1)S(1)}, u32[]{:S(2)}, u32[]{:S(2)}) collective-permute-start(bf16[128,256]{1,0:T(8,128)(2,1)S(1)} %get-tuple-element.48), channel_id=1, source_target_pairs={{0,1},{1,0},{2,3},{3,2},{4,5},{5,4},{6,7},{7,6},{8,9},{9,8},{10,11... | collective-permute-start | bytes 196616 | tf_op jit(solution)/shard_map/ppermute | solution.py:384
  47.0 0.0 copy-done
  47.0 1.3 %shard_map.87.sums_ref = f32[128,4096]{1,0:T(8,128)S(1)} custom-call(bf16[128,256]{1,0:T(8,128)(2,1)S(1)} %get-tuple-element.49.keep_ref, bf16[256,4096]{1,0:T(8,128)(2,1)S(1)} %copy-done), custom_call_target="tpu_custom_call" | custom-call | flops 300000000 | bytes 4000000 | tf_op jit(solution)/shard_map/pallas_call | solution.py:394
  48.3 2.6 %collective-permute-done.2.got_ref = bf16[128,256]{1,0:T(8,128)(2,1)S(1)} collective-permute-done((bf16[128,256]{1,0:T(8,128)(2,1)S(1)}, bf16[128,256]{1,0:T(8,128)(2,1)S(1)}, u32[]{:S(2)}, u32[]{:S(2)}) %collective-permute-start.2) | collective-permute-done | bytes 65568 | tf_op jit(solution)/shard_map/ppermute | solution.py:384
  50.9 0.0 collective-permute-done.3.across_ref
  50.9 1.6 %shard_map.88 = (bf16[16,4096]{1,0:T(8,128)(2,1)S(1)}, bf16[16,4096]{1,0:T(8,128)(2,1)S(1)}, bf16[16,4096]{1,0:T(8,128)(2,1)S(1)}, bf16[16,4096]{1,0:T(8,128)(2,...) custom-call(bf16[128,256]{1,0:T(8,128)(2,1)S(1)} %collective-permute, ...), custom_call_target="tpu_custom_call" | custom-call | flops 300000000 | bytes 6000000 | tf_op jit(solution)/shard_map/pallas_call | solution.py:403
  52.5 10.5 %collective-permute-start.4 = (bf16[16,4096]{1,0:T(8,128)(2,1)S(1)}, bf16[16,4096]{1,0:T(8,128)(2,1)S(1)}, u32[]{:S(2)}, u32[]{:S(2)}) collective-permute-start(bf16[16,4096]{1,0:T(8,128)(2,1)S(1)} %get-tuple-element.51), channel_id=1, source_target_pairs={{0,2},{1,15},{2,4},{3,1},{4,6},{5,3},{6,8},{7,5},{8,10},{9,7},{10,... | collective-permute-start | bytes 393224 | tf_op jit(solution)/shard_map/ppermute | solution.py:291
  63.0 1.9 %collective-permute-start.8 = (bf16[16,4096]{1,0:T(8,128)(2,1)S(1)}, bf16[16,4096]{1,0:T(8,128)(2,1)S(1)}, u32[]{:S(2)}, u32[]{:S(2)}) collective-permute-start(bf16[16,4096]{1,0:T(8,128)(2,1)S(1)} %get-tuple-element.56), channel_id=1, source_target_pairs={{0,14},{1,3},{2,0},{3,5},{4,2},{5,7},{6,4},{7,9},{8,6},{9,11},{10,... | collective-permute-start | bytes 393224 | tf_op jit(solution)/shard_map/ppermute | solution.py:291
  65.0 3.2 %collective-permute-done.4 = bf16[16,4096]{1,0:T(8,128)(2,1)S(1)} collective-permute-done((bf16[16,4096]{1,0:T(8,128)(2,1)S(1)}, bf16[16,4096]{1,0:T(8,128)(2,1)S(1)}, u32[]{:S(2)}, u32[]{:S(2)}) %collective-permute-start.4) | collective-permute-done | bytes 131104 | tf_op jit(solution)/shard_map/ppermute | solution.py:291
  68.2 6.6 %collective-permute-start.5 = (bf16[16,4096]{1,0:T(8,128)(2,1)S(1)}, bf16[16,4096]{1,0:T(8,128)(2,1)S(1)}, u32[]{:S(2)}, u32[]{:S(2)}) collective-permute-start(bf16[16,4096]{1,0:T(8,128)(2,1)S(1)} %add_convert_fusion.5), channel_id=1, source_target_pairs={{0,2},{1,15},{2,4},{3,1},{4,6},{5,3},{6,8},{7,5},{8,10},{9,7},{10,... | collective-permute-start | bytes 393224 | tf_op jit(solution)/shard_map/ppermute | solution.py:291
  74.8 0.0 collective-permute-done.8
  74.8 1.9 %collective-permute-start.9 = (bf16[16,4096]{1,0:T(8,128)(2,1)S(1)}, bf16[16,4096]{1,0:T(8,128)(2,1)S(1)}, u32[]{:S(2)}, u32[]{:S(2)}) collective-permute-start(bf16[16,4096]{1,0:T(8,128)(2,1)S(1)} %add_convert_fusion.2), channel_id=1, source_target_pairs={{0,14},{1,3},{2,0},{3,5},{4,2},{5,7},{6,4},{7,9},{8,6},{9,11},{10,... | collective-permute-start | bytes 393224 | tf_op jit(solution)/shard_map/ppermute | solution.py:291
  76.8 2.3 %collective-permute-done.5 = bf16[16,4096]{1,0:T(8,128)(2,1)S(1)} collective-permute-done((bf16[16,4096]{1,0:T(8,128)(2,1)S(1)}, bf16[16,4096]{1,0:T(8,128)(2,1)S(1)}, u32[]{:S(2)}, u32[]{:S(2)}) %collective-permute-start.5) | collective-permute-done | bytes 131104 | tf_op jit(solution)/shard_map/ppermute | solution.py:291
  79.1 6.5 %collective-permute-start.6 = (bf16[16,4096]{1,0:T(8,128)(2,1)S(1)}, bf16[16,4096]{1,0:T(8,128)(2,1)S(1)}, u32[]{:S(2)}, u32[]{:S(2)}) collective-permute-start(bf16[16,4096]{1,0:T(8,128)(2,1)S(1)} %add_convert_fusion.4), channel_id=1, source_target_pairs={{0,2},{1,15},{2,4},{3,1},{4,6},{5,3},{6,8},{7,5},{8,10},{9,7},{10,... | collective-permute-start | bytes 393224 | tf_op jit(solution)/shard_map/ppermute | solution.py:291
  85.6 1.1 %collective-permute-done.9 = bf16[16,4096]{1,0:T(8,128)(2,1)S(1)} collective-permute-done((bf16[16,4096]{1,0:T(8,128)(2,1)S(1)}, bf16[16,4096]{1,0:T(8,128)(2,1)S(1)}, u32[]{:S(2)}, u32[]{:S(2)}) %collective-permute-start.9) | collective-permute-done | bytes 131104 | tf_op jit(solution)/shard_map/ppermute | solution.py:291
  86.8 1.9 %collective-permute-start.10 = (bf16[16,4096]{1,0:T(8,128)(2,1)S(1)}, bf16[16,4096]{1,0:T(8,128)(2,1)S(1)}, u32[]{:S(2)}, u32[]{:S(2)}) collective-permute-start(bf16[16,4096]{1,0:T(8,128)(2,1)S(1)} %add_convert_fusion.1), channel_id=1, source_target_pairs={{0,14},{1,3},{2,0},{3,5},{4,2},{5,7},{6,4},{7,9},{8,6},{9,11},{10,... | collective-permute-start | bytes 393224 | tf_op jit(solution)/shard_map/ppermute | solution.py:291
  88.7 2.1 %collective-permute-done.6 = bf16[16,4096]{1,0:T(8,128)(2,1)S(1)} collective-permute-done((bf16[16,4096]{1,0:T(8,128)(2,1)S(1)}, bf16[16,4096]{1,0:T(8,128)(2,1)S(1)}, u32[]{:S(2)}, u32[]{:S(2)}) %collective-permute-start.6) | collective-permute-done | bytes 131104 | tf_op jit(solution)/shard_map/ppermute | solution.py:291
  90.8 6.6 %collective-permute-start.7 = (bf16[16,4096]{1,0:T(8,128)(2,1)S(1)}, bf16[16,4096]{1,0:T(8,128)(2,1)S(1)}, u32[]{:S(2)}, u32[]{:S(2)}) collective-permute-start(bf16[16,4096]{1,0:T(8,128)(2,1)S(1)} %add_convert_fusion.3), channel_id=1, source_target_pairs={{0,2},{1,15},{2,4},{3,1},{4,6},{5,3},{6,8},{7,5},{8,10},{9,7},{10,... | collective-permute-start | bytes 393224 | tf_op jit(solution)/shard_map/ppermute | solution.py:291
  97.4 0.0 collective-permute-done.10
  97.4 2.5 %collective-permute-done.7 = bf16[16,4096]{1,0:T(8,128)(2,1)S(1)} collective-permute-done((bf16[16,4096]{1,0:T(8,128)(2,1)S(1)}, bf16[16,4096]{1,0:T(8,128)(2,1)S(1)}, u32[]{:S(2)}, u32[]{:S(2)}) %collective-permute-start.7) | collective-permute-done | bytes 131104 | tf_op jit(solution)/shard_map/ppermute | solution.py:291
  99.9 0.7 add_convert_fusion
  (5 shorter events, 0.2 us)
Async XLA Ops:
  0.0 10.7 %copy-start.4 = (bf16[256,256]{1,0:T(8,128)(2,1)S(1)}, bf16[256,256]{1,0:T(8,128)(2,1)}, u32[]{:S(2)}) copy-start(bf16[256,256]{1,0:T(8,128)(2,1)} %k_ref.1) | copy-start | bytes 393220
  0.0 10.7 %copy-start.2 = (f32[2,8,256]{2,1,0:T(8,128)S(1)}, f32[2,8,256]{2,1,0:T(8,128)}, u32[]{:S(2)}) copy-start(f32[2,8,256]{2,1,0:T(8,128)} %refs_4_.1) | copy-start | bytes 49156
  0.0 10.7 %copy-start.3 = (bf16[256,256]{1,0:T(8,128)(2,1)S(1)}, bf16[256,256]{1,0:T(8,128)(2,1)}, u32[]{:S(2)}) copy-start(bf16[256,256]{1,0:T(8,128)(2,1)} %q_ref.1) | copy-start | bytes 393220
  6.7 35.8 %collective-permute-start.1 = (bf16[128,4096]{1,0:T(8,128)(2,1)S(1)}, bf16[128,4096]{1,0:T(8,128)(2,1)S(1)}, u32[]{:S(2)}, u32[]{:S(2)}) collective-permute-start(bf16[128,4096]{1,0:T(8,128)(2,1)S(1)} %get-tuple-element.47), channel_id=1, source_target_pairs={{0,1},{1,0},{2,3},{3,2},{4,5},{5,4},{6,7},{7,6},{8,9},{9,8},{10,11... | collective-permute-start | bytes 3145736 | tf_op jit(solution)/shard_map/ppermute | solution.py:349
  8.7 3.2 %collective-permute-start = (bf16[2,128,256]{2,1,0:T(8,128)(2,1)S(1)}, bf16[2,128,256]{2,1,0:T(8,128)(2,1)S(1)}, u32[]{:S(2)}, u32[]{:S(2)}) collective-permute-start(bf16[2,128,256]{2,1,0:T(8,128)(2,1)S(1)} %get-tuple-element.38.mine_ref), channel_id=1, source_target_pairs={{0,16},{16,0},{32,48},{48,32},{64,80},{80,64},{96,112},{112,96},{1... | collective-permute-start | bytes 393224 | tf_op jit(solution)/shard_map/ppermute | solution.py:348
  10.7 30.9 %copy-start.1 = (bf16[256,256]{1,0:T(8,128)(2,1)S(1)}, bf16[256,256]{1,0:T(8,128)(2,1)}, u32[]{:S(2)}) copy-start(bf16[256,256]{1,0:T(8,128)(2,1)} %refs_5_.1) | copy-start | bytes 393220
  11.9 35.1 %copy-start = (bf16[256,4096]{1,0:T(8,128)(2,1)S(1)}, bf16[256,4096]{1,0:T(8,128)(2,1)}, u32[]{:S(2)}) copy-start(bf16[256,4096]{1,0:T(8,128)(2,1)} %mine_ref.1) | copy-start | bytes 6291460
  42.6 8.3 %collective-permute-start.3 = (bf16[128,4096]{1,0:T(8,128)(2,1)S(1)}, bf16[128,4096]{1,0:T(8,128)(2,1)S(1)}, u32[]{:S(2)}, u32[]{:S(2)}) collective-permute-start(bf16[128,4096]{1,0:T(8,128)(2,1)S(1)} %collective-permute-done.1.direct_ref), channel_id=1, source_target_pairs={{0,16},{16,0},{32,48},{48,32},{64,80},{80,64},{96,112},{112,96},{1... | collective-permute-start | bytes 3145736 | tf_op jit(solution)/shard_map/ppermute | solution.py:385
  44.5 6.4 %collective-permute-start.2 = (bf16[128,256]{1,0:T(8,128)(2,1)S(1)}, bf16[128,256]{1,0:T(8,128)(2,1)S(1)}, u32[]{:S(2)}, u32[]{:S(2)}) collective-permute-start(bf16[128,256]{1,0:T(8,128)(2,1)S(1)} %get-tuple-element.48), channel_id=1, source_target_pairs={{0,1},{1,0},{2,3},{3,2},{4,5},{5,4},{6,7},{7,6},{8,9},{9,8},{10,11... | collective-permute-start | bytes 196616 | tf_op jit(solution)/shard_map/ppermute | solution.py:384
  52.5 15.7 %collective-permute-start.4 = (bf16[16,4096]{1,0:T(8,128)(2,1)S(1)}, bf16[16,4096]{1,0:T(8,128)(2,1)S(1)}, u32[]{:S(2)}, u32[]{:S(2)}) collective-permute-start(bf16[16,4096]{1,0:T(8,128)(2,1)S(1)} %get-tuple-element.51), channel_id=1, source_target_pairs={{0,2},{1,15},{2,4},{3,1},{4,6},{5,3},{6,8},{7,5},{8,10},{9,7},{10,... | collective-permute-start | bytes 393224 | tf_op jit(solution)/shard_map/ppermute | solution.py:291
  63.0 11.7 %collective-permute-start.8 = (bf16[16,4096]{1,0:T(8,128)(2,1)S(1)}, bf16[16,4096]{1,0:T(8,128)(2,1)S(1)}, u32[]{:S(2)}, u32[]{:S(2)}) collective-permute-start(bf16[16,4096]{1,0:T(8,128)(2,1)S(1)} %get-tuple-element.56), channel_id=1, source_target_pairs={{0,14},{1,3},{2,0},{3,5},{4,2},{5,7},{6,4},{7,9},{8,6},{9,11},{10,... | collective-permute-start | bytes 393224 | tf_op jit(solution)/shard_map/ppermute | solution.py:291
  68.2 10.9 %collective-permute-start.5 = (bf16[16,4096]{1,0:T(8,128)(2,1)S(1)}, bf16[16,4096]{1,0:T(8,128)(2,1)S(1)}, u32[]{:S(2)}, u32[]{:S(2)}) collective-permute-start(bf16[16,4096]{1,0:T(8,128)(2,1)S(1)} %add_convert_fusion.5), channel_id=1, source_target_pairs={{0,2},{1,15},{2,4},{3,1},{4,6},{5,3},{6,8},{7,5},{8,10},{9,7},{10,... | collective-permute-start | bytes 393224 | tf_op jit(solution)/shard_map/ppermute | solution.py:291
  74.8 11.9 %collective-permute-start.9 = (bf16[16,4096]{1,0:T(8,128)(2,1)S(1)}, bf16[16,4096]{1,0:T(8,128)(2,1)S(1)}, u32[]{:S(2)}, u32[]{:S(2)}) collective-permute-start(bf16[16,4096]{1,0:T(8,128)(2,1)S(1)} %add_convert_fusion.2), channel_id=1, source_target_pairs={{0,14},{1,3},{2,0},{3,5},{4,2},{5,7},{6,4},{7,9},{8,6},{9,11},{10,... | collective-permute-start | bytes 393224 | tf_op jit(solution)/shard_map/ppermute | solution.py:291
  79.1 11.6 %collective-permute-start.6 = (bf16[16,4096]{1,0:T(8,128)(2,1)S(1)}, bf16[16,4096]{1,0:T(8,128)(2,1)S(1)}, u32[]{:S(2)}, u32[]{:S(2)}) collective-permute-start(bf16[16,4096]{1,0:T(8,128)(2,1)S(1)} %add_convert_fusion.4), channel_id=1, source_target_pairs={{0,2},{1,15},{2,4},{3,1},{4,6},{5,3},{6,8},{7,5},{8,10},{9,7},{10,... | collective-permute-start | bytes 393224 | tf_op jit(solution)/shard_map/ppermute | solution.py:291
  86.8 10.6 %collective-permute-start.10 = (bf16[16,4096]{1,0:T(8,128)(2,1)S(1)}, bf16[16,4096]{1,0:T(8,128)(2,1)S(1)}, u32[]{:S(2)}, u32[]{:S(2)}) collective-permute-start(bf16[16,4096]{1,0:T(8,128)(2,1)S(1)} %add_convert_fusion.1), channel_id=1, source_target_pairs={{0,14},{1,3},{2,0},{3,5},{4,2},{5,7},{6,4},{7,9},{8,6},{9,11},{10,... | collective-permute-start | bytes 393224 | tf_op jit(solution)/shard_map/ppermute | solution.py:291
  90.8 9.1 %collective-permute-start.7 = (bf16[16,4096]{1,0:T(8,128)(2,1)S(1)}, bf16[16,4096]{1,0:T(8,128)(2,1)S(1)}, u32[]{:S(2)}, u32[]{:S(2)}) collective-permute-start(bf16[16,4096]{1,0:T(8,128)(2,1)S(1)} %add_convert_fusion.3), channel_id=1, source_target_pairs={{0,2},{1,15},{2,4},{3,1},{4,6},{5,3},{6,8},{7,5},{8,10},{9,7},{10,... | collective-permute-start | bytes 393224 | tf_op jit(solution)/shard_map/ppermute | solution.py:291

commit v5 on v4

--- a/solution.py
+++ b/solution.py
@@ -7,6 +7,7 @@
 
 DK = 128
 BLOCK = 64
+TILE = 128
 EPSILON = 1e-06
 F32 = jnp.float32
 BF16 = jnp.bfloat16
@@ -23,21 +24,23 @@
     return high, (matrix - high.astype(F32)).astype(BF16)
 
 
-def dot3(left, right):
-    (lh, ll), (rh, rl) = left, right
-    return dot(lh, rh) + (dot(lh, rl) + dot(ll, rh))
-
-
-def dot2(left, right):
-    high, low = halves(left)
-    return dot(high, right) + dot(low, right)
-
-
-def block_masks(tokens):
-    row = lax.broadcasted_iota(jnp.int32, (tokens, tokens), 0)
-    col = lax.broadcasted_iota(jnp.int32, (tokens, tokens), 1)
-    same = row // BLOCK == col // BLOCK
-    return row, col, same
+def paired(matrix):
+    return jnp.concatenate(halves(matrix), axis=1)
+
+
+def twice(matrix):
+    return jnp.concatenate([matrix, matrix], axis=0)
+
+
+def product(left, right):
+    wide = dot(left, twice(right))
+    return wide[:, :DK] + wide[:, DK:]
+
+
+def tile_masks():
+    row = lax.broadcasted_iota(jnp.int32, (TILE, TILE), 0)
+    col = lax.broadcasted_iota(jnp.int32, (TILE, TILE), 1)
+    return row, col, row // BLOCK == col // BLOCK
 
 
 def states_kernel(
@@ -58,91 +61,98 @@
         copy.wait()
     tokens = k_ref.shape[0]
     heads = lf_ref.shape[0]
-    blocks = tokens // BLOCK
-    row, col, same = block_masks(tokens)
+    tiles = tokens // TILE
+    row, col, same = tile_masks()
     inclusive = same & (row >= col)
     strict = same & (row > col)
     eye = (row == col).astype(F32)
-    log_forget = lf_ref[...]
-    rate = wr_ref[...]
+
+    def by_tile(ref):
+        return jnp.concatenate([ref[:, t * TILE : (t + 1) * TILE] for t in range(tiles)], axis=0)
+
+    log_forget, rate = by_tile(lf_ref), by_tile(wr_ref)
     exact = lax.Precision.HIGHEST
     cum = dot(log_forget, inclusive.astype(F32), ((1,), (1,)), exact)
     total = dot(log_forget, same.astype(F32), ((1,), (1,)), exact)
-    pad = jnp.zeros((8 - 3 * heads, tokens), F32)
+    count = tiles * heads
+    pad = jnp.zeros((16 - 3 * count, TILE), F32)
     columns = jnp.concatenate([cum, total, rate, pad], axis=0).T
-    eye_state = (
-        lax.broadcasted_iota(jnp.int32, (DK, DK), 0) == lax.broadcasted_iota(jnp.int32, (DK, DK), 1)
-    ).astype(F32)
-    inv_key_rows = []
-    lowers, keys, norms = [], [], []
-    for h in range(heads):
-        key = k_ref[:, h * DK : (h + 1) * DK]
+    units = [(t, h) for t in range(tiles) for h in range(heads)]
+    lowers, keys, norms, inverses = [], [], [], []
+    for n, (t, h) in enumerate(units):
+        key = k_ref[t * TILE : (t + 1) * TILE, h * DK : (h + 1) * DK]
         key_f = key.astype(F32)
         key_key = dot(key, key, ((1,), (1,)))
         inv_col = lax.rsqrt(jnp.sum(key_f * key_f, axis=1, keepdims=True) + EPSILON)
         inv_row = lax.rsqrt(jnp.sum(key_key * eye, axis=0, keepdims=True) + EPSILON)
-        inv_key_rows.append(inv_row)
-        rate_col = columns[:, 2 * heads + h : 2 * heads + h + 1]
-        lowers.append(jnp.where(strict, key_key * (rate_col * inv_col) * inv_row, 0.0))
+        rate_col = columns[:, 2 * count + n : 2 * count + n + 1]
+        lower = jnp.where(strict, key_key * (rate_col * inv_col) * inv_row, 0.0)
+        inverses.append(eye - jnp.where(row // 2 == col // 2, lower, 0.0))
+        lowers.append(paired(lower))
         keys.append((key, key_f))
         norms.append((inv_col, inv_row))
-    inverses = [eye - jnp.where(row // 2 == col // 2, lower, 0.0) for lower in lowers]
     width = 2
     while width < BLOCK:
-        band = (row // width != col // width) & (row // (2 * width) == col // (2 * width))
-        nexts = []
-        for h in range(heads):
-            inverse = halves(inverses[h])
-            inner = dot3(halves(jnp.where(band, lowers[h], 0.0)), inverse)
-            nexts.append(inverses[h] - dot3(inverse, halves(inner)))
-        inverses = nexts
+        band = ((row // width != col // width) & (row // (2 * width) == col // (2 * width))).astype(F32).astype(BF16)
+        band = jnp.concatenate([band, band], axis=1)
+        split = [paired(inverse) for inverse in inverses]
+        inner = [product(lowers[n] * band, split[n]) for n in range(count)]
+        inverses = [inverses[n] - product(split[n], paired(inner[n])) for n in range(count)]
         width *= 2
+    blocks = tokens // BLOCK
+    leaf = {}
+    for n, (t, h) in enumerate(units):
+        rows = slice(t * TILE, (t + 1) * TILE)
+        lanes = slice(h * DK, (h + 1) * DK)
+        key, key_f = keys[n]
+        inv_col, inv_row = norms[n]
+        cum_col = columns[:, n : n + 1]
+        total_col = columns[:, count + n : count + n + 1]
+        fading = jnp.exp(jnp.where(inclusive, cum_col - cum[n : n + 1], -1e30))
+        solved = inverses[n] * rate[n : n + 1]
+        bases = dot(paired(solved * inv_row), twice(key))
+        writes = dot(paired(solved * fading), twice(v_ref[rows, lanes]))
+        w_ref[rows, lanes] = bases
+        u_ref[rows, lanes] = writes
+        both = jnp.concatenate([writes * (jnp.exp(total_col - cum_col) * inv_col), bases * inv_col], axis=1)
+        turned = key_f.T
+        picked = [jnp.where(col // BLOCK == b, turned, 0.0).astype(BF16) for b in range(TILE // BLOCK)]
+        picked = jnp.concatenate([jnp.concatenate([p, p], axis=1) for p in picked], axis=0)
+        raw = dot(picked, jnp.concatenate(halves(both), axis=0))
+        for b in range(TILE // BLOCK):
+            part = raw[b * DK : (b + 1) * DK]
+            fade = jnp.exp(total[n : n + 1, b * BLOCK : b * BLOCK + 1])
+            leaf[h, t * (TILE // BLOCK) + b] = part[:, :DK], fade * (eye - part[:, DK:])
+
+    def merge(lead, trail):
+        moved = dot(trail[1].astype(BF16), jnp.concatenate(lead, axis=1).astype(BF16))
+        return moved[:, :DK] + trail[0], moved[:, DK:]
+
+    def stored(state):
+        return jnp.concatenate(state, axis=1).astype(BF16)
+
+    firsts = [merge(leaf[h, 0], leaf[h, 1]) for h in range(heads)]
+    seconds = [merge(leaf[h, 2], leaf[h, 3]) for h in range(heads)]
     for h in range(heads):
-        key, key_f = keys[h]
-        inv_col, inv_row = norms[h]
-        value = v_ref[:, h * DK : (h + 1) * DK]
-        cum_row = cum[h : h + 1]
-        cum_col = columns[:, h : h + 1]
-        total_col = columns[:, heads + h : heads + h + 1]
-        rate_row = rate[h : h + 1]
-        fading = jnp.exp(jnp.where(inclusive, cum_col - cum_row, -1e30))
-        solved = inverses[h] * rate_row
-        bases = dot2(solved * inv_row, key)
-        writes = dot2(solved * fading, value)
-        w_ref[:, h * DK : (h + 1) * DK] = bases
-        u_ref[:, h * DK : (h + 1) * DK] = writes
-        both = jnp.concatenate(
-            [writes * (jnp.exp(total_col - cum_col) * inv_col), bases * inv_col], axis=1
+        x_ref[h] = stored(merge(firsts[h], seconds[h]))
+    for h in range(heads):
+        y_ref[h, 0] = stored(leaf[h, 0])
+        y_ref[h, 1] = stored(firsts[h])
+        y_ref[h, 2] = dot(leaf[h, 2][1].astype(BF16), stored(firsts[h])).astype(BF16)
+        y_ref[h, 3] = stored(leaf[h, 2])
+    filler = jnp.zeros((8 - 2 * heads, TILE), F32)
+    for t in range(tiles):
+        found = [norms[t * heads + h][1] for h in range(heads)]
+        rows_ref[:, t * TILE : (t + 1) * TILE] = jnp.concatenate(
+            [cum[t * heads : (t + 1) * heads]] + found + [filler], axis=0
         )
-        both_high, both_low = halves(both)
-        leaf = []
-        for g in range(blocks):
-            span = slice(g * BLOCK, (g + 1) * BLOCK)
-            turned = key_f[span].T.astype(BF16)
-            raw = dot(turned, both_high[span]) + dot(turned, both_low[span])
-            fade = jnp.exp(total[h : h + 1, g * BLOCK : g * BLOCK + 1])
-            leaf.append(jnp.concatenate([raw[:, :DK], fade * (eye_state - raw[:, DK:])], axis=1))
-        short = [x.astype(BF16) for x in leaf]
-
-        def merge(lead, trail):
-            moved = dot(trail[:, DK:].astype(BF16), lead.astype(BF16))
-            return jnp.concatenate([moved[:, :DK] + trail[:, :DK], moved[:, DK:]], axis=1)
-
-        first = merge(leaf[0], leaf[1])
-        second = merge(leaf[2], leaf[3])
-        y_ref[h, 0] = short[0]
-        y_ref[h, 1] = first.astype(BF16)
-        y_ref[h, 2] = dot(short[2][:, DK:], first.astype(BF16)).astype(BF16)
-        y_ref[h, 3] = short[2]
-        x_ref[h] = merge(first, second).astype(BF16)
     half.wait()
-    rows_ref[...] = jnp.concatenate([cum] + inv_key_rows + [jnp.zeros((8 - 2 * heads, tokens), F32)], axis=0)
 
 
 def reads_kernel(q_ref, k_ref, w_ref, u_ref, rows_ref, y_ref, lw_ref, core_ref, lift_ref):
     tokens = k_ref.shape[0]
     heads = y_ref.shape[0]
-    row, col, same = block_masks(tokens)
+    row, col, same = tile_masks()
     inclusive = same & (row >= col)
     rows = rows_ref[...]
     columns = rows.T
@@ -150,36 +160,38 @@
     weights = lw_ref[...].reshape(heads * levels, tokens).T
     for h in range(heads):
         lanes = slice(h * DK, (h + 1) * DK)
-        query = q_ref[:, lanes]
-        key = k_ref[:, lanes]
-        query_f = query.astype(F32)
-        inv_query = lax.rsqrt(jnp.sum(query_f * query_f, axis=1, keepdims=True) + EPSILON)
-        query_key = dot(query, key, ((1,), (1,))) * inv_query * rows[heads + h : heads + h + 1]
-        cum_col = columns[:, h : h + 1]
-        fading = jnp.exp(jnp.where(inclusive, cum_col - rows[h : h + 1], -1e30))
-        own = dot3(halves(query_key * fading), halves(u_ref[:, lanes]))
-        masked = jnp.where(inclusive, query_key, 0.0)
-        reach = jnp.exp(cum_col) * (query_f * inv_query - dot3(halves(masked), halves(w_ref[:, lanes])))
-        reach_s = reach.astype(BF16)
 
         def weight(level, span):
             at = h * levels + level
             return weights[span, at : at + 1]
 
+        owns, reaches = [], []
+        for t in range(tokens // TILE):
+            here = slice(t * TILE, (t + 1) * TILE)
+            query = q_ref[here, lanes]
+            query_f = query.astype(F32)
+            inv_query = lax.rsqrt(jnp.sum(query_f * query_f, axis=1, keepdims=True) + EPSILON)
+            query_key = dot(query, k_ref[here, lanes], ((1,), (1,))) * inv_query * rows[heads + h : heads + h + 1, here]
+            cum_col = columns[here, h : h + 1]
+            fading = jnp.exp(jnp.where(inclusive, cum_col - rows[h : h + 1, here], -1e30))
+            owns.append(product(paired(query_key * fading), paired(u_ref[here, lanes])))
+            masked = jnp.where(inclusive, query_key, 0.0)
+            reach = query_f * inv_query - product(paired(masked), paired(w_ref[here, lanes]))
+            reaches.append((jnp.exp(cum_col) * reach).astype(BF16))
         spans = [slice(g * BLOCK, (g + 1) * BLOCK) for g in range(4)]
-        read1 = dot(reach_s[spans[1]], y_ref[h, 0])
-        read2 = dot(reach_s[spans[2]], y_ref[h, 1])
-        read3 = dot(reach_s[spans[3]], y_ref[h, 2])
-        near3 = dot(reach_s[spans[3]], y_ref[h, 3, :, :DK])
-        core_ref[spans[0], lanes] = weight(0, spans[0]) * own[spans[0]]
-        core_ref[spans[1], lanes] = weight(0, spans[1]) * own[spans[1]] + weight(1, spans[1]) * read1[:, :DK]
-        core_ref[spans[2], lanes] = weight(0, spans[2]) * own[spans[2]] + weight(2, spans[2]) * read2[:, :DK]
+        own = [owns[g // 2][spans[g % 2]] for g in range(4)]
+        reach = [reaches[g // 2][spans[g % 2]] for g in range(4)]
+        read1 = dot(reach[1], y_ref[h, 0])
+        read2 = dot(reach[2], y_ref[h, 1])
+        read3 = dot(reach[3], y_ref[h, 2])
+        near3 = dot(reach[3], y_ref[h, 3, :, :DK])
+        core_ref[spans[0], lanes] = weight(0, spans[0]) * own[0]
+        core_ref[spans[1], lanes] = weight(0, spans[1]) * own[1] + weight(1, spans[1]) * read1[:, :DK]
+        core_ref[spans[2], lanes] = weight(0, spans[2]) * own[2] + weight(2, spans[2]) * read2[:, :DK]
         core_ref[spans[3], lanes] = (
-            weight(0, spans[3]) * own[spans[3]]
-            + weight(1, spans[3]) * near3
-            + weight(2, spans[3]) * read3[:, :DK]
+            weight(0, spans[3]) * own[3] + weight(1, spans[3]) * near3 + weight(2, spans[3]) * read3[:, :DK]
         )
-        lift_ref[spans[0], lanes] = reach_s[spans[0]]
+        lift_ref[spans[0], lanes] = reach[0]
         lift_ref[spans[1], lanes] = read1[:, DK:].astype(BF16)
         lift_ref[spans[2], lanes] = read2[:, DK:].astype(BF16)
         lift_ref[spans[3], lanes] = read3[:, DK:].astype(BF16)
@@ -243,7 +255,7 @@
     chunk = tokens // (2 * ring)
     pair = lax.axis_index("head") // 2
     parity = lax.rem(lax.axis_index("head"), 2)
-    side = 1 - 2 * parity
+    side = 1 - 2 * lax.rem(lax.axis_index("head") + lax.axis_index("seq"), 2)
     for j in range(ring):
         kept = 2 * lax.rem(pair + ring + side * (ring // 2 - j), ring) + parity
         given = 2 * lax.rem(pair + ring - side * (ring // 2 - j), ring) + 1 - parity
@@ -285,10 +297,15 @@
     ring = len(terms)
     half = ring // 2
     count = 2 * ring
+    slabs = lax.axis_size("seq")
 
     def hop(block, way):
-        route = [(z, (z + 2 * way * (1 - 2 * (z % 2))) % count) for z in range(count)]
-        return lax.ppermute(block, "head", route).astype(F32)
+        route = []
+        for s in range(slabs):
+            for z in range(count):
+                step = 2 * way * (1 - 2 * ((s + z) % 2))
+                route.append((s * count + z, s * count + (z + step) % count))
+        return lax.ppermute(block, ("seq", "head"), route).astype(F32)
 
     ahead, behind = terms[0], terms[ring - 1]
     for t in range(1, half):

time: 101 us -> 99.8 us (0.988)
  Pallas kernels: 12.4 us -> 10 us
    pallas_call x1, Pallas kernels: 6.7 us -> 4.26 us  [on_device(): call(states_kernel, (shape((heads, DK, 2 * DK)), shape((heads, 4, DK, 2 *...]
    ppermute x7, waiting for transfers between devices: 11.2 us -> 12.3 us  [hop(): return lax.ppermute(block, ('seq', 'head'), route).astype(F32)]
  transfers between devices with their start and end apart: 11 -> 11, of which waited for: 7 -> 6; matrix products, arithmetic and copies ran while one was open for 0% -> 0% of each run, Pallas kernels for 4% -> 4%
where the time goes in v5:
time: 99.8 us; the launch traced here: 99.3 us
  starting transfers between devices  44.5 us (45%)
  blocking collectives  28.8 us (29%)
  waiting for transfers between devices  14.9 us (15%)
  Pallas kernels  10 us (10%)
    ppermute x7, starting transfers between devices, hop(): return lax.ppermute(block, ('seq', 'head'), route).astype(F32)  36 us
    all_gather x2, blocking collectives, gathered(): return lax.all_gather(total, 'seq', axis=0, axis_index_groups=groups)  28.8 us
    ppermute x7, waiting for transfers between devices, hop(): return lax.ppermute(block, ('seq', 'head'), route).astype(F32)  12.3 us
    pallas_call x1, Pallas kernels, on_device(): call(states_kernel, (shape((heads, DK, 2 * DK)), shape((heads, 4, DK, 2 *...  4.26 us
    ppermute x1, starting transfers between devices, on_device(): got = lax.ppermute(give, 'head', pairs)  2.57 us
    ppermute x1, waiting for transfers between devices, on_device(): got = lax.ppermute(give, 'head', pairs)  2.54 us
    ppermute x1, starting transfers between devices, on_device(): direct = lax.ppermute(w_half, 'head', pairs)  2.02 us
  transfers between devices with their start and end apart: 11, of which 6 were waited for; matrix products, arithmetic and copies ran while one was open for 0% of the time, Pallas kernels for 4%

profile of v5, /device:TPU:34, one launch (start us, length us, event | category | flops | bytes accessed | tf_op | source)
XLA Modules:
  0.0 99.3 jit_solution(15420971947497866242)
XLA Ops:
  0.0 0.0 copy-start.4
  0.0 0.0 copy-start.2
  0.0 0.0 copy-start.3
  0.0 4.3 %shard_map.82 = (bf16[2,128,256]{2,1,0:T(8,128)(2,1)S(1)}, bf16[2,4,128,256]{3,2,1,0:T(8,128)(2,1)S(1)}, f32[256,256]{1,0:T(8,128)S(1)}, f32[256,256]{1,0:T(8,12...) custom-call(bf16[256,256]{1,0:T(8,128)(2,1)} %k_ref.1, bf16[256,256]{1,0:T(8,128)(2,1)} %v_in.1, ...), custom_call_target="tpu_custom_call" | custom-call | flops 2000000000 | bytes 1000000 | tf_op jit(solution)/shard_map/pallas_call | solution.py:332
  4.3 2.0 %collective-permute-start.1 = (bf16[128,4096]{1,0:T(8,128)(2,1)S(1)}, bf16[128,4096]{1,0:T(8,128)(2,1)S(1)}, u32[]{:S(2)}, u32[]{:S(2)}) collective-permute-start(bf16[128,4096]{1,0:T(8,128)(2,1)S(1)} %get-tuple-element.47), channel_id=1, source_target_pairs={{0,1},{1,0},{2,3},{3,2},{4,5},{5,4},{6,7},{7,6},{8,9},{9,8},{10,11... | collective-permute-start | bytes 3145736 | tf_op jit(solution)/shard_map/ppermute | solution.py:366
  6.3 1.9 %collective-permute-start = (bf16[2,128,256]{2,1,0:T(8,128)(2,1)S(1)}, bf16[2,128,256]{2,1,0:T(8,128)(2,1)S(1)}, u32[]{:S(2)}, u32[]{:S(2)}) collective-permute-start(bf16[2,128,256]{2,1,0:T(8,128)(2,1)S(1)} %get-tuple-element.38.mine_ref), channel_id=1, source_target_pairs={{0,16},{16,0},{32,48},{48,32},{64,80},{80,64},{96,112},{112,96},{1... | collective-permute-start | bytes 393224 | tf_op jit(solution)/shard_map/ppermute | solution.py:365
  8.2 0.0 copy-done.4
  8.2 0.0 copy-done.2
  8.2 0.0 copy-done.3
  8.3 0.0 copy-start.1
  8.3 1.2 %shard_map.83 = (f32[256,256]{1,0:T(8,128)S(1)}, bf16[256,256]{1,0:T(8,128)(2,1)S(1)}) custom-call(bf16[256,256]{1,0:T(8,128)(2,1)S(1)} %copy-done.3, bf16[256,256]{1,0:T(8,128)(2,1)S(1)} %copy-done.4, f32[256,256]{1,0:T(8,128)S(1)} %get-tuple-element.32.w_ref, f32[256,256]{1,0:T(8,128)S(1)} %get-tuple-element.33.u_ref, ...), custom_call_target="tpu_custom_call" | custom-call | flops 1000000000 | bytes 1000000 | tf_op jit(solution)/shard_map/pallas_call | solution.py:356
  9.4 0.0 copy-start
  9.4 0.1 collective-permute-done.theirs_ref
  9.5 0.2 shard_map.84
  9.7 16.0 %all-gather = bf16[8,128,256]{2,1,0:T(8,128)(2,1)S(1)} all-gather(bf16[2,128,256]{2,1,0:T(8,128)(2,1)S(1)} %get-tuple-element.39), channel_id=2, replica_groups={{0,32,64,96},{16,48,80,112},{128,160,192,224},{144,176,208,240},{256,28..., dimensions={0}, use_global_device_ids=true | all-gather | bytes 655360 | tf_op jit(solution)/shard_map/all_gather | solution.py:380
  25.8 0.6 shard_map.85
  26.4 12.8 %all-gather.1 = bf16[8,128,256]{2,1,0:T(8,128)(2,1)S(1)} all-gather(bf16[2,128,256]{2,1,0:T(8,128)(2,1)S(1)} %get-tuple-element.41), channel_id=3, replica_groups={{0,128,256,384},{16,144,272,400},{32,160,288,416},{48,176,304,432},{64,..., dimensions={0}, use_global_device_ids=true | all-gather | bytes 655360 | tf_op jit(solution)/shard_map/all_gather | solution.py:380
  39.1 0.0 copy-done.1
  39.1 0.9 shard_map.86
  40.1 0.0 collective-permute-done.1.direct_ref
  40.1 1.9 %collective-permute-start.3 = (bf16[128,4096]{1,0:T(8,128)(2,1)S(1)}, bf16[128,4096]{1,0:T(8,128)(2,1)S(1)}, u32[]{:S(2)}, u32[]{:S(2)}) collective-permute-start(bf16[128,4096]{1,0:T(8,128)(2,1)S(1)} %collective-permute-done.1.direct_ref), channel_id=1, source_target_pairs={{0,16},{16,0},{32,48},{48,32},{64,80},{80,64},{96,112},{112,96},{1... | collective-permute-start | bytes 3145736 | tf_op jit(solution)/shard_map/ppermute | solution.py:402
  42.0 2.6 %collective-permute-start.2 = (bf16[128,256]{1,0:T(8,128)(2,1)S(1)}, bf16[128,256]{1,0:T(8,128)(2,1)S(1)}, u32[]{:S(2)}, u32[]{:S(2)}) collective-permute-start(bf16[128,256]{1,0:T(8,128)(2,1)S(1)} %get-tuple-element.48), channel_id=1, source_target_pairs={{0,1},{1,0},{2,3},{3,2},{4,5},{5,4},{6,7},{7,6},{8,9},{9,8},{10,11... | collective-permute-start | bytes 196616 | tf_op jit(solution)/shard_map/ppermute | solution.py:401
  44.6 0.0 copy-done
  44.6 1.3 %shard_map.87.sums_ref = f32[128,4096]{1,0:T(8,128)S(1)} custom-call(bf16[128,256]{1,0:T(8,128)(2,1)S(1)} %get-tuple-element.49.keep_ref, bf16[256,4096]{1,0:T(8,128)(2,1)S(1)} %copy-done), custom_call_target="tpu_custom_call" | custom-call | flops 300000000 | bytes 4000000 | tf_op jit(solution)/shard_map/pallas_call | solution.py:411
  45.9 2.5 %collective-permute-done.2.got_ref = bf16[128,256]{1,0:T(8,128)(2,1)S(1)} collective-permute-done((bf16[128,256]{1,0:T(8,128)(2,1)S(1)}, bf16[128,256]{1,0:T(8,128)(2,1)S(1)}, u32[]{:S(2)}, u32[]{:S(2)}) %collective-permute-start.2) | collective-permute-done | bytes 65568 | tf_op jit(solution)/shard_map/ppermute | solution.py:401
  48.4 0.0 collective-permute-done.3.across_ref
  48.4 1.6 %shard_map.88 = (bf16[16,4096]{1,0:T(8,128)(2,1)S(1)}, bf16[16,4096]{1,0:T(8,128)(2,1)S(1)}, bf16[16,4096]{1,0:T(8,128)(2,1)S(1)}, bf16[16,4096]{1,0:T(8,128)(2,...) custom-call(bf16[128,256]{1,0:T(8,128)(2,1)S(1)} %collective-permute, ...), custom_call_target="tpu_custom_call" | custom-call | flops 300000000 | bytes 6000000 | tf_op jit(solution)/shard_map/pallas_call | solution.py:420
  50.0 10.6 %collective-permute-start.4 = (bf16[16,4096]{1,0:T(8,128)(2,1)S(1)}, bf16[16,4096]{1,0:T(8,128)(2,1)S(1)}, u32[]{:S(2)}, u32[]{:S(2)}) collective-permute-start(bf16[16,4096]{1,0:T(8,128)(2,1)S(1)} %get-tuple-element.51), channel_id=1, source_target_pairs={{0,2},{1,15},{2,4},{3,1},{4,6},{5,3},{6,8},{7,5},{8,10},{9,7},{10,... | collective-permute-start | bytes 393224 | tf_op jit(solution)/shard_map/ppermute | solution.py:308
  60.6 1.9 %collective-permute-start.8 = (bf16[16,4096]{1,0:T(8,128)(2,1)S(1)}, bf16[16,4096]{1,0:T(8,128)(2,1)S(1)}, u32[]{:S(2)}, u32[]{:S(2)}) collective-permute-start(bf16[16,4096]{1,0:T(8,128)(2,1)S(1)} %get-tuple-element.56), channel_id=1, source_target_pairs={{0,14},{1,3},{2,0},{3,5},{4,2},{5,7},{6,4},{7,9},{8,6},{9,11},{10,... | collective-permute-start | bytes 393224 | tf_op jit(solution)/shard_map/ppermute | solution.py:308
  62.6 3.1 %collective-permute-done.4 = bf16[16,4096]{1,0:T(8,128)(2,1)S(1)} collective-permute-done((bf16[16,4096]{1,0:T(8,128)(2,1)S(1)}, bf16[16,4096]{1,0:T(8,128)(2,1)S(1)}, u32[]{:S(2)}, u32[]{:S(2)}) %collective-permute-start.4) | collective-permute-done | bytes 131104 | tf_op jit(solution)/shard_map/ppermute | solution.py:308
  65.7 6.6 %collective-permute-start.5 = (bf16[16,4096]{1,0:T(8,128)(2,1)S(1)}, bf16[16,4096]{1,0:T(8,128)(2,1)S(1)}, u32[]{:S(2)}, u32[]{:S(2)}) collective-permute-start(bf16[16,4096]{1,0:T(8,128)(2,1)S(1)} %add_convert_fusion.5), channel_id=1, source_target_pairs={{0,2},{1,15},{2,4},{3,1},{4,6},{5,3},{6,8},{7,5},{8,10},{9,7},{10,... | collective-permute-start | bytes 393224 | tf_op jit(solution)/shard_map/ppermute | solution.py:308
  72.2 0.0 collective-permute-done.8
  72.3 1.9 %collective-permute-start.9 = (bf16[16,4096]{1,0:T(8,128)(2,1)S(1)}, bf16[16,4096]{1,0:T(8,128)(2,1)S(1)}, u32[]{:S(2)}, u32[]{:S(2)}) collective-permute-start(bf16[16,4096]{1,0:T(8,128)(2,1)S(1)} %add_convert_fusion.2), channel_id=1, source_target_pairs={{0,14},{1,3},{2,0},{3,5},{4,2},{5,7},{6,4},{7,9},{8,6},{9,11},{10,... | collective-permute-start | bytes 393224 | tf_op jit(solution)/shard_map/ppermute | solution.py:308
  74.2 3.9 %collective-permute-done.5 = bf16[16,4096]{1,0:T(8,128)(2,1)S(1)} collective-permute-done((bf16[16,4096]{1,0:T(8,128)(2,1)S(1)}, bf16[16,4096]{1,0:T(8,128)(2,1)S(1)}, u32[]{:S(2)}, u32[]{:S(2)}) %collective-permute-start.5) | collective-permute-done | bytes 131104 | tf_op jit(solution)/shard_map/ppermute | solution.py:308
  78.1 6.6 %collective-permute-start.6 = (bf16[16,4096]{1,0:T(8,128)(2,1)S(1)}, bf16[16,4096]{1,0:T(8,128)(2,1)S(1)}, u32[]{:S(2)}, u32[]{:S(2)}) collective-permute-start(bf16[16,4096]{1,0:T(8,128)(2,1)S(1)} %add_convert_fusion.4), channel_id=1, source_target_pairs={{0,2},{1,15},{2,4},{3,1},{4,6},{5,3},{6,8},{7,5},{8,10},{9,7},{10,... | collective-permute-start | bytes 393224 | tf_op jit(solution)/shard_map/ppermute | solution.py:308
  84.7 0.0 collective-permute-done.9
  84.8 1.9 %collective-permute-start.10 = (bf16[16,4096]{1,0:T(8,128)(2,1)S(1)}, bf16[16,4096]{1,0:T(8,128)(2,1)S(1)}, u32[]{:S(2)}, u32[]{:S(2)}) collective-permute-start(bf16[16,4096]{1,0:T(8,128)(2,1)S(1)} %add_convert_fusion.1), channel_id=1, source_target_pairs={{0,14},{1,3},{2,0},{3,5},{4,2},{5,7},{6,4},{7,9},{8,6},{9,11},{10,... | collective-permute-start | bytes 393224 | tf_op jit(solution)/shard_map/ppermute | solution.py:308
  86.7 2.8 %collective-permute-done.6 = bf16[16,4096]{1,0:T(8,128)(2,1)S(1)} collective-permute-done((bf16[16,4096]{1,0:T(8,128)(2,1)S(1)}, bf16[16,4096]{1,0:T(8,128)(2,1)S(1)}, u32[]{:S(2)}, u32[]{:S(2)}) %collective-permute-start.6) | collective-permute-done | bytes 131104 | tf_op jit(solution)/shard_map/ppermute | solution.py:308
  89.6 6.6 %collective-permute-start.7 = (bf16[16,4096]{1,0:T(8,128)(2,1)S(1)}, bf16[16,4096]{1,0:T(8,128)(2,1)S(1)}, u32[]{:S(2)}, u32[]{:S(2)}) collective-permute-start(bf16[16,4096]{1,0:T(8,128)(2,1)S(1)} %add_convert_fusion.3), channel_id=1, source_target_pairs={{0,2},{1,15},{2,4},{3,1},{4,6},{5,3},{6,8},{7,5},{8,10},{9,7},{10,... | collective-permute-start | bytes 393224 | tf_op jit(solution)/shard_map/ppermute | solution.py:308
  96.1 0.0 collective-permute-done.10
  96.1 2.5 %collective-permute-done.7 = bf16[16,4096]{1,0:T(8,128)(2,1)S(1)} collective-permute-done((bf16[16,4096]{1,0:T(8,128)(2,1)S(1)}, bf16[16,4096]{1,0:T(8,128)(2,1)S(1)}, u32[]{:S(2)}, u32[]{:S(2)}) %collective-permute-start.7) | collective-permute-done | bytes 131104 | tf_op jit(solution)/shard_map/ppermute | solution.py:308
  98.6 0.7 add_convert_fusion
  (5 shorter events, 0.2 us)
Async XLA Ops:
  0.0 8.2 %copy-start.4 = (bf16[256,256]{1,0:T(8,128)(2,1)S(1)}, bf16[256,256]{1,0:T(8,128)(2,1)}, u32[]{:S(2)}) copy-start(bf16[256,256]{1,0:T(8,128)(2,1)} %k_ref.1) | copy-start | bytes 393220
  0.0 8.2 %copy-start.2 = (f32[2,8,256]{2,1,0:T(8,128)S(1)}, f32[2,8,256]{2,1,0:T(8,128)}, u32[]{:S(2)}) copy-start(f32[2,8,256]{2,1,0:T(8,128)} %refs_4_.1) | copy-start | bytes 49156
  0.0 8.2 %copy-start.3 = (bf16[256,256]{1,0:T(8,128)(2,1)S(1)}, bf16[256,256]{1,0:T(8,128)(2,1)}, u32[]{:S(2)}) copy-start(bf16[256,256]{1,0:T(8,128)(2,1)} %q_ref.1) | copy-start | bytes 393220
  4.3 35.8 %collective-permute-start.1 = (bf16[128,4096]{1,0:T(8,128)(2,1)S(1)}, bf16[128,4096]{1,0:T(8,128)(2,1)S(1)}, u32[]{:S(2)}, u32[]{:S(2)}) collective-permute-start(bf16[128,4096]{1,0:T(8,128)(2,1)S(1)} %get-tuple-element.47), channel_id=1, source_target_pairs={{0,1},{1,0},{2,3},{3,2},{4,5},{5,4},{6,7},{7,6},{8,9},{9,8},{10,11... | collective-permute-start | bytes 3145736 | tf_op jit(solution)/shard_map/ppermute | solution.py:366
  6.3 3.2 %collective-permute-start = (bf16[2,128,256]{2,1,0:T(8,128)(2,1)S(1)}, bf16[2,128,256]{2,1,0:T(8,128)(2,1)S(1)}, u32[]{:S(2)}, u32[]{:S(2)}) collective-permute-start(bf16[2,128,256]{2,1,0:T(8,128)(2,1)S(1)} %get-tuple-element.38.mine_ref), channel_id=1, source_target_pairs={{0,16},{16,0},{32,48},{48,32},{64,80},{80,64},{96,112},{112,96},{1... | collective-permute-start | bytes 393224 | tf_op jit(solution)/shard_map/ppermute | solution.py:365
  8.3 30.9 %copy-start.1 = (bf16[256,256]{1,0:T(8,128)(2,1)S(1)}, bf16[256,256]{1,0:T(8,128)(2,1)}, u32[]{:S(2)}) copy-start(bf16[256,256]{1,0:T(8,128)(2,1)} %refs_5_.1) | copy-start | bytes 393220
  9.4 35.2 %copy-start = (bf16[256,4096]{1,0:T(8,128)(2,1)S(1)}, bf16[256,4096]{1,0:T(8,128)(2,1)}, u32[]{:S(2)}) copy-start(bf16[256,4096]{1,0:T(8,128)(2,1)} %mine_ref.1) | copy-start | bytes 6291460
  40.1 8.3 %collective-permute-start.3 = (bf16[128,4096]{1,0:T(8,128)(2,1)S(1)}, bf16[128,4096]{1,0:T(8,128)(2,1)S(1)}, u32[]{:S(2)}, u32[]{:S(2)}) collective-permute-start(bf16[128,4096]{1,0:T(8,128)(2,1)S(1)} %collective-permute-done.1.direct_ref), channel_id=1, source_target_pairs={{0,16},{16,0},{32,48},{48,32},{64,80},{80,64},{96,112},{112,96},{1... | collective-permute-start | bytes 3145736 | tf_op jit(solution)/shard_map/ppermute | solution.py:402
  42.0 6.4 %collective-permute-start.2 = (bf16[128,256]{1,0:T(8,128)(2,1)S(1)}, bf16[128,256]{1,0:T(8,128)(2,1)S(1)}, u32[]{:S(2)}, u32[]{:S(2)}) collective-permute-start(bf16[128,256]{1,0:T(8,128)(2,1)S(1)} %get-tuple-element.48), channel_id=1, source_target_pairs={{0,1},{1,0},{2,3},{3,2},{4,5},{5,4},{6,7},{7,6},{8,9},{9,8},{10,11... | collective-permute-start | bytes 196616 | tf_op jit(solution)/shard_map/ppermute | solution.py:401
  50.0 15.6 %collective-permute-start.4 = (bf16[16,4096]{1,0:T(8,128)(2,1)S(1)}, bf16[16,4096]{1,0:T(8,128)(2,1)S(1)}, u32[]{:S(2)}, u32[]{:S(2)}) collective-permute-start(bf16[16,4096]{1,0:T(8,128)(2,1)S(1)} %get-tuple-element.51), channel_id=1, source_target_pairs={{0,2},{1,15},{2,4},{3,1},{4,6},{5,3},{6,8},{7,5},{8,10},{9,7},{10,... | collective-permute-start | bytes 393224 | tf_op jit(solution)/shard_map/ppermute | solution.py:308
  60.6 11.6 %collective-permute-start.8 = (bf16[16,4096]{1,0:T(8,128)(2,1)S(1)}, bf16[16,4096]{1,0:T(8,128)(2,1)S(1)}, u32[]{:S(2)}, u32[]{:S(2)}) collective-permute-start(bf16[16,4096]{1,0:T(8,128)(2,1)S(1)} %get-tuple-element.56), channel_id=1, source_target_pairs={{0,14},{1,3},{2,0},{3,5},{4,2},{5,7},{6,4},{7,9},{8,6},{9,11},{10,... | collective-permute-start | bytes 393224 | tf_op jit(solution)/shard_map/ppermute | solution.py:308
  65.7 12.4 %collective-permute-start.5 = (bf16[16,4096]{1,0:T(8,128)(2,1)S(1)}, bf16[16,4096]{1,0:T(8,128)(2,1)S(1)}, u32[]{:S(2)}, u32[]{:S(2)}) collective-permute-start(bf16[16,4096]{1,0:T(8,128)(2,1)S(1)} %add_convert_fusion.5), channel_id=1, source_target_pairs={{0,2},{1,15},{2,4},{3,1},{4,6},{5,3},{6,8},{7,5},{8,10},{9,7},{10,... | collective-permute-start | bytes 393224 | tf_op jit(solution)/shard_map/ppermute | solution.py:308
  72.3 12.4 %collective-permute-start.9 = (bf16[16,4096]{1,0:T(8,128)(2,1)S(1)}, bf16[16,4096]{1,0:T(8,128)(2,1)S(1)}, u32[]{:S(2)}, u32[]{:S(2)}) collective-permute-start(bf16[16,4096]{1,0:T(8,128)(2,1)S(1)} %add_convert_fusion.2), channel_id=1, source_target_pairs={{0,14},{1,3},{2,0},{3,5},{4,2},{5,7},{6,4},{7,9},{8,6},{9,11},{10,... | collective-permute-start | bytes 393224 | tf_op jit(solution)/shard_map/ppermute | solution.py:308
  78.1 11.4 %collective-permute-start.6 = (bf16[16,4096]{1,0:T(8,128)(2,1)S(1)}, bf16[16,4096]{1,0:T(8,128)(2,1)S(1)}, u32[]{:S(2)}, u32[]{:S(2)}) collective-permute-start(bf16[16,4096]{1,0:T(8,128)(2,1)S(1)} %add_convert_fusion.4), channel_id=1, source_target_pairs={{0,2},{1,15},{2,4},{3,1},{4,6},{5,3},{6,8},{7,5},{8,10},{9,7},{10,... | collective-permute-start | bytes 393224 | tf_op jit(solution)/shard_map/ppermute | solution.py:308
  84.8 11.4 %collective-permute-start.10 = (bf16[16,4096]{1,0:T(8,128)(2,1)S(1)}, bf16[16,4096]{1,0:T(8,128)(2,1)S(1)}, u32[]{:S(2)}, u32[]{:S(2)}) collective-permute-start(bf16[16,4096]{1,0:T(8,128)(2,1)S(1)} %add_convert_fusion.1), channel_id=1, source_target_pairs={{0,14},{1,3},{2,0},{3,5},{4,2},{5,7},{6,4},{7,9},{8,6},{9,11},{10,... | collective-permute-start | bytes 393224 | tf_op jit(solution)/shard_map/ppermute | solution.py:308
  89.6 9.1 %collective-permute-start.7 = (bf16[16,4096]{1,0:T(8,128)(2,1)S(1)}, bf16[16,4096]{1,0:T(8,128)(2,1)S(1)}, u32[]{:S(2)}, u32[]{:S(2)}) collective-permute-start(bf16[16,4096]{1,0:T(8,128)(2,1)S(1)} %add_convert_fusion.3), channel_id=1, source_target_pairs={{0,2},{1,15},{2,4},{3,1},{4,6},{5,3},{6,8},{7,5},{8,10},{9,7},{10,... | collective-permute-start | bytes 393224 | tf_op jit(solution)/shard_map/ppermute | solution.py:308

commit v6 on v5

--- a/solution.py
+++ b/solution.py
@@ -232,6 +232,10 @@
         total_ref[h] = joined(first, joined(four_ref[2, h], four_ref[3, h]))
 
 
+def hop_order(ring):
+    return [0, ring - 1] + list(range(1, ring - 1))
+
+
 def finish_kernel(outer, ring, core_ref, lift_ref, four_ref, before_ref, lw_ref, gate_ref, *rest):
     level_refs, keep_ref, give_ref, norm_ref = rest[:-3], rest[-3], rest[-2], rest[-1]
     digit = (lax.axis_index("seq") >> (outer - 2)) & 3
@@ -256,10 +260,10 @@
     pair = lax.axis_index("head") // 2
     parity = lax.rem(lax.axis_index("head"), 2)
     side = 1 - 2 * lax.rem(lax.axis_index("head") + lax.axis_index("seq"), 2)
-    for j in range(ring):
+    for n, j in enumerate(hop_order(ring)):
         kept = 2 * lax.rem(pair + ring + side * (ring // 2 - j), ring) + parity
         given = 2 * lax.rem(pair + ring - side * (ring // 2 - j), ring) + 1 - parity
-        rows = slice(j * chunk, (j + 1) * chunk)
+        rows = slice(n * chunk, (n + 1) * chunk)
         keep_ref[rows] = norm_ref[pl.ds(pl.multiple_of(kept * chunk, chunk), chunk)]
         give_ref[rows] = norm_ref[pl.ds(pl.multiple_of(given * chunk, chunk), chunk)]
 
@@ -268,14 +272,18 @@
     sums_ref[...] = dot(keep_ref[...], mine_ref[...])
 
 
-def project_kernel(got_ref, sums_ref, direct_ref, across_ref, *out_refs):
+def project_direct_kernel(got_ref, sums_ref, direct_ref, first_ref, others_ref):
     second = lax.rem(lax.axis_index("seq"), 2) == 1
-    one, two = got_ref[:, :DK], got_ref[:, DK:]
-    sums = (
-        sums_ref[...]
-        + dot(jnp.where(second, two, one), direct_ref[...])
-        + dot(jnp.where(second, one, two), across_ref[...])
-    )
+    sums = sums_ref[...] + dot(jnp.where(second, got_ref[:, DK:], got_ref[:, :DK]), direct_ref[...])
+    count = first_ref.shape[0]
+    first_ref[...] = sums[:count]
+    others_ref[...] = sums[count:]
+
+
+def project_kernel(start, got_ref, sums_ref, across_ref, *out_refs):
+    second = lax.rem(lax.axis_index("seq"), 2) == 1
+    rows = slice(start, start + sums_ref.shape[0])
+    sums = sums_ref[...] + dot(jnp.where(second, got_ref[rows, :DK], got_ref[rows, DK:]), across_ref[...])
     chunk = out_refs[0].shape[0]
     for j, out_ref in enumerate(out_refs):
         out_ref[...] = sums[j * chunk : (j + 1) * chunk].astype(BF16)
@@ -397,35 +405,54 @@
         1_000_000,
         [pltpu.VMEM((tokens, wide), BF16)],
     )(core, lifted, four, before, level_weight, gate, *collected)
-    give, direct = lax.optimization_barrier((give, direct))
     got = lax.ppermute(give, "head", pairs)
-    across = lax.ppermute(direct, "seq", cores)
     columns = w_out.shape[1]
     step = columns // 4
     chunk = tokens // ring
+    count = ring // 2
+    lead = 2 * chunk
+    rest = tokens // 2 - lead
 
     def by_columns(rows):
         return pl.BlockSpec((rows, step), lambda c: (0, c))
 
     whole = pl.BlockSpec((tokens // 2, wide), lambda c: (0, 0))
-    sums = pl.pallas_call(
-        project_own_kernel,
-        grid=(columns // step,),
-        out_shape=shape((tokens // 2, columns), F32),
-        in_specs=[whole, by_columns(wide)],
-        out_specs=by_columns(tokens // 2),
-        compiler_params=pltpu.CompilerParams(vmem_limit_bytes=16 << 20),
-        cost_estimate=pl.CostEstimate(flops=300_000_000, bytes_accessed=4_000_000, transcendentals=0),
+
+    def project(body, out_shape, in_specs, flops):
+        return pl.pallas_call(
+            body,
+            grid=(columns // step,),
+            out_shape=out_shape,
+            in_specs=in_specs,
+            out_specs=[by_columns(out.shape[0]) for out in out_shape],
+            compiler_params=pltpu.CompilerParams(vmem_limit_bytes=16 << 20),
+            cost_estimate=pl.CostEstimate(flops=flops, bytes_accessed=4_000_000, transcendentals=0),
+        )
+
+    (sums,) = project(
+        project_own_kernel, [shape((tokens // 2, columns), F32)], [whole, by_columns(wide)], 300_000_000
     )(keep, w_out)
-    terms = pl.pallas_call(
-        project_kernel,
-        grid=(columns // step,),
-        out_shape=[shape((chunk, columns))] * (ring // 2),
-        in_specs=[whole, by_columns(tokens // 2), by_columns(DK), by_columns(DK)],
-        out_specs=[by_columns(chunk)] * (ring // 2),
-        compiler_params=pltpu.CompilerParams(vmem_limit_bytes=16 << 20),
-        cost_estimate=pl.CostEstimate(flops=300_000_000, bytes_accessed=6_000_000, transcendentals=0),
-    )(got, sums, direct, across)
+    got, direct, sums = lax.optimization_barrier((got, direct, sums))
+    across = lax.ppermute(direct, "seq", cores)
+    first, others = project(
+        project_direct_kernel,
+        [shape((lead, columns), F32), shape((rest, columns), F32)],
+        [whole, by_columns(tokens // 2), by_columns(DK)],
+        150_000_000,
+    )(got, sums, direct)
+    ends = project(
+        lambda *refs: project_kernel(0, *refs),
+        [shape((chunk, columns))] * 2,
+        [whole, by_columns(lead), by_columns(DK)],
+        40_000_000,
+    )(got, first, across)
+    middle = project(
+        lambda *refs: project_kernel(lead, *refs),
+        [shape((chunk, columns))] * (count - 2),
+        [whole, by_columns(rest), by_columns(DK)],
+        120_000_000,
+    )(got, others, across) if count > 2 else []
+    terms = [ends[0], *middle, ends[1]]
     return ring_sum(terms)
 
 

time: 99.8 us -> 101 us (1.012)
  the two profiles are of different devices: /device:TPU:34 before, /device:TPU:38 now
where the time goes in v6:
time: 101 us
  starting transfers between devices  44.2 us (44%)
  blocking collectives  28.8 us (29%)
  waiting for transfers between devices  14.9 us (15%)
  Pallas kernels  11.7 us (12%)
    ppermute x7, starting transfers between devices, hop(): return lax.ppermute(block, ('seq', 'head'), route).astype(F32)  35.9 us
    all_gather x2, blocking collectives, gathered(): return lax.all_gather(total, 'seq', axis=0, axis_index_groups=groups)  28.8 us
    ppermute x7, waiting for transfers between devices, hop(): return lax.ppermute(block, ('seq', 'head'), route).astype(F32)  11 us
    pallas_call x1, Pallas kernels, on_device(): call(states_kernel, (shape((heads, DK, 2 * DK)), shape((heads, 4, DK, 2 *...  4.25 us
    ppermute x1, waiting for transfers between devices, on_device(): got = lax.ppermute(give, 'head', pairs)  2.47 us
    ppermute x1, starting transfers between devices, on_device(): got = lax.ppermute(give, 'head', pairs)  2.42 us
  transfers between devices with their start and end apart: 11, of which 7 were waited for; matrix products, arithmetic and copies ran while one was open for 0% of the time, Pallas kernels for 6%

profile of v6, /device:TPU:38, one launch (start us, length us, event | category | flops | bytes accessed | tf_op | source)
XLA Modules:
  0.0 100.7 jit_solution(11311669013916945644)
XLA Ops:
  0.0 0.0 copy-start.4
  0.0 0.0 copy-start.2
  0.0 0.0 copy-start.3
  0.0 4.3 %shard_map.82 = (bf16[2,128,256]{2,1,0:T(8,128)(2,1)S(1)}, bf16[2,4,128,256]{3,2,1,0:T(8,128)(2,1)S(1)}, f32[256,256]{1,0:T(8,128)S(1)}, f32[256,256]{1,0:T(8,12...) custom-call(bf16[256,256]{1,0:T(8,128)(2,1)} %k_ref.1, bf16[256,256]{1,0:T(8,128)(2,1)} %v_in.1, ...), custom_call_target="tpu_custom_call" | custom-call | flops 2000000000 | bytes 1000000 | tf_op jit(solution)/shard_map/pallas_call | solution.py:340
  4.3 2.0 %collective-permute-start.2 = (bf16[128,4096]{1,0:T(8,128)(2,1)S(1)}, bf16[128,4096]{1,0:T(8,128)(2,1)S(1)}, u32[]{:S(2)}, u32[]{:S(2)}) collective-permute-start(bf16[128,4096]{1,0:T(8,128)(2,1)S(1)} %get-tuple-element.50), channel_id=1, source_target_pairs={{0,1},{1,0},{2,3},{3,2},{4,5},{5,4},{6,7},{7,6},{8,9},{9,8},{10,11... | collective-permute-start | bytes 3145736 | tf_op jit(solution)/shard_map/ppermute | solution.py:374
  6.3 1.9 %collective-permute-start = (bf16[2,128,256]{2,1,0:T(8,128)(2,1)S(1)}, bf16[2,128,256]{2,1,0:T(8,128)(2,1)S(1)}, u32[]{:S(2)}, u32[]{:S(2)}) collective-permute-start(bf16[2,128,256]{2,1,0:T(8,128)(2,1)S(1)} %get-tuple-element.41.mine_ref), channel_id=1, source_target_pairs={{0,16},{16,0},{32,48},{48,32},{64,80},{80,64},{96,112},{112,96},{1... | collective-permute-start | bytes 393224 | tf_op jit(solution)/shard_map/ppermute | solution.py:373
  8.2 0.0 copy-done.4
  8.2 0.0 copy-done.2
  8.2 0.0 copy-done.3
  8.3 0.0 copy-start.1
  8.3 1.2 %shard_map.83 = (f32[256,256]{1,0:T(8,128)S(1)}, bf16[256,256]{1,0:T(8,128)(2,1)S(1)}) custom-call(bf16[256,256]{1,0:T(8,128)(2,1)S(1)} %copy-done.3, bf16[256,256]{1,0:T(8,128)(2,1)S(1)} %copy-done.4, f32[256,256]{1,0:T(8,128)S(1)} %get-tuple-element.35.w_ref, f32[256,256]{1,0:T(8,128)S(1)} %get-tuple-element.36.u_ref, ...), custom_call_target="tpu_custom_call" | custom-call | flops 1000000000 | bytes 1000000 | tf_op jit(solution)/shard_map/pallas_call | solution.py:364
  9.4 0.0 copy-start
  9.4 0.1 collective-permute-done.theirs_ref
  9.5 0.2 shard_map.84
  9.7 16.0 %all-gather = bf16[8,128,256]{2,1,0:T(8,128)(2,1)S(1)} all-gather(bf16[2,128,256]{2,1,0:T(8,128)(2,1)S(1)} %get-tuple-element.42), channel_id=2, replica_groups={{0,32,64,96},{16,48,80,112},{128,160,192,224},{144,176,208,240},{256,28..., dimensions={0}, use_global_device_ids=true | all-gather | bytes 655360 | tf_op jit(solution)/shard_map/all_gather | solution.py:388
  25.7 0.6 shard_map.85
  26.3 12.8 %all-gather.1 = bf16[8,128,256]{2,1,0:T(8,128)(2,1)S(1)} all-gather(bf16[2,128,256]{2,1,0:T(8,128)(2,1)S(1)} %get-tuple-element.44), channel_id=3, replica_groups={{0,128,256,384},{16,144,272,400},{32,160,288,416},{48,176,304,432},{64,..., dimensions={0}, use_global_device_ids=true | all-gather | bytes 655360 | tf_op jit(solution)/shard_map/all_gather | solution.py:388
  39.1 0.0 copy-done.1
  39.1 0.9 shard_map.86
  40.0 2.4 %collective-permute-start.1 = (bf16[128,256]{1,0:T(8,128)(2,1)S(1)}, bf16[128,256]{1,0:T(8,128)(2,1)S(1)}, u32[]{:S(2)}, u32[]{:S(2)}) collective-permute-start(bf16[128,256]{1,0:T(8,128)(2,1)S(1)} %get-tuple-element.49), channel_id=1, source_target_pairs={{0,1},{1,0},{2,3},{3,2},{4,5},{5,4},{6,7},{7,6},{8,9},{9,8},{10,11... | collective-permute-start | bytes 196616 | tf_op jit(solution)/shard_map/ppermute | solution.py:408
  42.5 0.0 copy-done
  42.5 1.3 %shard_map.87.sums_ref = f32[128,4096]{1,0:T(8,128)S(1)} custom-call(bf16[128,256]{1,0:T(8,128)(2,1)S(1)} %get-tuple-element.51.keep_ref, bf16[256,4096]{1,0:T(8,128)(2,1)S(1)} %copy-done), custom_call_target="tpu_custom_call" | custom-call | flops 300000000 | bytes 4000000 | tf_op jit(solution)/shard_map/pallas_call | solution.py:432
  43.7 2.5 %collective-permute-done.1.got_ref.refs_0_ = bf16[128,256]{1,0:T(8,128)(2,1)S(1)} collective-permute-done((bf16[128,256]{1,0:T(8,128)(2,1)S(1)}, bf16[128,256]{1,0:T(8,128)(2,1)S(1)}, u32[]{:S(2)}, u32[]{:S(2)}) %collective-permute-start.1) | collective-permute-done | bytes 65568 | tf_op jit(solution)/shard_map/ppermute | solution.py:408
  46.2 0.0 collective-permute-done.2.direct_ref
  46.2 1.9 %collective-permute-start.3 = (bf16[128,4096]{1,0:T(8,128)(2,1)S(1)}, bf16[128,4096]{1,0:T(8,128)(2,1)S(1)}, u32[]{:S(2)}, u32[]{:S(2)}) collective-permute-start(bf16[128,4096]{1,0:T(8,128)(2,1)S(1)} %collective-permute-done.2.direct_ref), channel_id=1, source_target_pairs={{0,16},{16,0},{32,48},{48,32},{64,80},{80,64},{96,112},{112,96},{1... | collective-permute-start | bytes 3145736 | tf_op jit(solution)/shard_map/ppermute | solution.py:436
  48.1 1.3 %shard_map.88 = (f32[32,4096]{1,0:T(8,128)S(1)}, f32[96,4096]{1,0:T(8,128)S(1)}) custom-call(bf16[128,256]{1,0:T(8,128)(2,1)S(1)} %collective-permute-done.1.got_ref.refs_0_, f32[128,4096]{1,0:T(8,128)S(1)} %shard_map.87.sums_ref, bf16[128,4096]{1,0:T(8,128)(2,1)S(1)} %collective-permute-done.2.direct_ref), custom_call_target="tpu_custom_call" | custom-call | flops 150000000 | bytes 4000000 | tf_op jit(solution)/shard_map/pallas_call | solution.py:437
  49.4 1.3 %collective-permute-done.3.refs_2_ = bf16[128,4096]{1,0:T(8,128)(2,1)S(1)} collective-permute-done((bf16[128,4096]{1,0:T(8,128)(2,1)S(1)}, bf16[128,4096]{1,0:T(8,128)(2,1)S(1)}, u32[]{:S(2)}, u32[]{:S(2)}) %collective-permute-start.3) | collective-permute-done | bytes 1048608 | tf_op jit(solution)/shard_map/ppermute | solution.py:436
  50.7 0.9 shard_map.89
  51.6 10.4 %collective-permute-start.4 = (bf16[16,4096]{1,0:T(8,128)(2,1)S(1)}, bf16[16,4096]{1,0:T(8,128)(2,1)S(1)}, u32[]{:S(2)}, u32[]{:S(2)}) collective-permute-start(bf16[16,4096]{1,0:T(8,128)(2,1)S(1)} %get-tuple-element.56), channel_id=1, source_target_pairs={{0,2},{1,15},{2,4},{3,1},{4,6},{5,3},{6,8},{7,5},{8,10},{9,7},{10,... | collective-permute-start | bytes 393224 | tf_op jit(solution)/shard_map/ppermute | solution.py:316
  62.1 1.9 %collective-permute-start.8 = (bf16[16,4096]{1,0:T(8,128)(2,1)S(1)}, bf16[16,4096]{1,0:T(8,128)(2,1)S(1)}, u32[]{:S(2)}, u32[]{:S(2)}) collective-permute-start(bf16[16,4096]{1,0:T(8,128)(2,1)S(1)} %get-tuple-element.62), channel_id=1, source_target_pairs={{0,14},{1,3},{2,0},{3,5},{4,2},{5,7},{6,4},{7,9},{8,6},{9,11},{10,... | collective-permute-start | bytes 393224 | tf_op jit(solution)/shard_map/ppermute | solution.py:316
  64.0 1.1 %shard_map.90 = (bf16[16,4096]{1,0:T(8,128)(2,1)S(1)}, bf16[16,4096]{1,0:T(8,128)(2,1)S(1)}, bf16[16,4096]{1,0:T(8,128)(2,1)S(1)}, bf16[16,4096]{1,0:T(8,128)(2,...) custom-call(bf16[128,256]{1,0:T(8,128)(2,1)S(1)} %collective-permute-done.1.got_ref.refs_0_, ...), custom_call_target="tpu_custom_call" | custom-call | flops 120000000 | bytes 4000000 | tf_op jit(solution)/shard_map/pallas_call | solution.py:449
  65.1 1.2 %collective-permute-done.4 = bf16[16,4096]{1,0:T(8,128)(2,1)S(1)} collective-permute-done((bf16[16,4096]{1,0:T(8,128)(2,1)S(1)}, bf16[16,4096]{1,0:T(8,128)(2,1)S(1)}, u32[]{:S(2)}, u32[]{:S(2)}) %collective-permute-start.4) | collective-permute-done | bytes 131104 | tf_op jit(solution)/shard_map/ppermute | solution.py:316
  66.4 6.6 %collective-permute-start.5 = (bf16[16,4096]{1,0:T(8,128)(2,1)S(1)}, bf16[16,4096]{1,0:T(8,128)(2,1)S(1)}, u32[]{:S(2)}, u32[]{:S(2)}) collective-permute-start(bf16[16,4096]{1,0:T(8,128)(2,1)S(1)} %add_convert_fusion.5), channel_id=1, source_target_pairs={{0,2},{1,15},{2,4},{3,1},{4,6},{5,3},{6,8},{7,5},{8,10},{9,7},{10,... | collective-permute-start | bytes 393224 | tf_op jit(solution)/shard_map/ppermute | solution.py:316
  73.0 0.0 collective-permute-done.8
  73.1 1.9 %collective-permute-start.9 = (bf16[16,4096]{1,0:T(8,128)(2,1)S(1)}, bf16[16,4096]{1,0:T(8,128)(2,1)S(1)}, u32[]{:S(2)}, u32[]{:S(2)}) collective-permute-start(bf16[16,4096]{1,0:T(8,128)(2,1)S(1)} %add_convert_fusion.2), channel_id=1, source_target_pairs={{0,14},{1,3},{2,0},{3,5},{4,2},{5,7},{6,4},{7,9},{8,6},{9,11},{10,... | collective-permute-start | bytes 393224 | tf_op jit(solution)/shard_map/ppermute | solution.py:316
  75.0 4.5 %collective-permute-done.5 = bf16[16,4096]{1,0:T(8,128)(2,1)S(1)} collective-permute-done((bf16[16,4096]{1,0:T(8,128)(2,1)S(1)}, bf16[16,4096]{1,0:T(8,128)(2,1)S(1)}, u32[]{:S(2)}, u32[]{:S(2)}) %collective-permute-start.5) | collective-permute-done | bytes 131104 | tf_op jit(solution)/shard_map/ppermute | solution.py:316
  79.5 6.6 %collective-permute-start.6 = (bf16[16,4096]{1,0:T(8,128)(2,1)S(1)}, bf16[16,4096]{1,0:T(8,128)(2,1)S(1)}, u32[]{:S(2)}, u32[]{:S(2)}) collective-permute-start(bf16[16,4096]{1,0:T(8,128)(2,1)S(1)} %add_convert_fusion.4), channel_id=1, source_target_pairs={{0,2},{1,15},{2,4},{3,1},{4,6},{5,3},{6,8},{7,5},{8,10},{9,7},{10,... | collective-permute-start | bytes 393224 | tf_op jit(solution)/shard_map/ppermute | solution.py:316
  86.1 0.0 collective-permute-done.9
  86.1 1.9 %collective-permute-start.10 = (bf16[16,4096]{1,0:T(8,128)(2,1)S(1)}, bf16[16,4096]{1,0:T(8,128)(2,1)S(1)}, u32[]{:S(2)}, u32[]{:S(2)}) collective-permute-start(bf16[16,4096]{1,0:T(8,128)(2,1)S(1)} %add_convert_fusion.1), channel_id=1, source_target_pairs={{0,14},{1,3},{2,0},{3,5},{4,2},{5,7},{6,4},{7,9},{8,6},{9,11},{10,... | collective-permute-start | bytes 393224 | tf_op jit(solution)/shard_map/ppermute | solution.py:316
  88.0 2.9 %collective-permute-done.6 = bf16[16,4096]{1,0:T(8,128)(2,1)S(1)} collective-permute-done((bf16[16,4096]{1,0:T(8,128)(2,1)S(1)}, bf16[16,4096]{1,0:T(8,128)(2,1)S(1)}, u32[]{:S(2)}, u32[]{:S(2)}) %collective-permute-start.6) | collective-permute-done | bytes 131104 | tf_op jit(solution)/shard_map/ppermute | solution.py:316
  90.9 6.6 %collective-permute-start.7 = (bf16[16,4096]{1,0:T(8,128)(2,1)S(1)}, bf16[16,4096]{1,0:T(8,128)(2,1)S(1)}, u32[]{:S(2)}, u32[]{:S(2)}) collective-permute-start(bf16[16,4096]{1,0:T(8,128)(2,1)S(1)} %add_convert_fusion.3), channel_id=1, source_target_pairs={{0,2},{1,15},{2,4},{3,1},{4,6},{5,3},{6,8},{7,5},{8,10},{9,7},{10,... | collective-permute-start | bytes 393224 | tf_op jit(solution)/shard_map/ppermute | solution.py:316
  97.5 0.0 collective-permute-done.10
  97.5 2.5 %collective-permute-done.7 = bf16[16,4096]{1,0:T(8,128)(2,1)S(1)} collective-permute-done((bf16[16,4096]{1,0:T(8,128)(2,1)S(1)}, bf16[16,4096]{1,0:T(8,128)(2,1)S(1)}, u32[]{:S(2)}, u32[]{:S(2)}) %collective-permute-start.7) | collective-permute-done | bytes 131104 | tf_op jit(solution)/shard_map/ppermute | solution.py:316
  100.0 0.7 add_convert_fusion
  (5 shorter events, 0.2 us)
Async XLA Ops:
  0.0 8.2 %copy-start.4 = (bf16[256,256]{1,0:T(8,128)(2,1)S(1)}, bf16[256,256]{1,0:T(8,128)(2,1)}, u32[]{:S(2)}) copy-start(bf16[256,256]{1,0:T(8,128)(2,1)} %k_ref.1) | copy-start | bytes 393220
  0.0 8.2 %copy-start.2 = (f32[2,8,256]{2,1,0:T(8,128)S(1)}, f32[2,8,256]{2,1,0:T(8,128)}, u32[]{:S(2)}) copy-start(f32[2,8,256]{2,1,0:T(8,128)} %refs_4_.1) | copy-start | bytes 49156
  0.0 8.2 %copy-start.3 = (bf16[256,256]{1,0:T(8,128)(2,1)S(1)}, bf16[256,256]{1,0:T(8,128)(2,1)}, u32[]{:S(2)}) copy-start(bf16[256,256]{1,0:T(8,128)(2,1)} %q_ref.1) | copy-start | bytes 393220
  4.3 41.9 %collective-permute-start.2 = (bf16[128,4096]{1,0:T(8,128)(2,1)S(1)}, bf16[128,4096]{1,0:T(8,128)(2,1)S(1)}, u32[]{:S(2)}, u32[]{:S(2)}) collective-permute-start(bf16[128,4096]{1,0:T(8,128)(2,1)S(1)} %get-tuple-element.50), channel_id=1, source_target_pairs={{0,1},{1,0},{2,3},{3,2},{4,5},{5,4},{6,7},{7,6},{8,9},{9,8},{10,11... | collective-permute-start | bytes 3145736 | tf_op jit(solution)/shard_map/ppermute | solution.py:374
  6.3 3.2 %collective-permute-start = (bf16[2,128,256]{2,1,0:T(8,128)(2,1)S(1)}, bf16[2,128,256]{2,1,0:T(8,128)(2,1)S(1)}, u32[]{:S(2)}, u32[]{:S(2)}) collective-permute-start(bf16[2,128,256]{2,1,0:T(8,128)(2,1)S(1)} %get-tuple-element.41.mine_ref), channel_id=1, source_target_pairs={{0,16},{16,0},{32,48},{48,32},{64,80},{80,64},{96,112},{112,96},{1... | collective-permute-start | bytes 393224 | tf_op jit(solution)/shard_map/ppermute | solution.py:373
  8.3 30.8 %copy-start.1 = (bf16[256,256]{1,0:T(8,128)(2,1)S(1)}, bf16[256,256]{1,0:T(8,128)(2,1)}, u32[]{:S(2)}) copy-start(bf16[256,256]{1,0:T(8,128)(2,1)} %refs_5_.1) | copy-start | bytes 393220
  9.4 33.0 %copy-start = (bf16[256,4096]{1,0:T(8,128)(2,1)S(1)}, bf16[256,4096]{1,0:T(8,128)(2,1)}, u32[]{:S(2)}) copy-start(bf16[256,4096]{1,0:T(8,128)(2,1)} %mine_ref.1) | copy-start | bytes 6291460
  40.0 6.2 %collective-permute-start.1 = (bf16[128,256]{1,0:T(8,128)(2,1)S(1)}, bf16[128,256]{1,0:T(8,128)(2,1)S(1)}, u32[]{:S(2)}, u32[]{:S(2)}) collective-permute-start(bf16[128,256]{1,0:T(8,128)(2,1)S(1)} %get-tuple-element.49), channel_id=1, source_target_pairs={{0,1},{1,0},{2,3},{3,2},{4,5},{5,4},{6,7},{7,6},{8,9},{9,8},{10,11... | collective-permute-start | bytes 196616 | tf_op jit(solution)/shard_map/ppermute | solution.py:408
  46.2 4.5 %collective-permute-start.3 = (bf16[128,4096]{1,0:T(8,128)(2,1)S(1)}, bf16[128,4096]{1,0:T(8,128)(2,1)S(1)}, u32[]{:S(2)}, u32[]{:S(2)}) collective-permute-start(bf16[128,4096]{1,0:T(8,128)(2,1)S(1)} %collective-permute-done.2.direct_ref), channel_id=1, source_target_pairs={{0,16},{16,0},{32,48},{48,32},{64,80},{80,64},{96,112},{112,96},{1... | collective-permute-start | bytes 3145736 | tf_op jit(solution)/shard_map/ppermute | solution.py:436
  51.6 14.7 %collective-permute-start.4 = (bf16[16,4096]{1,0:T(8,128)(2,1)S(1)}, bf16[16,4096]{1,0:T(8,128)(2,1)S(1)}, u32[]{:S(2)}, u32[]{:S(2)}) collective-permute-start(bf16[16,4096]{1,0:T(8,128)(2,1)S(1)} %get-tuple-element.56), channel_id=1, source_target_pairs={{0,2},{1,15},{2,4},{3,1},{4,6},{5,3},{6,8},{7,5},{8,10},{9,7},{10,... | collective-permute-start | bytes 393224 | tf_op jit(solution)/shard_map/ppermute | solution.py:316
  62.1 10.9 %collective-permute-start.8 = (bf16[16,4096]{1,0:T(8,128)(2,1)S(1)}, bf16[16,4096]{1,0:T(8,128)(2,1)S(1)}, u32[]{:S(2)}, u32[]{:S(2)}) collective-permute-start(bf16[16,4096]{1,0:T(8,128)(2,1)S(1)} %get-tuple-element.62), channel_id=1, source_target_pairs={{0,14},{1,3},{2,0},{3,5},{4,2},{5,7},{6,4},{7,9},{8,6},{9,11},{10,... | collective-permute-start | bytes 393224 | tf_op jit(solution)/shard_map/ppermute | solution.py:316
  66.4 13.0 %collective-permute-start.5 = (bf16[16,4096]{1,0:T(8,128)(2,1)S(1)}, bf16[16,4096]{1,0:T(8,128)(2,1)S(1)}, u32[]{:S(2)}, u32[]{:S(2)}) collective-permute-start(bf16[16,4096]{1,0:T(8,128)(2,1)S(1)} %add_convert_fusion.5), channel_id=1, source_target_pairs={{0,2},{1,15},{2,4},{3,1},{4,6},{5,3},{6,8},{7,5},{8,10},{9,7},{10,... | collective-permute-start | bytes 393224 | tf_op jit(solution)/shard_map/ppermute | solution.py:316
  73.1 13.0 %collective-permute-start.9 = (bf16[16,4096]{1,0:T(8,128)(2,1)S(1)}, bf16[16,4096]{1,0:T(8,128)(2,1)S(1)}, u32[]{:S(2)}, u32[]{:S(2)}) collective-permute-start(bf16[16,4096]{1,0:T(8,128)(2,1)S(1)} %add_convert_fusion.2), channel_id=1, source_target_pairs={{0,14},{1,3},{2,0},{3,5},{4,2},{5,7},{6,4},{7,9},{8,6},{9,11},{10,... | collective-permute-start | bytes 393224 | tf_op jit(solution)/shard_map/ppermute | solution.py:316
  79.5 11.4 %collective-permute-start.6 = (bf16[16,4096]{1,0:T(8,128)(2,1)S(1)}, bf16[16,4096]{1,0:T(8,128)(2,1)S(1)}, u32[]{:S(2)}, u32[]{:S(2)}) collective-permute-start(bf16[16,4096]{1,0:T(8,128)(2,1)S(1)} %add_convert_fusion.4), channel_id=1, source_target_pairs={{0,2},{1,15},{2,4},{3,1},{4,6},{5,3},{6,8},{7,5},{8,10},{9,7},{10,... | collective-permute-start | bytes 393224 | tf_op jit(solution)/shard_map/ppermute | solution.py:316
  86.1 11.4 %collective-permute-start.10 = (bf16[16,4096]{1,0:T(8,128)(2,1)S(1)}, bf16[16,4096]{1,0:T(8,128)(2,1)S(1)}, u32[]{:S(2)}, u32[]{:S(2)}) collective-permute-start(bf16[16,4096]{1,0:T(8,128)(2,1)S(1)} %add_convert_fusion.1), channel_id=1, source_target_pairs={{0,14},{1,3},{2,0},{3,5},{4,2},{5,7},{6,4},{7,9},{8,6},{9,11},{10,... | collective-permute-start | bytes 393224 | tf_op jit(solution)/shard_map/ppermute | solution.py:316
  90.9 9.1 %collective-permute-start.7 = (bf16[16,4096]{1,0:T(8,128)(2,1)S(1)}, bf16[16,4096]{1,0:T(8,128)(2,1)S(1)}, u32[]{:S(2)}, u32[]{:S(2)}) collective-permute-start(bf16[16,4096]{1,0:T(8,128)(2,1)S(1)} %add_convert_fusion.3), channel_id=1, source_target_pairs={{0,2},{1,15},{2,4},{3,1},{4,6},{5,3},{6,8},{7,5},{8,10},{9,7},{10,... | collective-permute-start | bytes 393224 | tf_op jit(solution)/shard_map/ppermute | solution.py:316

commit v7 on v6

--- a/solution.py
+++ b/solution.py
@@ -268,22 +268,22 @@
         give_ref[rows] = norm_ref[pl.ds(pl.multiple_of(given * chunk, chunk), chunk)]
 
 
-def project_own_kernel(keep_ref, mine_ref, sums_ref):
-    sums_ref[...] = dot(keep_ref[...], mine_ref[...])
-
-
-def project_direct_kernel(got_ref, sums_ref, direct_ref, first_ref, others_ref):
-    second = lax.rem(lax.axis_index("seq"), 2) == 1
-    sums = sums_ref[...] + dot(jnp.where(second, got_ref[:, DK:], got_ref[:, :DK]), direct_ref[...])
+def project_own_kernel(keep_ref, mine_ref, first_ref, others_ref):
+    sums = dot(keep_ref[...], mine_ref[...])
     count = first_ref.shape[0]
     first_ref[...] = sums[:count]
     others_ref[...] = sums[count:]
 
 
-def project_kernel(start, got_ref, sums_ref, across_ref, *out_refs):
+def project_kernel(start, got_ref, sums_ref, direct_ref, across_ref, *out_refs):
     second = lax.rem(lax.axis_index("seq"), 2) == 1
     rows = slice(start, start + sums_ref.shape[0])
-    sums = sums_ref[...] + dot(jnp.where(second, got_ref[rows, :DK], got_ref[rows, DK:]), across_ref[...])
+    one, two = got_ref[rows, :DK], got_ref[rows, DK:]
+    sums = (
+        sums_ref[...]
+        + dot(jnp.where(second, two, one), direct_ref[...])
+        + dot(jnp.where(second, one, two), across_ref[...])
+    )
     chunk = out_refs[0].shape[0]
     for j, out_ref in enumerate(out_refs):
         out_ref[...] = sums[j * chunk : (j + 1) * chunk].astype(BF16)
@@ -405,7 +405,9 @@
         1_000_000,
         [pltpu.VMEM((tokens, wide), BF16)],
     )(core, lifted, four, before, level_weight, gate, *collected)
+    give, direct = lax.optimization_barrier((give, direct))
     got = lax.ppermute(give, "head", pairs)
+    across = lax.ppermute(direct, "seq", cores)
     columns = w_out.shape[1]
     step = columns // 4
     chunk = tokens // ring
@@ -429,29 +431,24 @@
             cost_estimate=pl.CostEstimate(flops=flops, bytes_accessed=4_000_000, transcendentals=0),
         )
 
-    (sums,) = project(
-        project_own_kernel, [shape((tokens // 2, columns), F32)], [whole, by_columns(wide)], 300_000_000
+    first, others = project(
+        project_own_kernel,
+        [shape((lead, columns), F32), shape((rest, columns), F32)],
+        [whole, by_columns(wide)],
+        300_000_000,
     )(keep, w_out)
-    got, direct, sums = lax.optimization_barrier((got, direct, sums))
-    across = lax.ppermute(direct, "seq", cores)
-    first, others = project(
-        project_direct_kernel,
-        [shape((lead, columns), F32), shape((rest, columns), F32)],
-        [whole, by_columns(tokens // 2), by_columns(DK)],
-        150_000_000,
-    )(got, sums, direct)
     ends = project(
         lambda *refs: project_kernel(0, *refs),
         [shape((chunk, columns))] * 2,
-        [whole, by_columns(lead), by_columns(DK)],
-        40_000_000,
-    )(got, first, across)
+        [whole, by_columns(lead), by_columns(DK), by_columns(DK)],
+        80_000_000,
+    )(got, first, direct, across)
     middle = project(
         lambda *refs: project_kernel(lead, *refs),
         [shape((chunk, columns))] * (count - 2),
-        [whole, by_columns(rest), by_columns(DK)],
-        120_000_000,
-    )(got, others, across) if count > 2 else []
+        [whole, by_columns(rest), by_columns(DK), by_columns(DK)],
+        240_000_000,
+    )(got, others, direct, across) if count > 2 else []
     terms = [ends[0], *middle, ends[1]]
     return ring_sum(terms)
 

time: 101 us -> 99.2 us (0.982)
  the two profiles are of different devices: /device:TPU:38 before, /device:TPU:34 now
where the time goes in v7:
time: 99.2 us; the launch traced here: 98.7 us
  starting transfers between devices  44.5 us (45%)
  blocking collectives  28.8 us (29%)
  waiting for transfers between devices  13.3 us (13%)
  Pallas kernels  11 us (11%)
    ppermute x7, starting transfers between devices, hop(): return lax.ppermute(block, ('seq', 'head'), route).astype(F32)  36.1 us
    all_gather x2, blocking collectives, gathered(): return lax.all_gather(total, 'seq', axis=0, axis_index_groups=groups)  28.8 us
    ppermute x7, waiting for transfers between devices, hop(): return lax.ppermute(block, ('seq', 'head'), route).astype(F32)  10.7 us
    pallas_call x1, Pallas kernels, on_device(): call(states_kernel, (shape((heads, DK, 2 * DK)), shape((heads, 4, DK, 2 *...  4.26 us
    ppermute x1, starting transfers between devices, on_device(): got = lax.ppermute(give, 'head', pairs)  2.59 us
    ppermute x1, waiting for transfers between devices, on_device(): got = lax.ppermute(give, 'head', pairs)  2.5 us
    ppermute x1, starting transfers between devices, on_device(): direct = lax.ppermute(w_half, 'head', pairs)  2.02 us
  transfers between devices with their start and end apart: 11, of which 6 were waited for; matrix products, arithmetic and copies ran while one was open for 0% of the time, Pallas kernels for 6%

profile of v7, /device:TPU:34, one launch (start us, length us, event | category | flops | bytes accessed | tf_op | source)
XLA Modules:
  0.0 98.7 jit_solution(774696236763154773)
XLA Ops:
  0.0 0.0 copy-start.4
  0.0 0.0 copy-start.2
  0.0 0.0 copy-start.3
  0.0 4.3 %shard_map.82 = (bf16[2,128,256]{2,1,0:T(8,128)(2,1)S(1)}, bf16[2,4,128,256]{3,2,1,0:T(8,128)(2,1)S(1)}, f32[256,256]{1,0:T(8,128)S(1)}, f32[256,256]{1,0:T(8,12...) custom-call(bf16[256,256]{1,0:T(8,128)(2,1)} %k_ref.1, bf16[256,256]{1,0:T(8,128)(2,1)} %v_in.1, ...), custom_call_target="tpu_custom_call" | custom-call | flops 2000000000 | bytes 1000000 | tf_op jit(solution)/shard_map/pallas_call | solution.py:340
  4.3 2.0 %collective-permute-start.1 = (bf16[128,4096]{1,0:T(8,128)(2,1)S(1)}, bf16[128,4096]{1,0:T(8,128)(2,1)S(1)}, u32[]{:S(2)}, u32[]{:S(2)}) collective-permute-start(bf16[128,4096]{1,0:T(8,128)(2,1)S(1)} %get-tuple-element.49), channel_id=1, source_target_pairs={{0,1},{1,0},{2,3},{3,2},{4,5},{5,4},{6,7},{7,6},{8,9},{9,8},{10,11... | collective-permute-start | bytes 3145736 | tf_op jit(solution)/shard_map/ppermute | solution.py:374
  6.3 1.9 %collective-permute-start = (bf16[2,128,256]{2,1,0:T(8,128)(2,1)S(1)}, bf16[2,128,256]{2,1,0:T(8,128)(2,1)S(1)}, u32[]{:S(2)}, u32[]{:S(2)}) collective-permute-start(bf16[2,128,256]{2,1,0:T(8,128)(2,1)S(1)} %get-tuple-element.40.mine_ref), channel_id=1, source_target_pairs={{0,16},{16,0},{32,48},{48,32},{64,80},{80,64},{96,112},{112,96},{1... | collective-permute-start | bytes 393224 | tf_op jit(solution)/shard_map/ppermute | solution.py:373
  8.2 0.0 copy-done.4
  8.2 0.0 copy-done.2
  8.2 0.0 copy-done.3
  8.3 0.0 copy-start.1
  8.3 1.2 %shard_map.83 = (f32[256,256]{1,0:T(8,128)S(1)}, bf16[256,256]{1,0:T(8,128)(2,1)S(1)}) custom-call(bf16[256,256]{1,0:T(8,128)(2,1)S(1)} %copy-done.3, bf16[256,256]{1,0:T(8,128)(2,1)S(1)} %copy-done.4, f32[256,256]{1,0:T(8,128)S(1)} %get-tuple-element.34.w_ref, f32[256,256]{1,0:T(8,128)S(1)} %get-tuple-element.35.u_ref, ...), custom_call_target="tpu_custom_call" | custom-call | flops 1000000000 | bytes 1000000 | tf_op jit(solution)/shard_map/pallas_call | solution.py:364
  9.4 0.0 copy-start
  9.4 0.1 collective-permute-done.theirs_ref
  9.5 0.2 shard_map.84
  9.7 16.0 %all-gather = bf16[8,128,256]{2,1,0:T(8,128)(2,1)S(1)} all-gather(bf16[2,128,256]{2,1,0:T(8,128)(2,1)S(1)} %get-tuple-element.41), channel_id=2, replica_groups={{0,32,64,96},{16,48,80,112},{128,160,192,224},{144,176,208,240},{256,28..., dimensions={0}, use_global_device_ids=true | all-gather | bytes 655360 | tf_op jit(solution)/shard_map/all_gather | solution.py:388
  25.8 0.6 shard_map.85
  26.3 12.8 %all-gather.1 = bf16[8,128,256]{2,1,0:T(8,128)(2,1)S(1)} all-gather(bf16[2,128,256]{2,1,0:T(8,128)(2,1)S(1)} %get-tuple-element.43), channel_id=3, replica_groups={{0,128,256,384},{16,144,272,400},{32,160,288,416},{48,176,304,432},{64,..., dimensions={0}, use_global_device_ids=true | all-gather | bytes 655360 | tf_op jit(solution)/shard_map/all_gather | solution.py:388
  39.1 0.0 copy-done.1
  39.1 0.9 shard_map.86
  40.1 0.0 collective-permute-done.1.refs_2_
  40.1 1.9 %collective-permute-start.3 = (bf16[128,4096]{1,0:T(8,128)(2,1)S(1)}, bf16[128,4096]{1,0:T(8,128)(2,1)S(1)}, u32[]{:S(2)}, u32[]{:S(2)}) collective-permute-start(bf16[128,4096]{1,0:T(8,128)(2,1)S(1)} %collective-permute-done.1.refs_2_), channel_id=1, source_target_pairs={{0,16},{16,0},{32,48},{48,32},{64,80},{80,64},{96,112},{112,96},{1... | collective-permute-start | bytes 3145736 | tf_op jit(solution)/shard_map/ppermute | solution.py:410
  42.0 2.6 %collective-permute-start.2 = (bf16[128,256]{1,0:T(8,128)(2,1)S(1)}, bf16[128,256]{1,0:T(8,128)(2,1)S(1)}, u32[]{:S(2)}, u32[]{:S(2)}) collective-permute-start(bf16[128,256]{1,0:T(8,128)(2,1)S(1)} %get-tuple-element.50), channel_id=1, source_target_pairs={{0,1},{1,0},{2,3},{3,2},{4,5},{5,4},{6,7},{7,6},{8,9},{9,8},{10,11... | collective-permute-start | bytes 196616 | tf_op jit(solution)/shard_map/ppermute | solution.py:409
  44.6 0.0 copy-done
  44.6 1.3 %shard_map.87 = (f32[32,4096]{1,0:T(8,128)S(1)}, f32[96,4096]{1,0:T(8,128)S(1)}) custom-call(bf16[128,256]{1,0:T(8,128)(2,1)S(1)} %get-tuple-element.51.keep_ref, bf16[256,4096]{1,0:T(8,128)(2,1)S(1)} %copy-done), custom_call_target="tpu_custom_call" | custom-call | flops 300000000 | bytes 4000000 | tf_op jit(solution)/shard_map/pallas_call | solution.py:434
  45.9 2.5 %collective-permute-done.2.refs_0_ = bf16[128,256]{1,0:T(8,128)(2,1)S(1)} collective-permute-done((bf16[128,256]{1,0:T(8,128)(2,1)S(1)}, bf16[128,256]{1,0:T(8,128)(2,1)S(1)}, u32[]{:S(2)}, u32[]{:S(2)}) %collective-permute-start.2) | collective-permute-done | bytes 65568 | tf_op jit(solution)/shard_map/ppermute | solution.py:409
  48.4 0.0 collective-permute-done.3.refs_3_
  48.4 1.1 %shard_map.88 = (bf16[16,4096]{1,0:T(8,128)(2,1)S(1)}, bf16[16,4096]{1,0:T(8,128)(2,1)S(1)}) custom-call(bf16[128,256]{1,0:T(8,128)(2,1)S(1)} %collective-permute-done.2.refs_0_, f32[32,4096]{1,0:T(8,128)S(1)} %get-tuple-element.52.refs_1_, bf16[128,4096]{1,0:T(8,128)(2,1)S(1)} %collective-permute-done.1.refs_2_, ...), custom_call_target="tpu_custom_call" | custom-call | flops 80000000 | bytes 4000000 | tf_op jit(solution)/shard_map/pallas_call | solution.py:440
  49.5 10.6 %collective-permute-start.4 = (bf16[16,4096]{1,0:T(8,128)(2,1)S(1)}, bf16[16,4096]{1,0:T(8,128)(2,1)S(1)}, u32[]{:S(2)}, u32[]{:S(2)}) collective-permute-start(bf16[16,4096]{1,0:T(8,128)(2,1)S(1)} %get-tuple-element.54), channel_id=1, source_target_pairs={{0,2},{1,15},{2,4},{3,1},{4,6},{5,3},{6,8},{7,5},{8,10},{9,7},{10,... | collective-permute-start | bytes 393224 | tf_op jit(solution)/shard_map/ppermute | solution.py:316
  60.1 1.9 %collective-permute-start.8 = (bf16[16,4096]{1,0:T(8,128)(2,1)S(1)}, bf16[16,4096]{1,0:T(8,128)(2,1)S(1)}, u32[]{:S(2)}, u32[]{:S(2)}) collective-permute-start(bf16[16,4096]{1,0:T(8,128)(2,1)S(1)} %get-tuple-element.60), channel_id=1, source_target_pairs={{0,14},{1,3},{2,0},{3,5},{4,2},{5,7},{6,4},{7,9},{8,6},{9,11},{10,... | collective-permute-start | bytes 393224 | tf_op jit(solution)/shard_map/ppermute | solution.py:316
  62.1 1.5 %shard_map.89 = (bf16[16,4096]{1,0:T(8,128)(2,1)S(1)}, bf16[16,4096]{1,0:T(8,128)(2,1)S(1)}, bf16[16,4096]{1,0:T(8,128)(2,1)S(1)}, bf16[16,4096]{1,0:T(8,128)(2,...) custom-call(bf16[128,256]{1,0:T(8,128)(2,1)S(1)} %collective-permute-done.2.refs_0_, ...), custom_call_target="tpu_custom_call" | custom-call | flops 240000000 | bytes 4000000 | tf_op jit(solution)/shard_map/pallas_call | solution.py:446
  63.5 1.5 %collective-permute-done.4 = bf16[16,4096]{1,0:T(8,128)(2,1)S(1)} collective-permute-done((bf16[16,4096]{1,0:T(8,128)(2,1)S(1)}, bf16[16,4096]{1,0:T(8,128)(2,1)S(1)}, u32[]{:S(2)}, u32[]{:S(2)}) %collective-permute-start.4) | collective-permute-done | bytes 131104 | tf_op jit(solution)/shard_map/ppermute | solution.py:316
  65.1 6.6 %collective-permute-start.5 = (bf16[16,4096]{1,0:T(8,128)(2,1)S(1)}, bf16[16,4096]{1,0:T(8,128)(2,1)S(1)}, u32[]{:S(2)}, u32[]{:S(2)}) collective-permute-start(bf16[16,4096]{1,0:T(8,128)(2,1)S(1)} %add_convert_fusion.5), channel_id=1, source_target_pairs={{0,2},{1,15},{2,4},{3,1},{4,6},{5,3},{6,8},{7,5},{8,10},{9,7},{10,... | collective-permute-start | bytes 393224 | tf_op jit(solution)/shard_map/ppermute | solution.py:316
  71.7 0.0 collective-permute-done.8
  71.7 1.9 %collective-permute-start.9 = (bf16[16,4096]{1,0:T(8,128)(2,1)S(1)}, bf16[16,4096]{1,0:T(8,128)(2,1)S(1)}, u32[]{:S(2)}, u32[]{:S(2)}) collective-permute-start(bf16[16,4096]{1,0:T(8,128)(2,1)S(1)} %add_convert_fusion.2), channel_id=1, source_target_pairs={{0,14},{1,3},{2,0},{3,5},{4,2},{5,7},{6,4},{7,9},{8,6},{9,11},{10,... | collective-permute-start | bytes 393224 | tf_op jit(solution)/shard_map/ppermute | solution.py:316
  73.7 3.9 %collective-permute-done.5 = bf16[16,4096]{1,0:T(8,128)(2,1)S(1)} collective-permute-done((bf16[16,4096]{1,0:T(8,128)(2,1)S(1)}, bf16[16,4096]{1,0:T(8,128)(2,1)S(1)}, u32[]{:S(2)}, u32[]{:S(2)}) %collective-permute-start.5) | collective-permute-done | bytes 131104 | tf_op jit(solution)/shard_map/ppermute | solution.py:316
  77.6 6.6 %collective-permute-start.6 = (bf16[16,4096]{1,0:T(8,128)(2,1)S(1)}, bf16[16,4096]{1,0:T(8,128)(2,1)S(1)}, u32[]{:S(2)}, u32[]{:S(2)}) collective-permute-start(bf16[16,4096]{1,0:T(8,128)(2,1)S(1)} %add_convert_fusion.4), channel_id=1, source_target_pairs={{0,2},{1,15},{2,4},{3,1},{4,6},{5,3},{6,8},{7,5},{8,10},{9,7},{10,... | collective-permute-start | bytes 393224 | tf_op jit(solution)/shard_map/ppermute | solution.py:316
  84.2 0.0 collective-permute-done.9
  84.3 1.9 %collective-permute-start.10 = (bf16[16,4096]{1,0:T(8,128)(2,1)S(1)}, bf16[16,4096]{1,0:T(8,128)(2,1)S(1)}, u32[]{:S(2)}, u32[]{:S(2)}) collective-permute-start(bf16[16,4096]{1,0:T(8,128)(2,1)S(1)} %add_convert_fusion.1), channel_id=1, source_target_pairs={{0,14},{1,3},{2,0},{3,5},{4,2},{5,7},{6,4},{7,9},{8,6},{9,11},{10,... | collective-permute-start | bytes 393224 | tf_op jit(solution)/shard_map/ppermute | solution.py:316
  86.2 2.8 %collective-permute-done.6 = bf16[16,4096]{1,0:T(8,128)(2,1)S(1)} collective-permute-done((bf16[16,4096]{1,0:T(8,128)(2,1)S(1)}, bf16[16,4096]{1,0:T(8,128)(2,1)S(1)}, u32[]{:S(2)}, u32[]{:S(2)}) %collective-permute-start.6) | collective-permute-done | bytes 131104 | tf_op jit(solution)/shard_map/ppermute | solution.py:316
  89.0 6.6 %collective-permute-start.7 = (bf16[16,4096]{1,0:T(8,128)(2,1)S(1)}, bf16[16,4096]{1,0:T(8,128)(2,1)S(1)}, u32[]{:S(2)}, u32[]{:S(2)}) collective-permute-start(bf16[16,4096]{1,0:T(8,128)(2,1)S(1)} %add_convert_fusion.3), channel_id=1, source_target_pairs={{0,2},{1,15},{2,4},{3,1},{4,6},{5,3},{6,8},{7,5},{8,10},{9,7},{10,... | collective-permute-start | bytes 393224 | tf_op jit(solution)/shard_map/ppermute | solution.py:316
  95.5 0.0 collective-permute-done.10
  95.5 2.5 %collective-permute-done.7 = bf16[16,4096]{1,0:T(8,128)(2,1)S(1)} collective-permute-done((bf16[16,4096]{1,0:T(8,128)(2,1)S(1)}, bf16[16,4096]{1,0:T(8,128)(2,1)S(1)}, u32[]{:S(2)}, u32[]{:S(2)}) %collective-permute-start.7) | collective-permute-done | bytes 131104 | tf_op jit(solution)/shard_map/ppermute | solution.py:316
  98.0 0.7 add_convert_fusion
  (5 shorter events, 0.2 us)
Async XLA Ops:
  0.0 8.2 %copy-start.4 = (bf16[256,256]{1,0:T(8,128)(2,1)S(1)}, bf16[256,256]{1,0:T(8,128)(2,1)}, u32[]{:S(2)}) copy-start(bf16[256,256]{1,0:T(8,128)(2,1)} %k_ref.1) | copy-start | bytes 393220
  0.0 8.2 %copy-start.2 = (f32[2,8,256]{2,1,0:T(8,128)S(1)}, f32[2,8,256]{2,1,0:T(8,128)}, u32[]{:S(2)}) copy-start(f32[2,8,256]{2,1,0:T(8,128)} %refs_4_.1) | copy-start | bytes 49156
  0.0 8.2 %copy-start.3 = (bf16[256,256]{1,0:T(8,128)(2,1)S(1)}, bf16[256,256]{1,0:T(8,128)(2,1)}, u32[]{:S(2)}) copy-start(bf16[256,256]{1,0:T(8,128)(2,1)} %q_ref.1) | copy-start | bytes 393220
  4.3 35.8 %collective-permute-start.1 = (bf16[128,4096]{1,0:T(8,128)(2,1)S(1)}, bf16[128,4096]{1,0:T(8,128)(2,1)S(1)}, u32[]{:S(2)}, u32[]{:S(2)}) collective-permute-start(bf16[128,4096]{1,0:T(8,128)(2,1)S(1)} %get-tuple-element.49), channel_id=1, source_target_pairs={{0,1},{1,0},{2,3},{3,2},{4,5},{5,4},{6,7},{7,6},{8,9},{9,8},{10,11... | collective-permute-start | bytes 3145736 | tf_op jit(solution)/shard_map/ppermute | solution.py:374
  6.3 3.2 %collective-permute-start = (bf16[2,128,256]{2,1,0:T(8,128)(2,1)S(1)}, bf16[2,128,256]{2,1,0:T(8,128)(2,1)S(1)}, u32[]{:S(2)}, u32[]{:S(2)}) collective-permute-start(bf16[2,128,256]{2,1,0:T(8,128)(2,1)S(1)} %get-tuple-element.40.mine_ref), channel_id=1, source_target_pairs={{0,16},{16,0},{32,48},{48,32},{64,80},{80,64},{96,112},{112,96},{1... | collective-permute-start | bytes 393224 | tf_op jit(solution)/shard_map/ppermute | solution.py:373
  8.3 30.9 %copy-start.1 = (bf16[256,256]{1,0:T(8,128)(2,1)S(1)}, bf16[256,256]{1,0:T(8,128)(2,1)}, u32[]{:S(2)}) copy-start(bf16[256,256]{1,0:T(8,128)(2,1)} %refs_5_.1) | copy-start | bytes 393220
  9.4 35.2 %copy-start = (bf16[256,4096]{1,0:T(8,128)(2,1)S(1)}, bf16[256,4096]{1,0:T(8,128)(2,1)}, u32[]{:S(2)}) copy-start(bf16[256,4096]{1,0:T(8,128)(2,1)} %mine_ref.1) | copy-start | bytes 6291460
  40.1 8.3 %collective-permute-start.3 = (bf16[128,4096]{1,0:T(8,128)(2,1)S(1)}, bf16[128,4096]{1,0:T(8,128)(2,1)S(1)}, u32[]{:S(2)}, u32[]{:S(2)}) collective-permute-start(bf16[128,4096]{1,0:T(8,128)(2,1)S(1)} %collective-permute-done.1.refs_2_), channel_id=1, source_target_pairs={{0,16},{16,0},{32,48},{48,32},{64,80},{80,64},{96,112},{112,96},{1... | collective-permute-start | bytes 3145736 | tf_op jit(solution)/shard_map/ppermute | solution.py:410
  42.0 6.4 %collective-permute-start.2 = (bf16[128,256]{1,0:T(8,128)(2,1)S(1)}, bf16[128,256]{1,0:T(8,128)(2,1)S(1)}, u32[]{:S(2)}, u32[]{:S(2)}) collective-permute-start(bf16[128,256]{1,0:T(8,128)(2,1)S(1)} %get-tuple-element.50), channel_id=1, source_target_pairs={{0,1},{1,0},{2,3},{3,2},{4,5},{5,4},{6,7},{7,6},{8,9},{9,8},{10,11... | collective-permute-start | bytes 196616 | tf_op jit(solution)/shard_map/ppermute | solution.py:409
  49.5 15.5 %collective-permute-start.4 = (bf16[16,4096]{1,0:T(8,128)(2,1)S(1)}, bf16[16,4096]{1,0:T(8,128)(2,1)S(1)}, u32[]{:S(2)}, u32[]{:S(2)}) collective-permute-start(bf16[16,4096]{1,0:T(8,128)(2,1)S(1)} %get-tuple-element.54), channel_id=1, source_target_pairs={{0,2},{1,15},{2,4},{3,1},{4,6},{5,3},{6,8},{7,5},{8,10},{9,7},{10,... | collective-permute-start | bytes 393224 | tf_op jit(solution)/shard_map/ppermute | solution.py:316
  60.1 11.5 %collective-permute-start.8 = (bf16[16,4096]{1,0:T(8,128)(2,1)S(1)}, bf16[16,4096]{1,0:T(8,128)(2,1)S(1)}, u32[]{:S(2)}, u32[]{:S(2)}) collective-permute-start(bf16[16,4096]{1,0:T(8,128)(2,1)S(1)} %get-tuple-element.60), channel_id=1, source_target_pairs={{0,14},{1,3},{2,0},{3,5},{4,2},{5,7},{6,4},{7,9},{8,6},{9,11},{10,... | collective-permute-start | bytes 393224 | tf_op jit(solution)/shard_map/ppermute | solution.py:316
  65.1 12.4 %collective-permute-start.5 = (bf16[16,4096]{1,0:T(8,128)(2,1)S(1)}, bf16[16,4096]{1,0:T(8,128)(2,1)S(1)}, u32[]{:S(2)}, u32[]{:S(2)}) collective-permute-start(bf16[16,4096]{1,0:T(8,128)(2,1)S(1)} %add_convert_fusion.5), channel_id=1, source_target_pairs={{0,2},{1,15},{2,4},{3,1},{4,6},{5,3},{6,8},{7,5},{8,10},{9,7},{10,... | collective-permute-start | bytes 393224 | tf_op jit(solution)/shard_map/ppermute | solution.py:316
  71.7 12.5 %collective-permute-start.9 = (bf16[16,4096]{1,0:T(8,128)(2,1)S(1)}, bf16[16,4096]{1,0:T(8,128)(2,1)S(1)}, u32[]{:S(2)}, u32[]{:S(2)}) collective-permute-start(bf16[16,4096]{1,0:T(8,128)(2,1)S(1)} %add_convert_fusion.2), channel_id=1, source_target_pairs={{0,14},{1,3},{2,0},{3,5},{4,2},{5,7},{6,4},{7,9},{8,6},{9,11},{10,... | collective-permute-start | bytes 393224 | tf_op jit(solution)/shard_map/ppermute | solution.py:316
  77.6 11.3 %collective-permute-start.6 = (bf16[16,4096]{1,0:T(8,128)(2,1)S(1)}, bf16[16,4096]{1,0:T(8,128)(2,1)S(1)}, u32[]{:S(2)}, u32[]{:S(2)}) collective-permute-start(bf16[16,4096]{1,0:T(8,128)(2,1)S(1)} %add_convert_fusion.4), channel_id=1, source_target_pairs={{0,2},{1,15},{2,4},{3,1},{4,6},{5,3},{6,8},{7,5},{8,10},{9,7},{10,... | collective-permute-start | bytes 393224 | tf_op jit(solution)/shard_map/ppermute | solution.py:316
  84.3 11.3 %collective-permute-start.10 = (bf16[16,4096]{1,0:T(8,128)(2,1)S(1)}, bf16[16,4096]{1,0:T(8,128)(2,1)S(1)}, u32[]{:S(2)}, u32[]{:S(2)}) collective-permute-start(bf16[16,4096]{1,0:T(8,128)(2,1)S(1)} %add_convert_fusion.1), channel_id=1, source_target_pairs={{0,14},{1,3},{2,0},{3,5},{4,2},{5,7},{6,4},{7,9},{8,6},{9,11},{10,... | collective-permute-start | bytes 393224 | tf_op jit(solution)/shard_map/ppermute | solution.py:316
  89.0 9.1 %collective-permute-start.7 = (bf16[16,4096]{1,0:T(8,128)(2,1)S(1)}, bf16[16,4096]{1,0:T(8,128)(2,1)S(1)}, u32[]{:S(2)}, u32[]{:S(2)}) collective-permute-start(bf16[16,4096]{1,0:T(8,128)(2,1)S(1)} %add_convert_fusion.3), channel_id=1, source_target_pairs={{0,2},{1,15},{2,4},{3,1},{4,6},{5,3},{6,8},{7,5},{8,10},{9,7},{10,... | collective-permute-start | bytes 393224 | tf_op jit(solution)/shard_map/ppermute | solution.py:316

commit v8 on v7

--- a/solution.py
+++ b/solution.py
@@ -259,7 +259,7 @@
     chunk = tokens // (2 * ring)
     pair = lax.axis_index("head") // 2
     parity = lax.rem(lax.axis_index("head"), 2)
-    side = 1 - 2 * lax.rem(lax.axis_index("head") + lax.axis_index("seq"), 2)
+    side = 1 - 2 * parity
     for n, j in enumerate(hop_order(ring)):
         kept = 2 * lax.rem(pair + ring + side * (ring // 2 - j), ring) + parity
         given = 2 * lax.rem(pair + ring - side * (ring // 2 - j), ring) + 1 - parity
@@ -305,15 +305,10 @@
     ring = len(terms)
     half = ring // 2
     count = 2 * ring
-    slabs = lax.axis_size("seq")
 
     def hop(block, way):
-        route = []
-        for s in range(slabs):
-            for z in range(count):
-                step = 2 * way * (1 - 2 * ((s + z) % 2))
-                route.append((s * count + z, s * count + (z + step) % count))
-        return lax.ppermute(block, ("seq", "head"), route).astype(F32)
+        route = [(z, (z + 2 * way * (1 - 2 * (z % 2))) % count) for z in range(count)]
+        return lax.ppermute(block, "head", route).astype(F32)
 
     ahead, behind = terms[0], terms[ring - 1]
     for t in range(1, half):

time: 99.2 us -> 98.3 us (level)
  no operation moved by 1% of the time
where the time goes in v8:
time: 98.3 us; the launch traced here: 97.9 us
  starting transfers between devices  44.5 us (45%)
  blocking collectives  28.8 us (29%)
  waiting for transfers between devices  12.4 us (13%)
  Pallas kernels  11 us (11%)
    ppermute x7, starting transfers between devices, hop(): return lax.ppermute(block, 'head', route).astype(F32)  36.1 us
    all_gather x2, blocking collectives, gathered(): return lax.all_gather(total, 'seq', axis=0, axis_index_groups=groups)  28.8 us
    ppermute x7, waiting for transfers between devices, hop(): return lax.ppermute(block, 'head', route).astype(F32)  9.84 us
    pallas_call x1, Pallas kernels, on_device(): call(states_kernel, (shape((heads, DK, 2 * DK)), shape((heads, 4, DK, 2 *...  4.26 us
    ppermute x1, starting transfers between devices, on_device(): got = lax.ppermute(give, 'head', pairs)  2.59 us
    ppermute x1, waiting for transfers between devices, on_device(): got = lax.ppermute(give, 'head', pairs)  2.51 us
    ppermute x1, starting transfers between devices, on_device(): direct = lax.ppermute(w_half, 'head', pairs)  2.02 us
  transfers between devices with their start and end apart: 11, of which 6 were waited for; matrix products, arithmetic and copies ran while one was open for 0% of the time, Pallas kernels for 6%

profile of v8, /device:TPU:34, one launch (start us, length us, event | category | flops | bytes accessed | tf_op | source)
XLA Modules:
  0.0 97.9 jit_solution(1072860097176179172)
XLA Ops:
  0.0 0.0 copy-start.4
  0.0 0.0 copy-start.2
  0.0 0.0 copy-start.3
  0.0 4.3 %shard_map.82 = (bf16[2,128,256]{2,1,0:T(8,128)(2,1)S(1)}, bf16[2,4,128,256]{3,2,1,0:T(8,128)(2,1)S(1)}, f32[256,256]{1,0:T(8,128)S(1)}, f32[256,256]{1,0:T(8,12...) custom-call(bf16[256,256]{1,0:T(8,128)(2,1)} %k_ref.1, bf16[256,256]{1,0:T(8,128)(2,1)} %v_in.1, ...), custom_call_target="tpu_custom_call" | custom-call | flops 2000000000 | bytes 1000000 | tf_op jit(solution)/shard_map/pallas_call | solution.py:335
  4.3 2.0 %collective-permute-start.1 = (bf16[128,4096]{1,0:T(8,128)(2,1)S(1)}, bf16[128,4096]{1,0:T(8,128)(2,1)S(1)}, u32[]{:S(2)}, u32[]{:S(2)}) collective-permute-start(bf16[128,4096]{1,0:T(8,128)(2,1)S(1)} %get-tuple-element.49), channel_id=1, source_target_pairs={{0,1},{1,0},{2,3},{3,2},{4,5},{5,4},{6,7},{7,6},{8,9},{9,8},{10,11... | collective-permute-start | bytes 3145736 | tf_op jit(solution)/shard_map/ppermute | solution.py:369
  6.3 1.9 %collective-permute-start = (bf16[2,128,256]{2,1,0:T(8,128)(2,1)S(1)}, bf16[2,128,256]{2,1,0:T(8,128)(2,1)S(1)}, u32[]{:S(2)}, u32[]{:S(2)}) collective-permute-start(bf16[2,128,256]{2,1,0:T(8,128)(2,1)S(1)} %get-tuple-element.40.mine_ref), channel_id=1, source_target_pairs={{0,16},{16,0},{32,48},{48,32},{64,80},{80,64},{96,112},{112,96},{1... | collective-permute-start | bytes 393224 | tf_op jit(solution)/shard_map/ppermute | solution.py:368
  8.2 0.0 copy-done.4
  8.2 0.0 copy-done.2
  8.2 0.0 copy-done.3
  8.3 0.0 copy-start.1
  8.3 1.2 %shard_map.83 = (f32[256,256]{1,0:T(8,128)S(1)}, bf16[256,256]{1,0:T(8,128)(2,1)S(1)}) custom-call(bf16[256,256]{1,0:T(8,128)(2,1)S(1)} %copy-done.3, bf16[256,256]{1,0:T(8,128)(2,1)S(1)} %copy-done.4, f32[256,256]{1,0:T(8,128)S(1)} %get-tuple-element.34.w_ref, f32[256,256]{1,0:T(8,128)S(1)} %get-tuple-element.35.u_ref, ...), custom_call_target="tpu_custom_call" | custom-call | flops 1000000000 | bytes 1000000 | tf_op jit(solution)/shard_map/pallas_call | solution.py:359
  9.4 0.0 copy-start
  9.4 0.1 collective-permute-done.theirs_ref
  9.5 0.2 shard_map.84
  9.7 16.0 %all-gather = bf16[8,128,256]{2,1,0:T(8,128)(2,1)S(1)} all-gather(bf16[2,128,256]{2,1,0:T(8,128)(2,1)S(1)} %get-tuple-element.41), channel_id=2, replica_groups={{0,32,64,96},{16,48,80,112},{128,160,192,224},{144,176,208,240},{256,28..., dimensions={0}, use_global_device_ids=true | all-gather | bytes 655360 | tf_op jit(solution)/shard_map/all_gather | solution.py:383
  25.8 0.6 shard_map.85
  26.3 12.8 %all-gather.1 = bf16[8,128,256]{2,1,0:T(8,128)(2,1)S(1)} all-gather(bf16[2,128,256]{2,1,0:T(8,128)(2,1)S(1)} %get-tuple-element.43), channel_id=3, replica_groups={{0,128,256,384},{16,144,272,400},{32,160,288,416},{48,176,304,432},{64,..., dimensions={0}, use_global_device_ids=true | all-gather | bytes 655360 | tf_op jit(solution)/shard_map/all_gather | solution.py:383
  39.1 0.0 copy-done.1
  39.1 0.9 shard_map.86
  40.1 0.0 collective-permute-done.1.refs_2_
  40.1 1.9 %collective-permute-start.3 = (bf16[128,4096]{1,0:T(8,128)(2,1)S(1)}, bf16[128,4096]{1,0:T(8,128)(2,1)S(1)}, u32[]{:S(2)}, u32[]{:S(2)}) collective-permute-start(bf16[128,4096]{1,0:T(8,128)(2,1)S(1)} %collective-permute-done.1.refs_2_), channel_id=1, source_target_pairs={{0,16},{16,0},{32,48},{48,32},{64,80},{80,64},{96,112},{112,96},{1... | collective-permute-start | bytes 3145736 | tf_op jit(solution)/shard_map/ppermute | solution.py:405
  42.0 2.6 %collective-permute-start.2 = (bf16[128,256]{1,0:T(8,128)(2,1)S(1)}, bf16[128,256]{1,0:T(8,128)(2,1)S(1)}, u32[]{:S(2)}, u32[]{:S(2)}) collective-permute-start(bf16[128,256]{1,0:T(8,128)(2,1)S(1)} %get-tuple-element.50), channel_id=1, source_target_pairs={{0,1},{1,0},{2,3},{3,2},{4,5},{5,4},{6,7},{7,6},{8,9},{9,8},{10,11... | collective-permute-start | bytes 196616 | tf_op jit(solution)/shard_map/ppermute | solution.py:404
  44.6 0.0 copy-done
  44.6 1.3 %shard_map.87 = (f32[32,4096]{1,0:T(8,128)S(1)}, f32[96,4096]{1,0:T(8,128)S(1)}) custom-call(bf16[128,256]{1,0:T(8,128)(2,1)S(1)} %get-tuple-element.51.keep_ref, bf16[256,4096]{1,0:T(8,128)(2,1)S(1)} %copy-done), custom_call_target="tpu_custom_call" | custom-call | flops 300000000 | bytes 4000000 | tf_op jit(solution)/shard_map/pallas_call | solution.py:429
  45.9 2.5 %collective-permute-done.2.refs_0_ = bf16[128,256]{1,0:T(8,128)(2,1)S(1)} collective-permute-done((bf16[128,256]{1,0:T(8,128)(2,1)S(1)}, bf16[128,256]{1,0:T(8,128)(2,1)S(1)}, u32[]{:S(2)}, u32[]{:S(2)}) %collective-permute-start.2) | collective-permute-done | bytes 65568 | tf_op jit(solution)/shard_map/ppermute | solution.py:404
  48.4 0.0 collective-permute-done.3.refs_3_
  48.4 1.1 %shard_map.88 = (bf16[16,4096]{1,0:T(8,128)(2,1)S(1)}, bf16[16,4096]{1,0:T(8,128)(2,1)S(1)}) custom-call(bf16[128,256]{1,0:T(8,128)(2,1)S(1)} %collective-permute-done.2.refs_0_, f32[32,4096]{1,0:T(8,128)S(1)} %get-tuple-element.52.refs_1_, bf16[128,4096]{1,0:T(8,128)(2,1)S(1)} %collective-permute-done.1.refs_2_, ...), custom_call_target="tpu_custom_call" | custom-call | flops 80000000 | bytes 4000000 | tf_op jit(solution)/shard_map/pallas_call | solution.py:435
  49.5 10.6 %collective-permute-start.4 = (bf16[16,4096]{1,0:T(8,128)(2,1)S(1)}, bf16[16,4096]{1,0:T(8,128)(2,1)S(1)}, u32[]{:S(2)}, u32[]{:S(2)}) collective-permute-start(bf16[16,4096]{1,0:T(8,128)(2,1)S(1)} %get-tuple-element.54), channel_id=1, source_target_pairs={{0,2},{1,15},{2,4},{3,1},{4,6},{5,3},{6,8},{7,5},{8,10},{9,7},{10,... | collective-permute-start | bytes 393224 | tf_op jit(solution)/shard_map/ppermute | solution.py:311
  60.1 1.9 %collective-permute-start.8 = (bf16[16,4096]{1,0:T(8,128)(2,1)S(1)}, bf16[16,4096]{1,0:T(8,128)(2,1)S(1)}, u32[]{:S(2)}, u32[]{:S(2)}) collective-permute-start(bf16[16,4096]{1,0:T(8,128)(2,1)S(1)} %get-tuple-element.60), channel_id=1, source_target_pairs={{0,14},{1,3},{2,0},{3,5},{4,2},{5,7},{6,4},{7,9},{8,6},{9,11},{10,... | collective-permute-start | bytes 393224 | tf_op jit(solution)/shard_map/ppermute | solution.py:311
  62.1 1.5 %shard_map.89 = (bf16[16,4096]{1,0:T(8,128)(2,1)S(1)}, bf16[16,4096]{1,0:T(8,128)(2,1)S(1)}, bf16[16,4096]{1,0:T(8,128)(2,1)S(1)}, bf16[16,4096]{1,0:T(8,128)(2,...) custom-call(bf16[128,256]{1,0:T(8,128)(2,1)S(1)} %collective-permute-done.2.refs_0_, ...), custom_call_target="tpu_custom_call" | custom-call | flops 240000000 | bytes 4000000 | tf_op jit(solution)/shard_map/pallas_call | solution.py:441
  63.5 1.7 %collective-permute-done.4 = bf16[16,4096]{1,0:T(8,128)(2,1)S(1)} collective-permute-done((bf16[16,4096]{1,0:T(8,128)(2,1)S(1)}, bf16[16,4096]{1,0:T(8,128)(2,1)S(1)}, u32[]{:S(2)}, u32[]{:S(2)}) %collective-permute-start.4) | collective-permute-done | bytes 131104 | tf_op jit(solution)/shard_map/ppermute | solution.py:311
  65.3 6.6 %collective-permute-start.5 = (bf16[16,4096]{1,0:T(8,128)(2,1)S(1)}, bf16[16,4096]{1,0:T(8,128)(2,1)S(1)}, u32[]{:S(2)}, u32[]{:S(2)}) collective-permute-start(bf16[16,4096]{1,0:T(8,128)(2,1)S(1)} %add_convert_fusion.5), channel_id=1, source_target_pairs={{0,2},{1,15},{2,4},{3,1},{4,6},{5,3},{6,8},{7,5},{8,10},{9,7},{10,... | collective-permute-start | bytes 393224 | tf_op jit(solution)/shard_map/ppermute | solution.py:311
  71.8 0.0 collective-permute-done.8
  71.9 1.9 %collective-permute-start.9 = (bf16[16,4096]{1,0:T(8,128)(2,1)S(1)}, bf16[16,4096]{1,0:T(8,128)(2,1)S(1)}, u32[]{:S(2)}, u32[]{:S(2)}) collective-permute-start(bf16[16,4096]{1,0:T(8,128)(2,1)S(1)} %add_convert_fusion.2), channel_id=1, source_target_pairs={{0,14},{1,3},{2,0},{3,5},{4,2},{5,7},{6,4},{7,9},{8,6},{9,11},{10,... | collective-permute-start | bytes 393224 | tf_op jit(solution)/shard_map/ppermute | solution.py:311
  73.8 3.6 %collective-permute-done.5 = bf16[16,4096]{1,0:T(8,128)(2,1)S(1)} collective-permute-done((bf16[16,4096]{1,0:T(8,128)(2,1)S(1)}, bf16[16,4096]{1,0:T(8,128)(2,1)S(1)}, u32[]{:S(2)}, u32[]{:S(2)}) %collective-permute-start.5) | collective-permute-done | bytes 131104 | tf_op jit(solution)/shard_map/ppermute | solution.py:311
  77.5 6.6 %collective-permute-start.6 = (bf16[16,4096]{1,0:T(8,128)(2,1)S(1)}, bf16[16,4096]{1,0:T(8,128)(2,1)S(1)}, u32[]{:S(2)}, u32[]{:S(2)}) collective-permute-start(bf16[16,4096]{1,0:T(8,128)(2,1)S(1)} %add_convert_fusion.4), channel_id=1, source_target_pairs={{0,2},{1,15},{2,4},{3,1},{4,6},{5,3},{6,8},{7,5},{8,10},{9,7},{10,... | collective-permute-start | bytes 393224 | tf_op jit(solution)/shard_map/ppermute | solution.py:311
  84.1 0.0 collective-permute-done.9
  84.1 1.9 %collective-permute-start.10 = (bf16[16,4096]{1,0:T(8,128)(2,1)S(1)}, bf16[16,4096]{1,0:T(8,128)(2,1)S(1)}, u32[]{:S(2)}, u32[]{:S(2)}) collective-permute-start(bf16[16,4096]{1,0:T(8,128)(2,1)S(1)} %add_convert_fusion.1), channel_id=1, source_target_pairs={{0,14},{1,3},{2,0},{3,5},{4,2},{5,7},{6,4},{7,9},{8,6},{9,11},{10,... | collective-permute-start | bytes 393224 | tf_op jit(solution)/shard_map/ppermute | solution.py:311
  86.0 2.0 %collective-permute-done.6 = bf16[16,4096]{1,0:T(8,128)(2,1)S(1)} collective-permute-done((bf16[16,4096]{1,0:T(8,128)(2,1)S(1)}, bf16[16,4096]{1,0:T(8,128)(2,1)S(1)}, u32[]{:S(2)}, u32[]{:S(2)}) %collective-permute-start.6) | collective-permute-done | bytes 131104 | tf_op jit(solution)/shard_map/ppermute | solution.py:311
  88.1 6.6 %collective-permute-start.7 = (bf16[16,4096]{1,0:T(8,128)(2,1)S(1)}, bf16[16,4096]{1,0:T(8,128)(2,1)S(1)}, u32[]{:S(2)}, u32[]{:S(2)}) collective-permute-start(bf16[16,4096]{1,0:T(8,128)(2,1)S(1)} %add_convert_fusion.3), channel_id=1, source_target_pairs={{0,2},{1,15},{2,4},{3,1},{4,6},{5,3},{6,8},{7,5},{8,10},{9,7},{10,... | collective-permute-start | bytes 393224 | tf_op jit(solution)/shard_map/ppermute | solution.py:311
  94.7 0.0 collective-permute-done.10
  94.7 2.5 %collective-permute-done.7 = bf16[16,4096]{1,0:T(8,128)(2,1)S(1)} collective-permute-done((bf16[16,4096]{1,0:T(8,128)(2,1)S(1)}, bf16[16,4096]{1,0:T(8,128)(2,1)S(1)}, u32[]{:S(2)}, u32[]{:S(2)}) %collective-permute-start.7) | collective-permute-done | bytes 131104 | tf_op jit(solution)/shard_map/ppermute | solution.py:311
  97.2 0.7 add_convert_fusion
  (5 shorter events, 0.2 us)
Async XLA Ops:
  0.0 8.2 %copy-start.4 = (bf16[256,256]{1,0:T(8,128)(2,1)S(1)}, bf16[256,256]{1,0:T(8,128)(2,1)}, u32[]{:S(2)}) copy-start(bf16[256,256]{1,0:T(8,128)(2,1)} %k_ref.1) | copy-start | bytes 393220
  0.0 8.2 %copy-start.2 = (f32[2,8,256]{2,1,0:T(8,128)S(1)}, f32[2,8,256]{2,1,0:T(8,128)}, u32[]{:S(2)}) copy-start(f32[2,8,256]{2,1,0:T(8,128)} %refs_4_.1) | copy-start | bytes 49156
  0.0 8.2 %copy-start.3 = (bf16[256,256]{1,0:T(8,128)(2,1)S(1)}, bf16[256,256]{1,0:T(8,128)(2,1)}, u32[]{:S(2)}) copy-start(bf16[256,256]{1,0:T(8,128)(2,1)} %q_ref.1) | copy-start | bytes 393220
  4.3 35.8 %collective-permute-start.1 = (bf16[128,4096]{1,0:T(8,128)(2,1)S(1)}, bf16[128,4096]{1,0:T(8,128)(2,1)S(1)}, u32[]{:S(2)}, u32[]{:S(2)}) collective-permute-start(bf16[128,4096]{1,0:T(8,128)(2,1)S(1)} %get-tuple-element.49), channel_id=1, source_target_pairs={{0,1},{1,0},{2,3},{3,2},{4,5},{5,4},{6,7},{7,6},{8,9},{9,8},{10,11... | collective-permute-start | bytes 3145736 | tf_op jit(solution)/shard_map/ppermute | solution.py:369
  6.3 3.2 %collective-permute-start = (bf16[2,128,256]{2,1,0:T(8,128)(2,1)S(1)}, bf16[2,128,256]{2,1,0:T(8,128)(2,1)S(1)}, u32[]{:S(2)}, u32[]{:S(2)}) collective-permute-start(bf16[2,128,256]{2,1,0:T(8,128)(2,1)S(1)} %get-tuple-element.40.mine_ref), channel_id=1, source_target_pairs={{0,16},{16,0},{32,48},{48,32},{64,80},{80,64},{96,112},{112,96},{1... | collective-permute-start | bytes 393224 | tf_op jit(solution)/shard_map/ppermute | solution.py:368
  8.3 30.9 %copy-start.1 = (bf16[256,256]{1,0:T(8,128)(2,1)S(1)}, bf16[256,256]{1,0:T(8,128)(2,1)}, u32[]{:S(2)}) copy-start(bf16[256,256]{1,0:T(8,128)(2,1)} %refs_5_.1) | copy-start | bytes 393220
  9.4 35.2 %copy-start = (bf16[256,4096]{1,0:T(8,128)(2,1)S(1)}, bf16[256,4096]{1,0:T(8,128)(2,1)}, u32[]{:S(2)}) copy-start(bf16[256,4096]{1,0:T(8,128)(2,1)} %mine_ref.1) | copy-start | bytes 6291460
  40.1 8.3 %collective-permute-start.3 = (bf16[128,4096]{1,0:T(8,128)(2,1)S(1)}, bf16[128,4096]{1,0:T(8,128)(2,1)S(1)}, u32[]{:S(2)}, u32[]{:S(2)}) collective-permute-start(bf16[128,4096]{1,0:T(8,128)(2,1)S(1)} %collective-permute-done.1.refs_2_), channel_id=1, source_target_pairs={{0,16},{16,0},{32,48},{48,32},{64,80},{80,64},{96,112},{112,96},{1... | collective-permute-start | bytes 3145736 | tf_op jit(solution)/shard_map/ppermute | solution.py:405
  42.0 6.4 %collective-permute-start.2 = (bf16[128,256]{1,0:T(8,128)(2,1)S(1)}, bf16[128,256]{1,0:T(8,128)(2,1)S(1)}, u32[]{:S(2)}, u32[]{:S(2)}) collective-permute-start(bf16[128,256]{1,0:T(8,128)(2,1)S(1)} %get-tuple-element.50), channel_id=1, source_target_pairs={{0,1},{1,0},{2,3},{3,2},{4,5},{5,4},{6,7},{7,6},{8,9},{9,8},{10,11... | collective-permute-start | bytes 196616 | tf_op jit(solution)/shard_map/ppermute | solution.py:404
  49.5 15.7 %collective-permute-start.4 = (bf16[16,4096]{1,0:T(8,128)(2,1)S(1)}, bf16[16,4096]{1,0:T(8,128)(2,1)S(1)}, u32[]{:S(2)}, u32[]{:S(2)}) collective-permute-start(bf16[16,4096]{1,0:T(8,128)(2,1)S(1)} %get-tuple-element.54), channel_id=1, source_target_pairs={{0,2},{1,15},{2,4},{3,1},{4,6},{5,3},{6,8},{7,5},{8,10},{9,7},{10,... | collective-permute-start | bytes 393224 | tf_op jit(solution)/shard_map/ppermute | solution.py:311
  60.1 11.7 %collective-permute-start.8 = (bf16[16,4096]{1,0:T(8,128)(2,1)S(1)}, bf16[16,4096]{1,0:T(8,128)(2,1)S(1)}, u32[]{:S(2)}, u32[]{:S(2)}) collective-permute-start(bf16[16,4096]{1,0:T(8,128)(2,1)S(1)} %get-tuple-element.60), channel_id=1, source_target_pairs={{0,14},{1,3},{2,0},{3,5},{4,2},{5,7},{6,4},{7,9},{8,6},{9,11},{10,... | collective-permute-start | bytes 393224 | tf_op jit(solution)/shard_map/ppermute | solution.py:311
  65.3 12.2 %collective-permute-start.5 = (bf16[16,4096]{1,0:T(8,128)(2,1)S(1)}, bf16[16,4096]{1,0:T(8,128)(2,1)S(1)}, u32[]{:S(2)}, u32[]{:S(2)}) collective-permute-start(bf16[16,4096]{1,0:T(8,128)(2,1)S(1)} %add_convert_fusion.5), channel_id=1, source_target_pairs={{0,2},{1,15},{2,4},{3,1},{4,6},{5,3},{6,8},{7,5},{8,10},{9,7},{10,... | collective-permute-start | bytes 393224 | tf_op jit(solution)/shard_map/ppermute | solution.py:311
  71.9 12.2 %collective-permute-start.9 = (bf16[16,4096]{1,0:T(8,128)(2,1)S(1)}, bf16[16,4096]{1,0:T(8,128)(2,1)S(1)}, u32[]{:S(2)}, u32[]{:S(2)}) collective-permute-start(bf16[16,4096]{1,0:T(8,128)(2,1)S(1)} %add_convert_fusion.2), channel_id=1, source_target_pairs={{0,14},{1,3},{2,0},{3,5},{4,2},{5,7},{6,4},{7,9},{8,6},{9,11},{10,... | collective-permute-start | bytes 393224 | tf_op jit(solution)/shard_map/ppermute | solution.py:311
  77.5 10.5 %collective-permute-start.6 = (bf16[16,4096]{1,0:T(8,128)(2,1)S(1)}, bf16[16,4096]{1,0:T(8,128)(2,1)S(1)}, u32[]{:S(2)}, u32[]{:S(2)}) collective-permute-start(bf16[16,4096]{1,0:T(8,128)(2,1)S(1)} %add_convert_fusion.4), channel_id=1, source_target_pairs={{0,2},{1,15},{2,4},{3,1},{4,6},{5,3},{6,8},{7,5},{8,10},{9,7},{10,... | collective-permute-start | bytes 393224 | tf_op jit(solution)/shard_map/ppermute | solution.py:311
  84.1 10.6 %collective-permute-start.10 = (bf16[16,4096]{1,0:T(8,128)(2,1)S(1)}, bf16[16,4096]{1,0:T(8,128)(2,1)S(1)}, u32[]{:S(2)}, u32[]{:S(2)}) collective-permute-start(bf16[16,4096]{1,0:T(8,128)(2,1)S(1)} %add_convert_fusion.1), channel_id=1, source_target_pairs={{0,14},{1,3},{2,0},{3,5},{4,2},{5,7},{6,4},{7,9},{8,6},{9,11},{10,... | collective-permute-start | bytes 393224 | tf_op jit(solution)/shard_map/ppermute | solution.py:311
  88.1 9.1 %collective-permute-start.7 = (bf16[16,4096]{1,0:T(8,128)(2,1)S(1)}, bf16[16,4096]{1,0:T(8,128)(2,1)S(1)}, u32[]{:S(2)}, u32[]{:S(2)}) collective-permute-start(bf16[16,4096]{1,0:T(8,128)(2,1)S(1)} %add_convert_fusion.3), channel_id=1, source_target_pairs={{0,2},{1,15},{2,4},{3,1},{4,6},{5,3},{6,8},{7,5},{8,10},{9,7},{10,... | collective-permute-start | bytes 393224 | tf_op jit(solution)/shard_map/ppermute | solution.py:311
